TPU v7x, 128 devices: a whole 4x4x4 slice. The times are simulated.
128 devices in a mesh: row: 8 (over y, z_hi), col: 16 (over x, z_lo, core).
Axes of the slice: x: 4, y: 4, z: 4 (z_hi: 2, z_lo: 2; z = z_hi * 2 + z_lo), core: 2. Of those that a mesh axis runs over, the one named last changes fastest.
Arguments:
- x_seq: bfloat16 [4096, 4096], P(('row', 'col')), may hold values from -6 to 6
- dy_seq: bfloat16 [4096, 4096], P(('row', 'col')), may hold values from -3 to 3
- gate_vals: bfloat16 [224, 32, 4096], P('col', 'row'), may hold values from -0.125 to 0.125
- gate_idx: int32 [224, 32], P('col'), may hold values from 0 to 63, as said below
- up_vals: bfloat16 [224, 32, 4096], P('col', 'row'), may hold values from -0.125 to 0.125
- up_idx: int32 [224, 32], P('col'), may hold values from 0 to 63, as said below
- down_vals: bfloat16 [224, 32, 4096], P('col', 'row'), may hold values from -0.0625 to 0.0625
- down_idx: int32 [224, 32], P('col'), may hold values from 0 to 63, as said below
Outputs:
- y_seq: bfloat16 [4096, 4096], P(('row', 'col'))
- dx_seq: bfloat16 [4096, 4096], P(('row', 'col'))
- d_gate_vals: bfloat16 [224, 32, 4096], P('col', 'row')
- d_up_vals: bfloat16 [224, 32, 4096], P('col', 'row')
- d_down_vals: bfloat16 [224, 32, 4096], P('col', 'row')
Inputs may be any that keep to these rules, and one draw needn't show every extreme that they name: `gate_idx`: each row lists 32 distinct block numbers. `up_idx`: each row lists 32 distinct block numbers. `down_idx`: each row lists 32 distinct block numbers.
All inputs are finite; a program needn't handle non-finite values.
Results may differ from a plain program's by a relative error of at most 0.023.
Values may be sent and summed in bfloat16 or wider, within the bound.
No kernel may reach another device: no remote copies, remote signals or barrier semaphores. Data moves between devices by JAX's collectives and lax.ppermute only.
A program may use at most 192 MiB of HBM per device.

v0:
```python
import jax
import jax.numpy as jnp
from jax import lax
from jax.sharding import PartitionSpec as P

BLK = 64


def per_device(x_seq, dy_seq, gate_vals, gate_idx, up_vals, up_idx, down_vals, down_idx):
    panels, kept = gate_idx.shape
    edge = BLK
    square = edge * edge
    width = x_seq.shape[1]
    dblocks = width // edge
    gate_all, up_all = (
        lax.all_gather(gate_vals, "row", axis=1, tiled=True),
        lax.all_gather(up_vals, "row", axis=1, tiled=True),
    )
    down_all = lax.all_gather(down_vals, "row", axis=1, tiled=True)
    gate_w = gate_all.reshape(panels, kept, edge, edge)
    up_w = up_all.reshape(panels, kept, edge, edge)
    down_w = down_all.reshape(panels, kept, edge, edge)
    x_flip = x_seq.T
    x_part = lax.all_to_all(x_flip, "col", split_axis=0, concat_axis=1, tiled=True)
    x_cols = lax.all_gather(x_part, "col", axis=0, tiled=True)
    rows = x_cols.shape[1]
    x_blocks = x_cols.reshape(dblocks, edge, rows)

    def forward_panel(carry, items):
        gate_ids, up_ids, gate_blk, up_blk = items
        gate_in = jnp.take(x_blocks, gate_ids, axis=0)
        up_in = jnp.take(x_blocks, up_ids, axis=0)
        gate_part = jnp.einsum("jab,jar->br", gate_blk, gate_in, preferred_element_type=jnp.float32)
        up_part = jnp.einsum("jab,jar->br", up_blk, up_in, preferred_element_type=jnp.float32)
        return (carry, (gate_part, up_part))

    _, (gate, up) = lax.scan(forward_panel, 0, (gate_idx, up_idx, gate_w, up_w))
    sigma = jax.nn.sigmoid(gate)
    hidden = (gate * sigma * up).astype(jnp.bfloat16)

    def output_panel(total, items):
        down_ids, down_blk, hidden_part = items
        contrib = jnp.einsum(
            "jbc,br->jcr", down_blk, hidden_part, preferred_element_type=jnp.float32
        )
        return (total.at[down_ids].add(contrib), None)

    empty_cols = jnp.zeros((dblocks, edge, rows), jnp.float32)
    y_cols, _ = lax.scan(output_panel, empty_cols, (down_idx, down_w, hidden))
    y_cols = y_cols.reshape(width, rows)
    dy_flip = dy_seq.T
    y_part = lax.psum_scatter(y_cols.astype(jnp.bfloat16), "col", scatter_dimension=0, tiled=True)
    y_seq = lax.all_to_all(y_part, "col", split_axis=1, concat_axis=0, tiled=True).T
    dy_part = lax.all_to_all(dy_flip, "col", split_axis=0, concat_axis=1, tiled=True)
    dy_cols = lax.all_gather(dy_part, "col", axis=0, tiled=True)
    dy_blocks = dy_cols.reshape(dblocks, edge, rows)

    def hidden_panel(carry, items):
        down_ids, down_blk, hidden_part = items
        dy_in = jnp.take(dy_blocks, down_ids, axis=0)
        back = jnp.einsum("jbc,jcr->br", down_blk, dy_in, preferred_element_type=jnp.float32)
        grad = jnp.einsum("br,jcr->jbc", hidden_part, dy_in, preferred_element_type=jnp.float32)
        return (carry, (back, grad.reshape(kept, square)))

    _, (d_hidden, down_term) = lax.scan(hidden_panel, 0, (down_idx, down_w, hidden))
    d_gate = (d_hidden * up * sigma * (1.0 + gate * (1.0 - sigma))).astype(jnp.bfloat16)
    d_up = (d_hidden * gate * sigma).astype(jnp.bfloat16)
    d_down_vals = lax.psum_scatter(
        down_term.astype(jnp.bfloat16), "row", scatter_dimension=1, tiled=True
    )

    def input_panel(total, items):
        gate_ids, up_ids, gate_blk, up_blk, gate_back, up_back = items
        gate_in = jnp.take(x_blocks, gate_ids, axis=0)
        up_in = jnp.take(x_blocks, up_ids, axis=0)
        gate_grad = jnp.einsum(
            "jar,br->jab", gate_in, gate_back, preferred_element_type=jnp.float32
        )
        up_grad = jnp.einsum("jar,br->jab", up_in, up_back, preferred_element_type=jnp.float32)
        gate_contrib = jnp.einsum(
            "jab,br->jar", gate_blk, gate_back, preferred_element_type=jnp.float32
        )
        up_contrib = jnp.einsum("jab,br->jar", up_blk, up_back, preferred_element_type=jnp.float32)
        total = total.at[gate_ids].add(gate_contrib).at[up_ids].add(up_contrib)
        return (total, (gate_grad.reshape(kept, square), up_grad.reshape(kept, square)))

    dx_cols, (gate_term, up_term) = lax.scan(
        input_panel, empty_cols, (gate_idx, up_idx, gate_w, up_w, d_gate, d_up)
    )
    dx_cols = dx_cols.reshape(width, rows)
    dx_part = lax.psum_scatter(dx_cols.astype(jnp.bfloat16), "col", scatter_dimension=0, tiled=True)
    dx_seq = lax.all_to_all(dx_part, "col", split_axis=1, concat_axis=0, tiled=True).T
    gate_sum, up_sum = (
        lax.psum_scatter(
            gate_term.astype(jnp.bfloat16), "row", scatter_dimension=1, tiled=True
        ).astype(jnp.float32),
        lax.psum_scatter(
            up_term.astype(jnp.bfloat16), "row", scatter_dimension=1, tiled=True
        ).astype(jnp.float32),
    )
    d_gate_vals = gate_sum.astype(jnp.bfloat16)
    d_up_vals = up_sum.astype(jnp.bfloat16)
    return (y_seq, dx_seq, d_gate_vals, d_up_vals, d_down_vals)


def solution(mesh):
    in_specs = (
        P(("row", "col"), None),
        P(("row", "col"), None),
        P("col", "row", None),
        P("col", None),
        P("col", "row", None),
        P("col", None),
        P("col", "row", None),
        P("col", None),
    )
    out_specs = (
        P(("row", "col"), None),
        P(("row", "col"), None),
        P("col", "row", None),
        P("col", "row", None),
        P("col", "row", None),
    )
    return jax.shard_map(
        per_device, mesh=mesh, in_specs=in_specs, out_specs=out_specs, check_vma=False
    )
```

profile of v0, /device:TPU:26, one launch (start us, length us, event | category | flops | bytes accessed | tf_op | source)
XLA Modules:
  0.0 1888.4 jit_solution(8297591659506306367)
XLA Ops:
  12.8 11.7 all_to_all.76
  37.3 44.9 %all-gather.6.cloned.1.call-done = bf16[14,32,4096]{2,0,1:T(8,128)(2,1)} async-done(((bf16[14,4,4096]{2,0,1:T(8,128)(2,1)}), bf16[14,32,4096]{2,0,1:T(8,128)(2,1)}) %all-gather.6.cloned.1.call-update) | async-done | bytes 3670032 | tf_op jit(solution)/shard_map/all_gather | solution.py:19
  82.2 6.0 copy.59
  88.2 11.1 reshape.136
  99.4 54.6 %all-gather.12.cloned.1.call-done = bf16[14,32,4096]{2,0,1:T(8,128)(2,1)} async-done(((bf16[14,4,4096]{2,0,1:T(8,128)(2,1)}), bf16[14,32,4096]{2,0,1:T(8,128)(2,1)}) %all-gather.12.cloned.1.call-update) | async-done | bytes 3670032 | tf_op jit(solution)/shard_map/all_gather | solution.py:17
  153.9 6.0 copy.65
  160.0 11.0 reshape.139
  171.0 54.6 %all-gather.8.cloned.1.call-done = bf16[14,32,4096]{2,0,1:T(8,128)(2,1)} async-done(((bf16[14,4,4096]{2,0,1:T(8,128)(2,1)}), bf16[14,32,4096]{2,0,1:T(8,128)(2,1)}) %all-gather.8.cloned.1.call-update) | async-done | bytes 3670032 | tf_op jit(solution)/shard_map/all_gather | solution.py:16
  225.6 6.0 copy.61
  231.7 11.1 reshape.137
  242.7 29.1 %all-gather.10.cloned.1.call-done = bf16[4096,512]{0,1:T(8,128)(2,1)} async-done(((bf16[256,512]{0,1:T(8,128)(2,1)}), bf16[4096,512]{0,1:T(8,128)(2,1)}) %all-gather.10.cloned.1.call-update) | async-done | bytes 4194320 | tf_op jit(solution)/shard_map/all_gather | solution.py:25
  271.9 6.5 copy.63
  281.3 154.4 %while.48 = (s32[]{:T(128)}, f32[14,64,512]{2,1,0:T(8,128)}, f32[14,64,512]{2,1,0:T(8,128)}, bf16[14,32,64,64]{3,2,1,0:T(8,128)(2,1)}, s32[14,32]{1,0:T(8,128)},...) while((s32[]{:T(128)}, f32[14,64,512]{2,1,0:T(8,128)}, ...), condition=%wide.region_1.3_spmd, body=%wide.region_0.2_spmd.sunk | while | flops 270535040 | bytes 13905129 | solution.py:37
  438.4 6.5 copy.72
  448.7 112.6 %while.50 = (s32[]{:T(128)}, f32[14,64,512]{2,1,0:T(8,128)}, bf16[14,32,4096]{2,1,0:T(8,128)(2,1)}, bf16[14,32,64,64]{3,2,1,0:T(8,128)(2,1)}, s32[14,32]{1,0:T(8...) while((s32[]{:T(128)}, f32[14,64,512]{2,1,0:T(8,128)}, ...), condition=%wide.region_7.9_spmd, body=%wide.region_6.8_spmd.sunk | while | flops 270533824 | bytes 10950825 | solution.py:65
  570.6 204.4 %while.49 = (s32[]{:T(128)}, f32[64,64,512]{2,1,0:T(8,128)}, s32[14,32]{1,0:T(8,128)}, bf16[14,32,64,64]{3,2,1,0:T(8,128)(2,1)}, bf16[14,64,512]{2,1,0:T(8,128)(2,1)S(1)}, /*index=5*/s32[]{:T(128)}) while((s32[]{:T(128)}, f32[64,64,512]{2,1,0:T(8,128)}, s32[14,32]{1,0:T(8,128)}, bf16[14,32,64,64]{3,2,1,0:T(8,128)(2,1)}, ...), condition=%wide.region_4.6_spmd, body=%wide.region_2.5_spmd.sunk | while | flops 135266400 | bytes 17368528 | solution.py:49
  575.1 10.1 scatter_fusion
  589.6 10.2 scatter_fusion
  604.2 10.2 scatter_fusion
  618.9 10.2 scatter_fusion
  633.5 10.2 scatter_fusion
  648.1 10.2 scatter_fusion
  662.7 10.1 scatter_fusion
  677.3 10.2 scatter_fusion
  691.9 10.1 scatter_fusion
  706.5 10.2 scatter_fusion
  721.1 10.1 scatter_fusion
  735.7 10.1 scatter_fusion
  750.3 10.1 scatter_fusion
  764.9 10.1 scatter_fusion
  775.0 6.0 convert_element_type.35
  790.1 568.4 %while.51 = (s32[]{:T(128)}, f32[64,64,512]{2,1,0:T(8,128)}, bf16[14,32,4096]{2,1,0:T(8,128)(2,1)}, bf16[14,32,4096]{2,1,0:T(8,128)(2,1)}, s32[14,32]{1,0:T(8,12...) while((s32[]{:T(128)}, f32[64,64,512]{2,1,0:T(8,128)}, ...), condition=%wide.region_11.13_spmd, body=%wide.region_8.12_spmd.sunk | while | flops 541067840 | bytes 50081812 | solution.py:87
  809.6 10.2 scatter_fusion.1
  819.9 10.3 scatter_fusion.2
  850.5 10.1 scatter_fusion.1
  860.6 10.2 scatter_fusion.2
  891.0 10.2 scatter_fusion.1
  901.2 10.2 scatter_fusion.2
  931.6 10.2 scatter_fusion.1
  941.8 10.2 scatter_fusion.2
  972.3 10.1 scatter_fusion.1
  982.4 10.2 scatter_fusion.2
  1012.8 10.1 scatter_fusion.1
  1023.0 10.2 scatter_fusion.2
  1053.3 10.1 scatter_fusion.1
  1063.5 10.2 scatter_fusion.2
  1093.9 10.1 scatter_fusion.1
  1104.0 10.2 scatter_fusion.2
  1134.4 10.2 scatter_fusion.1
  1144.6 10.1 scatter_fusion.2
  1175.0 10.1 scatter_fusion.1
  1185.1 10.2 scatter_fusion.2
  1215.5 10.2 scatter_fusion.1
  1225.7 10.2 scatter_fusion.2
  1256.1 10.2 scatter_fusion.1
  1266.3 10.2 scatter_fusion.2
  1296.7 10.2 scatter_fusion.1
  1306.9 10.2 scatter_fusion.2
  1337.3 10.1 scatter_fusion.1
  1347.4 10.2 scatter_fusion.2
  1358.5 6.1 convert_element_type.39
  1371.7 55.4 %reduce-scatter.8.cloned.1.call-done = bf16[256,512]{1,0:T(8,128)(2,1)} async-done(((bf16[4096,512]{1,0:T(8,128)(2,1)}), bf16[256,512]{1,0:T(8,128)(2,1)}) %reduce-scatter.8.cloned.1.call-update) | async-done | bytes 262160 | tf_op jit(solution)/shard_map/reduce_scatter | solution.py:91
  1428.9 10.9 all-to-all-start.3
  1446.0 430.4 %all-reduce.6.cloned.1.call-done = (bf16[14,32,4096]{2,1,0:T(8,128)(2,1)}, bf16[14,32,4096]{2,1,0:T(8,128)(2,1)}, bf16[14,32,4096]{2,1,0:T(8,128)(2,1)}) async-done(((bf16[14,32,4096]{2,1,0:T(8,128)(2,1)}, bf16[14,32,4096]{2,1,0:T(8,128)(2,1)}, bf16[14,32,4096]{2,1,0:T(8,128)(2,1)}), (bf16[14,32,4096]{2,1,0:T(8,128)(2,1)}, bf16[14,32,4096]{2,1,0:T(8,128)(2,1)}, ...) | async-done | bytes 11010064
  (489 shorter events, 677.5 us)
Async XLA Ops:
  7.2 4.5 copy-start.1
  7.2 5.6 copy-start.2
  7.2 75.0 %all-gather.6.cloned.1.call-start = ((), (), s32[]{:S(2)}) async-start(), calls=%async_computation.6 | async-start | bytes 4718592 | tf_op jit(solution)/shard_map/all_gather | solution.py:19
  9.4 15.1 copy-start.3
  9.4 144.5 %all-gather.12.cloned.1.call-start = ((), (), s32[]{:S(2)}) async-start(), calls=%async_computation.9 | async-start | bytes 4718592 | tf_op jit(solution)/shard_map/all_gather | solution.py:17
  11.6 214.1 %all-gather.8.cloned.1.call-start = ((), (), s32[]{:S(2)}) async-start(), calls=%async_computation.7 | async-start | bytes 4718592 | tf_op jit(solution)/shard_map/all_gather | solution.py:16
  12.7 259.1 %all-gather.10.cloned.1.call-start = ((), (), s32[]{:S(2)}) async-start(), calls=%async_computation.8 | async-start | bytes 4456448 | tf_op jit(solution)/shard_map/all_gather | solution.py:25
  25.2 11.3 all-to-all-start.2
  30.9 407.4 %all-gather.14.cloned.1.call-start = ((), (), s32[]{:S(2)}) async-start(), calls=%async_computation.11 | async-start | bytes 4456448 | tf_op jit(solution)/shard_map/all_gather | solution.py:55
  36.5 0.7 copy-start
  37.2 1328.1 %reduce-scatter.6.cloned.1.call-start = ((), (), s32[]{:S(2)}) async-start(), calls=%async_computation.10 | async-start | bytes 4456448 | tf_op jit(solution)/shard_map/reduce_scatter | solution.py:52
  781.0 646.0 %reduce-scatter.8.cloned.1.call-start = ((), (), s32[]{:S(2)}) async-start(), calls=%async_computation.12 | async-start | bytes 4456448 | tf_op jit(solution)/shard_map/reduce_scatter | solution.py:91
  1364.6 511.8 %all-reduce.6.cloned.1.call-start = ((), (), s32[]{:S(2)}) async-start(), calls=%async_computation.13 | async-start | bytes 22020096
  1365.3 74.4 %copy-start.4 = (u32[128]{0:T(128)S(1)}, u32[128]{0:T(128)}, u32[]{:S(2)}) copy-start(u32[128]{0:T(128)} %constant.81) | copy-start | bytes 1540
  1367.2 61.7 %all-to-all-start.1 = ((bf16[256,16,32]{0,2,1:T(8,128)(2,1)}), bf16[256,16,32]{0,2,1:T(8,128)(2,1)S(1)}, u32[]{:S(2)}, u32[]{:S(2)}) async-start(bf16[256,16,32]{0,2,1:T(8,128)(2,1)} %bitcast.37), calls=%async_computation.2 | async-start | bytes 524288 | tf_op jit(solution)/shard_map/all_to_all | solution.py:53
  1428.9 16.4 all-to-all-start.3
Sparse Core Ops, SparseCore 0:
  10.4 71.8 all-gather.5
  84.6 69.3 all-gather.11
  156.3 69.3 all-gather.7
  227.1 44.6 all-gather.9
  273.9 45.1 all-gather.13
  781.2 60.8 reduce-scatter.5
  1364.7 62.3 reduce-scatter.7
  1429.8 446.5 all-reduce.5
where the time goes:
time: 1910 us; the launch traced here: 1890 us
  waiting for transfers between devices  679 us (36%)
  other arithmetic  506 us (26%)
  local copies, waits for them, and re-layouts  349 us (18%)
  matrix products  306 us (16%)
  starting transfers between devices  21.4 us (1%)
    unnamed x9, waiting for transfers between devices  431 us
    scatter-add x28, other arithmetic, input_panel(): total = total.at[gate_ids].add(gate_contrib).at[up_ids].add(up_contrib)  285 us
    scatter-add x14, other arithmetic, output_panel(): return (total.at[down_ids].add(contrib), None)  142 us
    reduce_scatter x1, waiting for transfers between devices, per_device(): lax.psum_scatter(dx_cols.astype(jnp.bfloat16), 'col', scatter_dimension=0...  55.4 us
    all_gather x1, waiting for transfers between devices, per_device(): lax.all_gather(gate_vals, 'row', axis=1, tiled=True)  54.6 us
    all_gather x1, waiting for transfers between devices, per_device(): lax.all_gather(up_vals, 'row', axis=1, tiled=True)  54.6 us
    dot_general x14, matrix products, output_panel(): jnp.einsum('jbc,br->jcr', down_blk, hidden_part, preferred_element_type=j...  52.7 us
    dot_general x14, matrix products, input_panel(): jnp.einsum('jab,br->jar', up_blk, up_back, preferred_element_type=jnp.flo...  52.4 us
  transfers between devices with their start and end apart: 11, of which 8 were waited for; matrix products, arithmetic and copies ran while one was open for 43% of the time, Pallas kernels for 0%

commit v1 on v0

v1 whole, which is shorter than its diff:
```python
import jax
import jax.numpy as jnp
from jax import lax
from jax.experimental import pallas as pl
from jax.experimental.pallas import tpu as pltpu
from jax.sharding import Mesh, PartitionSpec as P

BLK = 64
AXES = ("y", "zh", "x", "zl", "c")
Z = ("zh", "zl")
RING = 4
BF = jnp.bfloat16
F32 = jnp.float32
MIB = 1024 * 1024


def shift(value, axis, step):
    return lax.ppermute(value, axis, [(i, (i + step) % RING) for i in range(RING)])


def swap(value, axis):
    return lax.ppermute(value, axis, [(0, 1), (1, 0)])


def gather_direct(own, axis):
    below = shift(own, axis, 1)
    above = shift(own, axis, -1)
    across = shift(own, axis, 2)
    return [own, above, across, below]


def gather_ring(own, axis):
    half = own.shape[0] // 2
    below = shift(own, axis, 1)
    above = shift(own, axis, -1)
    across_a = shift(below[:half], axis, 1)
    across_b = shift(above[half:], axis, -1)
    return [own, above, across_a, across_b, below]


def scatter_direct(chunks, axis):
    from_below = shift(chunks[1], axis, 1)
    from_above = shift(chunks[3], axis, -1)
    from_across = shift(chunks[2], axis, 2)
    total = chunks[0].astype(F32) + from_below.astype(F32)
    total = total + from_above.astype(F32) + from_across.astype(F32)
    return total.astype(BF)


def left_half(shape):
    return lax.broadcasted_iota(jnp.int32, shape, len(shape) - 1) % (2 * BLK) < BLK


def flip(value):
    groups = value.shape[1] // 128
    parts = []
    for g in range(groups):
        parts.append(pltpu.roll(value[:, g * 128 : (g + 1) * 128], BLK, 1))
    return jnp.concatenate(parts, axis=1) if groups > 1 else parts[0]


def kernel_params(limit):
    return pltpu.CompilerParams(
        dimension_semantics=("arbitrary",), vmem_limit_bytes=limit * MIB
    )


def forward_kernel(half_panels, kept_here, place, gate_idx, up_idx, x_ref, tiles, w_ref, m_ref, h_ref):
    rows = x_ref.shape[0]
    zh = place[0]

    @pl.when(pl.program_id(0) == 0)
    def _():
        w_ref[...] = jnp.zeros_like(w_ref)
        mask = left_half((BLK, 2 * BLK))

        def put(step, carry):
            group = step // kept_here
            k = step % kept_here
            j = (group // 2) * (2 * kept_here) + (zh ^ (group % 2)) * kept_here + k
            for p in range(half_panels):
                tile = tiles[(group * half_panels + p) * kept_here + k]
                gate_row = pl.multiple_of(gate_idx[zh * half_panels + p, j] * BLK, BLK)
                up_row = pl.multiple_of(up_idx[zh * half_panels + p, j] * BLK, BLK)
                lanes = pl.ds(p * 2 * BLK, 2 * BLK)
                old = w_ref[pl.ds(gate_row, BLK), lanes]
                w_ref[pl.ds(gate_row, BLK), lanes] = jnp.where(mask, tile, old)
                old = w_ref[pl.ds(up_row, BLK), lanes]
                w_ref[pl.ds(up_row, BLK), lanes] = jnp.where(mask, old, tile)
            return carry

        lax.fori_loop(0, 2 * RING * kept_here, put, 0)

    both = jnp.dot(x_ref[...], w_ref[...], preferred_element_type=F32)
    mask = left_half((rows, 2 * BLK))
    previous = None
    for p in range(half_panels):
        lanes = slice(p * 2 * BLK, (p + 1) * 2 * BLK)
        here = both[:, lanes]
        turned = pltpu.roll(here, BLK, 1)
        gate = jnp.where(mask, here, turned)
        up = jnp.where(mask, turned, here)
        sigma = jax.nn.sigmoid(gate)
        silu = gate * sigma
        m_ref[:, lanes] = jnp.where(mask, up * sigma * (1.0 + gate * (1.0 - sigma)), silu)
        hidden = silu * up
        if p % 2 == 0:
            previous = hidden
        if p % 2 == 1:
            merged = jnp.where(mask, previous, hidden)
            h_ref[:, (p // 2) * 128 : (p // 2 + 1) * 128] = merged.astype(BF)
        elif p == half_panels - 1:
            merged = jnp.where(mask, hidden, 0.0)
            h_ref[:, (p // 2) * 128 : (p // 2 + 1) * 128] = merged.astype(BF)


def output_kernel(half_panels, kept_here, place, down_idx, h_ref, tiles, w_ref, y_ref):
    zh = place[0]
    pairs = kept_here // 2

    @pl.when(pl.program_id(0) == 0)
    def _():
        w_ref[...] = jnp.zeros_like(w_ref)
        mask = left_half((BLK, 2 * BLK))

        def put(step, carry):
            group = step // pairs
            m = step % pairs
            j = (group // 2) * (2 * kept_here) + (zh ^ (group % 2)) * kept_here + 2 * m
            for p in range(half_panels):
                tile = tiles[(group * half_panels + p) * pairs + m]
                turned = flip(tile)
                lanes = pl.ds((p // 2) * 128, 128)
                for h in range(2):
                    row = pl.multiple_of(down_idx[zh * half_panels + p, j + h] * BLK, BLK)
                    source = tile if h == p % 2 else turned
                    old = w_ref[pl.ds(row, BLK), lanes]
                    if p % 2 == 0:
                        w_ref[pl.ds(row, BLK), lanes] = jnp.where(mask, source, old)
                    else:
                        w_ref[pl.ds(row, BLK), lanes] = jnp.where(mask, old, source)
            return carry

        lax.fori_loop(0, 2 * RING * pairs, put, 0)

    width = w_ref.shape[0]
    step = min(width, 1024)
    for start in range(0, width, step):
        part = lax.dot_general(
            h_ref[...], w_ref[start : start + step, :], (((1,), (1,)), ((), ())),
            preferred_element_type=F32,
        )
        y_ref[:, start : start + step] = part.astype(BF)


def backward_kernel(half_panels, dy_ref, wd_ref, m_ref, w_ref, g_ref, dx_ref):
    rows = dy_ref.shape[0]
    d_hidden = jnp.dot(dy_ref[...], wd_ref[...], preferred_element_type=F32)
    mask = left_half((rows, 2 * BLK))
    for p in range(half_panels):
        if p % 2 == 0:
            here = d_hidden[:, (p // 2) * 128 : (p // 2 + 1) * 128]
            turned = pltpu.roll(here, BLK, 1)
            spread = jnp.where(mask, here, turned)
        else:
            spread = jnp.where(mask, turned, here)
        lanes = slice(p * 2 * BLK, (p + 1) * 2 * BLK)
        g_ref[:, lanes] = (spread * m_ref[:, lanes]).astype(BF)
    width = w_ref.shape[0]
    step = min(width, 1024)
    back = g_ref[...]
    blocks = dx_ref.shape
    for start in range(0, width, step):
        part = lax.dot_general(
            back, w_ref[start : start + step, :], (((1,), (1,)), ((), ())),
            preferred_element_type=F32,
        ).astype(BF)
        per = blocks[3]
        for rz in range(blocks[2]):
            for rx in range(blocks[1]):
                at = (rz * blocks[1] + rx) * per
                dx_ref[0, rx, rz, :, start : start + step] = part[at : at + per]


def down_grad_kernel(half_panels, kept_here, place, down_idx, dy_ref, h_ref, out_ref, acc):
    zh = place[0]
    pairs = kept_here // 2
    i = pl.program_id(0)
    cols = dy_ref.shape[1]
    part = lax.dot_general(
        dy_ref[...], h_ref[...], (((0,), (0,)), ((), ())), preferred_element_type=F32
    )
    acc[pl.ds(pl.multiple_of(i * cols, cols), cols), :] = part.astype(BF)

    @pl.when(i == pl.num_programs(0) - 1)
    def _():
        mask = left_half((BLK, 2 * BLK))

        def take(step, carry):
            group = step // pairs
            m = step % pairs
            j = (group // 2) * (2 * kept_here) + (zh ^ (group % 2)) * kept_here + 2 * m
            for p in range(half_panels):
                lanes = pl.ds((p // 2) * 128, 128)
                row0 = pl.multiple_of(down_idx[zh * half_panels + p, j] * BLK, BLK)
                row1 = pl.multiple_of(down_idx[zh * half_panels + p, j + 1] * BLK, BLK)
                first = acc[pl.ds(row0, BLK), lanes]
                second = acc[pl.ds(row1, BLK), lanes]
                if p % 2 == 0:
                    second = flip(second)
                else:
                    first = flip(first)
                out_ref[(group * half_panels + p) * pairs + m] = jnp.where(mask, first, second)
            return carry

        lax.fori_loop(0, 2 * RING * pairs, take, 0)


def input_grad_kernel(half_panels, kept_here, place, gate_idx, up_idx, x_ref, g_ref, out_ref, acc):
    zh = place[0]
    i = pl.program_id(0)
    cols = x_ref.shape[1]
    part = lax.dot_general(
        x_ref[...], g_ref[...], (((0,), (0,)), ((), ())), preferred_element_type=F32
    )
    acc[pl.ds(pl.multiple_of(i * cols, cols), cols), :] = part.astype(BF)

    @pl.when(i == pl.num_programs(0) - 1)
    def _():
        mask = left_half((BLK, 2 * BLK))

        def take(step, carry):
            group = step // kept_here
            k = step % kept_here
            j = (group // 2) * (2 * kept_here) + (zh ^ (group % 2)) * kept_here + k
            for p in range(half_panels):
                lanes = pl.ds(p * 2 * BLK, 2 * BLK)
                gate_row = pl.multiple_of(gate_idx[zh * half_panels + p, j] * BLK, BLK)
                up_row = pl.multiple_of(up_idx[zh * half_panels + p, j] * BLK, BLK)
                first = acc[pl.ds(gate_row, BLK), lanes]
                second = acc[pl.ds(up_row, BLK), lanes]
                out_ref[(group * half_panels + p) * kept_here + k] = jnp.where(mask, first, second)
            return carry

        lax.fori_loop(0, 2 * RING * kept_here, take, 0)


def cost(flops, nbytes):
    return pl.CostEstimate(flops=flops, bytes_accessed=nbytes, transcendentals=0)


def per_device(x_seq, dy_seq, gate_vals, gate_idx, up_vals, up_idx, down_vals, down_idx):
    panels, kept_here, square = gate_vals.shape
    per, width = x_seq.shape
    edge = BLK
    half = panels // 2
    zh = lax.axis_index("zh")
    place = jnp.reshape(zh, (1,)).astype(jnp.int32)
    shape = jax.ShapeDtypeStruct

    gate_blk = gate_vals.reshape(panels, kept_here, edge, edge)
    up_blk = up_vals.reshape(panels, kept_here, edge, edge)
    pair_gu = jnp.concatenate([gate_blk, up_blk], axis=3)
    down_blk = down_vals.reshape(panels, kept_here // 2, 2, edge, edge)
    pair_d = jnp.transpose(down_blk, (0, 1, 4, 2, 3)).reshape(
        panels, kept_here // 2, edge, 2 * edge
    )

    def spread(tiles):
        own = lax.dynamic_slice_in_dim(tiles, zh * half, half, 0)
        other = swap(lax.dynamic_slice_in_dim(tiles, (1 - zh) * half, half, 0), "zh")
        both = jnp.stack([own, other]).reshape(-1, edge, 2 * edge)
        return lax.all_gather(both, "y", axis=0, tiled=True)

    gu_tiles = spread(pair_gu)
    d_tiles = spread(pair_d)

    x_row = jnp.concatenate(gather_direct(x_seq, "x"), axis=0)
    x_own = gather_ring(x_row, Z)
    x_all = jnp.concatenate(x_own + [swap(v, "c") for v in x_own], axis=0)
    dy_row = jnp.concatenate(gather_direct(dy_seq, Z), axis=0)
    dy_own = gather_ring(dy_row, "x")
    dy_list = dy_own + [swap(v, "c") for v in dy_own]
    blocks = []
    for v in dy_list:
        for at in range(0, v.shape[0], per):
            blocks.append(v[at : at + per])
    dy_all = jnp.concatenate(
        [blocks[(c * RING + rx) * RING + rz] for c in range(2) for rz in range(RING) for rx in range(RING)],
        axis=0,
    )

    tokens = 2 * RING * RING * per
    rows = tokens // 4
    hid = -(-half * edge // 128) * 128
    two = half * 2 * edge
    full = lambda *dims: pl.BlockSpec(dims, lambda i: (0,) * len(dims))
    smem = pl.BlockSpec(memory_space=pltpu.SMEM)
    gu_flops = 2 * tokens * width * two
    d_flops = 2 * tokens * width * hid

    def part(fn, *extra):
        def body(*refs):
            fn(*extra, *refs)

        return body

    w_gu, mult, hidden = pl.pallas_call(
        part(forward_kernel, half, kept_here),
        grid=(4,),
        in_specs=[
            smem, smem, smem,
            pl.BlockSpec((rows, width), lambda i: (i, 0)),
            full(*gu_tiles.shape),
        ],
        out_specs=[
            full(width, two),
            pl.BlockSpec((rows, two), lambda i: (i, 0)),
            pl.BlockSpec((rows, hid), lambda i: (i, 0)),
        ],
        out_shape=[shape((width, two), BF), shape((tokens, two), F32), shape((tokens, hid), BF)],
        compiler_params=kernel_params(56),
        cost_estimate=cost(gu_flops, 24 * MIB),
        name="forward",
    )(place, gate_idx, up_idx, x_all, gu_tiles)

    w_d, y_part = pl.pallas_call(
        part(output_kernel, half, kept_here),
        grid=(4,),
        in_specs=[
            smem, smem,
            pl.BlockSpec((rows, hid), lambda i: (i, 0)),
            full(*d_tiles.shape),
        ],
        out_specs=[full(width, hid), pl.BlockSpec((rows, width), lambda i: (i, 0))],
        out_shape=[shape((width, hid), BF), shape((tokens, width), BF)],
        compiler_params=kernel_params(48),
        cost_estimate=cost(d_flops, 16 * MIB),
        name="outputs",
    )(place, down_idx, hidden, d_tiles)

    y_half = tokens // 2
    y_chip = (y_part[:y_half].astype(F32) + swap(y_part[y_half:], "c").astype(F32)).astype(BF)
    y_row = RING * per
    y_z = scatter_direct([y_chip[r * y_row : (r + 1) * y_row] for r in range(RING)], Z)
    y_seq = scatter_direct([y_z[r * per : (r + 1) * per] for r in range(RING)], "x")

    back, dx_part = pl.pallas_call(
        part(backward_kernel, half),
        grid=(4,),
        in_specs=[
            pl.BlockSpec((rows, width), lambda i: (i, 0)),
            full(width, hid),
            pl.BlockSpec((rows, two), lambda i: (i, 0)),
            full(width, two),
        ],
        out_specs=[
            pl.BlockSpec((rows, two), lambda i: (i, 0)),
            pl.BlockSpec((1, RING, RING // 2, per, width), lambda i: (i // 2, 0, i % 2, 0, 0)),
        ],
        out_shape=[shape((tokens, two), BF), shape((2, RING, RING, per, width), BF)],
        compiler_params=kernel_params(60),
        cost_estimate=cost(gu_flops + d_flops, 32 * MIB),
        name="backward",
    )(dy_all, w_d, mult, w_gu)

    dx_chip = (dx_part[0].astype(F32) + swap(dx_part[1], "c").astype(F32)).astype(BF)
    dx_x = scatter_direct([dx_chip[r] for r in range(RING)], "x")
    dx_seq = scatter_direct([dx_x[r] for r in range(RING)], Z)

    cols = 512
    gu_terms = pl.pallas_call(
        part(input_grad_kernel, half, kept_here),
        grid=(width // cols,),
        in_specs=[
            smem, smem, smem,
            pl.BlockSpec((tokens, cols), lambda i: (0, i)),
            full(tokens, two),
        ],
        out_specs=full(*gu_tiles.shape),
        out_shape=shape(gu_tiles.shape, BF),
        scratch_shapes=[pltpu.VMEM((width, two), BF)],
        compiler_params=kernel_params(48),
        cost_estimate=cost(gu_flops, 16 * MIB),
        name="input_grads",
    )(place, gate_idx, up_idx, x_all, back)

    d_terms = pl.pallas_call(
        part(down_grad_kernel, half, kept_here),
        grid=(width // cols,),
        in_specs=[
            smem, smem,
            pl.BlockSpec((tokens, cols), lambda i: (0, i)),
            full(tokens, hid),
        ],
        out_specs=full(*d_tiles.shape),
        out_shape=shape(d_tiles.shape, BF),
        scratch_shapes=[pltpu.VMEM((width, hid), BF)],
        compiler_params=kernel_params(48),
        cost_estimate=cost(d_flops, 12 * MIB),
        name="down_grads",
    )(place, down_idx, dy_all, hidden)

    def collect(terms, per_panel):
        summed = lax.psum_scatter(terms, "y", scatter_dimension=0, tiled=True)
        summed = summed.reshape(2, half, per_panel, edge, 2 * edge)
        other = swap(summed[1], "zh")
        low = jnp.where(zh == 0, summed[0], other)
        high = jnp.where(zh == 0, other, summed[0])
        return jnp.concatenate([low, high], axis=0)

    gu_grads = collect(gu_terms, kept_here)
    d_grads = collect(d_terms, kept_here // 2)
    d_gate_vals = gu_grads[..., :edge].reshape(panels, kept_here, square)
    d_up_vals = gu_grads[..., edge:].reshape(panels, kept_here, square)
    d_grads = d_grads.reshape(panels, kept_here // 2, edge, 2, edge)
    d_down_vals = jnp.transpose(d_grads, (0, 1, 3, 4, 2)).reshape(panels, kept_here, square)
    return (y_seq, dx_seq, d_gate_vals, d_up_vals, d_down_vals)


def solution(mesh):
    grid = Mesh(mesh.devices.reshape(4, 2, 4, 2, 2), AXES)
    row, col = ("y", "zh"), ("x", "zl", "c")
    tokens = P(row + col, None)
    vals = P(col, row, None)
    idx = P(col, None)
    return jax.shard_map(
        per_device,
        mesh=grid,
        in_specs=(tokens, tokens, vals, idx, vals, idx, vals, idx),
        out_specs=(tokens, tokens, vals, vals, vals),
        check_vma=False,
    )
```

time: 1910 us -> 351 us (0.18)
  waiting for transfers between devices: 679 us -> 107 us
  other arithmetic: 506 us -> 16.1 us
  matrix products: 306 us -> 0 us
  local copies, waits for them, and re-layouts: 349 us -> 72.6 us
  Pallas kernels: 0 us -> 75.1 us
  starting transfers between devices: 21.4 us -> 59 us
    unnamed x9 -> x4, waiting for transfers between devices: 431 us -> 0.07 us
    scatter-add x42 -> x0, other arithmetic: 427 us -> none  [the longest x28 285 us: input_panel(): total = total.at[gate_ids].add(gate_contrib).at[up_ids].add(up_contrib)]
    dot_general x126 -> x0, matrix products: 306 us -> none  [the longest x14 52.7 us: output_panel(): jnp.einsum('jbc,br->jcr', down_blk, hidden_part, preferred_element_type=j...]
    gather x70 -> x0, local copies, waits for them, and re-layouts: 202 us -> none  [the longest x14 40.4 us: forward_panel(): up_in = jnp.take(x_blocks, up_ids, axis=0)]
    all_gather x5 -> x2, waiting for transfers between devices: 183 us -> 0.02 us  [spread(): return lax.all_gather(both, 'y', axis=0, tiled=True)]
    ppermute x0 -> x42, waiting for transfers between devices: none -> 107 us  [the longest x26 69.2 us: shift(): lax.ppermute(value, axis, [(i, (i + step) % RING) for i in range(RING)])]
    pallas_call x0 -> x5, Pallas kernels: none -> 75.1 us  [the longest x1 21.2 us: per_device(): pl.pallas_call(part(backward_kernel, half), grid=(4,), in_specs=[pl.Block...]
    ppermute x0 -> x42, starting transfers between devices: none -> 58.8 us  [the longest x26 39.2 us: shift(): lax.ppermute(value, axis, [(i, (i + step) % RING) for i in range(RING)])]
  transfers between devices with their start and end apart: 11 -> 46, of which waited for: 8 -> 16; matrix products, arithmetic and copies ran while one was open for 43% -> 22% of each run, Pallas kernels for 0% -> 22%
where the time goes in v1:
time: 351 us; the launch traced here: 345 us
  waiting for transfers between devices  107 us (30%)
  Pallas kernels  75.1 us (21%)
  local copies, waits for them, and re-layouts  72.6 us (21%)
  starting transfers between devices  59 us (17%)
  other arithmetic  16.1 us (5%)
  between operations  14.4 us (4%)
    ppermute x26, waiting for transfers between devices, shift(): lax.ppermute(value, axis, [(i, (i + step) % RING) for i in range(RING)])  69.2 us
    unnamed x78, local copies, waits for them, and re-layouts  44.5 us
    ppermute x26, starting transfers between devices, shift(): lax.ppermute(value, axis, [(i, (i + step) % RING) for i in range(RING)])  39.2 us
    ppermute x16, waiting for transfers between devices, swap(): return lax.ppermute(value, axis, [(0, 1), (1, 0)])  38.2 us
    pallas_call x1, Pallas kernels, per_device(): pl.pallas_call(part(backward_kernel, half), grid=(4,), in_specs=[pl.Block...  21.2 us
    ppermute x16, starting transfers between devices, swap(): return lax.ppermute(value, axis, [(0, 1), (1, 0)])  19.6 us
    pallas_call x1, Pallas kernels, per_device(): pl.pallas_call(part(forward_kernel, half, kept_here), grid=(4,), in_specs...  17.7 us
    pallas_call x1, Pallas kernels, per_device(): pl.pallas_call(part(input_grad_kernel, half, kept_here), grid=(width // c...  13.8 us
  transfers between devices with their start and end apart: 46, of which 16 were waited for; matrix products, arithmetic and copies ran while one was open for 22% of the time, Pallas kernels for 22%

profile of v1, /device:TPU:26, one launch (start us, length us, event | category | flops | bytes accessed | tf_op | source)
XLA Modules:
  0.0 344.6 jit_solution(5384376148305237237)
XLA Ops:
  7.3 2.0 reshape.60
  9.2 1.9 reshape.61
  11.7 4.0 %collective-permute-start.12 = (bf16[7,4,64,128]{3,2,1,0:T(8,128)(2,1)S(1)}, bf16[7,4,64,128]{3,2,1,0:T(8,128)(2,1)S(1)}, u32[]{:S(2)}, u32[]{:S(2)}) collective-permute-start(bf16[7,4,64,128]{3,2,1,0:T(8,128)(2,1)S(1)} %get-tuple-element.26), channel_id=1, source_target_pairs={{0,16},{16,0},{1,17},{17,1},{2,18},{18,2},{3,19},{19,3},{4,20},{20... | collective-permute-start | bytes 1376264 | tf_op jit(solution)/shard_map/ppermute | solution.py:22
  15.6 10.5 %collective-permute-done.12 = bf16[7,4,64,128]{3,2,1,0:T(8,128)(2,1)S(1)} collective-permute-done((bf16[7,4,64,128]{3,2,1,0:T(8,128)(2,1)S(1)}, bf16[7,4,64,128]{3,2,1,0:T(8,128)(2,1)S(1)}, u32[]{:S(2)}, u32[]{:S(2)}) %collective-permute-start.12) | collective-permute-done | bytes 458784 | tf_op jit(solution)/shard_map/ppermute | solution.py:22
  26.1 1.0 pad_maximum_fusion.1
  27.8 2.4 collective-permute-start.1
  30.2 1.8 collective-permute-start.2
  32.0 3.4 collective-permute-start.21
  37.1 1.3 collective-permute-start.23
  39.2 2.3 collective-permute-done.1
  43.2 3.1 collective-permute-start.3
  47.9 0.9 collective-permute-done.23
  50.1 1.6 collective-permute-start.24
  53.3 2.0 copy.20
  55.2 1.6 collective-permute-start.13
  57.0 19.3 %collective-permute-done.13 = bf16[7,2,64,128]{3,2,1,0:T(8,128)(2,1)S(1)} collective-permute-done((bf16[7,2,64,128]{3,2,1,0:T(8,128)(2,1)}, bf16[7,2,64,128]{3,2,1,0:T(8,128)(2,1)S(1)}, u32[]{:S(2)}, u32[]{:S(2)}) %collective-permute-start.13) | collective-permute-done | bytes 229408 | tf_op jit(solution)/shard_map/ppermute | solution.py:22
  77.8 1.1 slice.238
  79.0 1.1 slice.239
  80.1 3.3 collective-permute-start.6
  83.4 1.4 collective-permute-start.26
  85.6 2.3 constant_dynamic-update-slice_fusion.12
  87.9 10.2 %collective-permute-done.26 = bf16[64,4096]{1,0:T(8,128)(2,1)S(1)} collective-permute-done((bf16[64,4096]{1,0:T(8,128)(2,1)S(1)}, bf16[64,4096]{1,0:T(8,128)(2,1)S(1)}, u32[]{:S(2)}, u32[]{:S(2)}) %collective-permute-start.26) | collective-permute-done | bytes 524320 | tf_op jit(solution)/shard_map/ppermute | solution.py:18
  98.1 3.0 collective-permute-start.27
  106.8 4.7 %collective-permute-done.27 = bf16[64,4096]{1,0:T(8,128)(2,1)S(1)} collective-permute-done((bf16[64,4096]{1,0:T(8,128)(2,1)S(1)}, bf16[64,4096]{1,0:T(8,128)(2,1)S(1)}, u32[]{:S(2)}, u32[]{:S(2)}) %collective-permute-start.27) | collective-permute-done | bytes 524320 | tf_op jit(solution)/shard_map/ppermute | solution.py:18
  112.9 1.7 constant_dynamic-update-slice_fusion.21
  120.5 2.4 constant_dynamic-update-slice_fusion.9
  122.8 1.0 constant_dynamic-update-slice_fusion.8
  125.1 1.1 constant_dynamic-update-slice_fusion.7
  135.5 0.9 constant_dynamic-update-slice_fusion.5
  137.1 1.1 constant_dynamic-update-slice_fusion.4.refs_3_
  139.7 17.7 %forward.1 = (bf16[4096,896]{1,0:T(8,128)(2,1)}, f32[1024,896]{1,0:T(8,128)}, bf16[1024,512]{1,0:T(8,128)(2,1)}) custom-call(s32[1]{0:T(128)} %bitcast.refs_0_, s32[14,32]{1,0:T(8,128)} %refs_1_.6, s32[14,32]{1,0:T(8,128)} %refs_2_.3, bf16[1024,4096]{1,0:T(8,128)(2,1)} %constant_dynamic-update-slice_fusion.4.refs_3_, ...), custom_call_target="tpu_custom_call" | custom-call | flops 7516192768 | bytes 25165824 | tf_op jit(solution)/shard_map/forward/pallas_call | solution.py:308
  157.3 1.2 copy-done.5
  158.6 12.1 %down_grads.1 = bf16[112,64,128]{2,1,0:T(8,128)(2,1)} custom-call(s32[1]{0:T(128)} %bitcast.refs_0_, s32[14,32]{1,0:T(8,128)S(1)} %copy-done.2, bf16[1024,4096]{1,0:T(8,128)(2,1)} %slice_dynamic-update-slice_fusion.refs_0_.refs_2_, bf16[1024,512]{1,0:T(8,128)(2,1)S(1)} %copy-done.5), custom_call_target="tpu_custom_call" | custom-call | flops 4294967296 | bytes 12582912 | tf_op jit(solution)/shard_map/down_grads/pallas_call | solution.py:388
  170.8 1.5 copy-done.1
  172.2 10.4 %outputs.1 = (bf16[4096,512]{1,0:T(8,128)(2,1)}, bf16[1024,4096]{1,0:T(8,128)(2,1)}) custom-call(s32[1]{0:T(128)} %bitcast.refs_0_, s32[14,32]{1,0:T(8,128)S(1)} %copy-done.2, bf16[1024,512]{1,0:T(8,128)(2,1)S(1)} %copy-done.6, bf16[112,64,128]{2,1,0:T(8,128)(2,1)S(1)} %copy-done.1), custom_call_target="tpu_custom_call" | custom-call | flops 4294967296 | bytes 16777216 | tf_op jit(solution)/shard_map/outputs/pallas_call | solution.py:327
  182.7 4.7 %slice.183 = bf16[512,4096]{1,0:T(8,128)(2,1)} slice(bf16[1024,4096]{1,0:T(8,128)(2,1)} %get-tuple-element.13), slice={[512:1024], [0:4096]} | slice | bytes 8388608 | tf_op jit(solution)/shard_map/slice | solution.py:343
  187.4 21.2 %backward.1 = (bf16[1024,896]{1,0:T(8,128)(2,1)}, bf16[2,4,4,32,4096]{4,3,2,1,0:T(8,128)(2,1)}) custom-call(bf16[1024,4096]{1,0:T(8,128)(2,1)} %slice_dynamic-update-slice_fusion.refs_0_.refs_2_, bf16[4096,512]{1,0:T(8,128)(2,1)} %get-tuple-element.14.refs_1_, f32[1024,896]{1,0:T(8,128)} %get-tuple-element.15.refs_2_, ...), custom_call_target="tpu_custom_call" | custom-call | flops 11811160064 | bytes 33554432 | tf_op jit(solution)/shard_map/backward/pallas_call | solution.py:348
  208.6 4.8 %slice_bitcast_fusion = bf16[4,4,32,4096]{3,2,1,0:T(8,128)(2,1)} fusion(bf16[2,4,4,32,4096]{4,3,2,1,0:T(8,128)(2,1)} %get-tuple-element.17), kind=kLoop, calls=%fused_computation.3 | loop fusion | bytes 8388608 | tf_op jit(solution)/shard_map/squeeze | solution.py:367
  213.9 1.1 fusion.13
  215.0 9.6 %collective-permute-start.41 = (bf16[7,2,64,128]{3,2,1,0:T(8,128)(2,1)S(1)}, bf16[7,2,64,128]{3,2,1,0:T(8,128)(2,1)S(1)}, u32[]{:S(2)}, u32[]{:S(2)}) collective-permute-start(bf16[7,2,64,128]{3,2,1,0:T(8,128)(2,1)S(1)} %bitcast.60), channel_id=1, source_target_pairs={{0,16},{16,0},{1,17},{17,1},{2,18},{18,2},{3,19},{19,3},{4,20},{20... | collective-permute-start | bytes 688136 | tf_op jit(solution)/shard_map/ppermute | solution.py:22
  224.6 13.8 %input_grads.1 = bf16[224,64,128]{2,1,0:T(8,128)(2,1)S(1)} custom-call(s32[1]{0:T(128)} %bitcast.refs_0_, s32[14,32]{1,0:T(8,128)S(1)} %copy-done.3, s32[14,32]{1,0:T(8,128)S(1)} %copy-done.4, bf16[1024,4096]{1,0:T(8,128)(2,1)} %constant_dynamic-update-slice_fusion.4.refs_3_, bf16[1024,896]{1,0:T(8,128)(2,1)S(1)} %copy-done.7), custom_call_target="tpu_custom_call" | custom-call | flops 7516192768 | bytes 16777216 | tf_op jit(solution)/shard_map/input_grads/pallas_call | solution.py:372
  238.4 1.8 copy-done
  240.8 1.4 reshape.69
  242.2 5.0 %add_convert_fusion = bf16[512,4096]{1,0:T(8,128)(2,1)S(1)} fusion(bf16[512,4096]{1,0:T(8,128)(2,1)} %collective-permute-done.14, bf16[1024,4096]{1,0:T(8,128)(2,1)} %get-tuple-element.13), kind=kLoop, calls=%fused_computation.2 | loop fusion | flops 8388608 | bytes 12582912 | tf_op jit(solution)/shard_map/convert_element_type | solution.py:343
  247.5 3.6 %collective-permute-start.17 = (bf16[128,4096]{1,0:T(8,128)(2,1)S(1)}, bf16[128,4096]{1,0:T(8,128)(2,1)S(1)}, u32[]{:S(2)}, u32[]{:S(2)}) collective-permute-start(bf16[128,4096]{1,0:T(8,128)(2,1)S(1)} %get-tuple-element.23), channel_id=1, source_target_pairs={{0,16},{2,18},{16,0},{18,2},{1,17},{3,19},{17,1},{19,3},{4,20},{6,... | collective-permute-start | bytes 3145736 | tf_op jit(solution)/shard_map/ppermute | solution.py:18
  251.7 1.4 collective-permute-start.15
  253.1 5.0 %fusion = bf16[4,4,32,4096]{3,2,1,0:T(8,128)(2,1)S(1)} fusion(bf16[4,4,32,4096]{3,2,1,0:T(8,128)(2,1)} %collective-permute-done.33, bf16[2,4,4,32,4096]{4,3,2,1,0:T(8,128)(2,1)} %get-tuple-element.17), kind=kLoop, calls=%fused_computation.1 | loop fusion | flops 8388608 | bytes 12582912 | tf_op jit(solution)/shard_map/convert_element_type | solution.py:367
  258.4 3.0 collective-permute-start.36
  261.4 13.8 %collective-permute-done.17 = bf16[128,4096]{1,0:T(8,128)(2,1)S(1)} collective-permute-done((bf16[128,4096]{1,0:T(8,128)(2,1)S(1)}, bf16[128,4096]{1,0:T(8,128)(2,1)S(1)}, u32[]{:S(2)}, u32[]{:S(2)}) %collective-permute-start.17) | collective-permute-done | bytes 1048608 | tf_op jit(solution)/shard_map/ppermute | solution.py:18
  275.6 20.2 %collective-permute-done.16 = bf16[128,4096]{1,0:T(8,128)(2,1)S(1)} collective-permute-done((bf16[128,4096]{1,0:T(8,128)(2,1)S(1)}, bf16[128,4096]{1,0:T(8,128)(2,1)S(1)}, u32[]{:S(2)}, u32[]{:S(2)}) %collective-permute-start.16) | collective-permute-done | bytes 1048608 | tf_op jit(solution)/shard_map/ppermute | solution.py:18
  295.8 0.9 collective-permute-done.15
  297.4 2.9 collective-permute-start.20
  300.4 2.0 collective-permute-start.18
  302.4 6.3 %collective-permute-done.35 = bf16[4,32,4096]{2,1,0:T(8,128)(2,1)S(1)} collective-permute-done((bf16[4,32,4096]{2,1,0:T(8,128)(2,1)S(1)}, bf16[4,32,4096]{2,1,0:T(8,128)(2,1)S(1)}, u32[]{:S(2)}, u32[]{:S(2)}) %collective-permute-start.35) | collective-permute-done | bytes 1048608 | tf_op jit(solution)/shard_map/ppermute | solution.py:18
  310.4 1.9 collective-permute-start.38
  312.3 2.0 collective-permute-done.20
  314.3 3.4 collective-permute-done.19
  318.5 1.2 fusion.12
  319.8 1.1 collective-permute-start.40
  320.9 3.4 collective-permute-done.38
  324.2 1.2 collective-permute-done.37
  326.2 8.4 %collective-permute-done.40 = bf16[7,4,64,128]{3,2,1,0:T(8,128)(2,1)S(1)} collective-permute-done((bf16[7,4,64,128]{3,2,1,0:T(8,128)(2,1)S(1)}, bf16[7,4,64,128]{3,2,1,0:T(8,128)(2,1)S(1)}, u32[]{:S(2)}, u32[]{:S(2)}) %collective-permute-start.40) | collective-permute-done | bytes 458784 | tf_op jit(solution)/shard_map/ppermute | solution.py:22
  335.1 1.4 reshape.66
  336.5 1.4 reshape.67
  (152 shorter events, 45.6 us)
Async XLA Ops:
  7.2 28.3 %copy-start.14 = (bf16[32,4096]{1,0:T(8,128)(2,1)S(1)}, bf16[32,4096]{1,0:T(8,128)(2,1)}, u32[]{:S(2)}) copy-start(bf16[32,4096]{1,0:T(8,128)(2,1)} %param.8) | copy-start | bytes 786436
  7.2 29.1 %copy-start.15 = (bf16[32,4096]{1,0:T(8,128)(2,1)S(1)}, bf16[32,4096]{1,0:T(8,128)(2,1)}, u32[]{:S(2)}) copy-start(bf16[32,4096]{1,0:T(8,128)(2,1)} %param.9) | copy-start | bytes 786436
  7.2 44.5 %copy-start.13 = (bf16[14,4,4096]{2,1,0:T(4,128)(2,1)S(1)}, bf16[14,4,4096]{2,1,0:T(4,128)(2,1)}, u32[]{:S(2)}) copy-start(bf16[14,4,4096]{2,1,0:T(4,128)(2,1)} %param.14) | copy-start | bytes 1376260
  7.2 132.5 %all-gather.3.cloned.1.call-start = ((), (), s32[]{:S(2)}) async-start(), calls=%async_computation.2 | async-start | bytes 4587520 | tf_op jit(solution)/shard_map/all_gather | solution.py:273
  11.7 14.5 %collective-permute-start.12 = (bf16[7,4,64,128]{3,2,1,0:T(8,128)(2,1)S(1)}, bf16[7,4,64,128]{3,2,1,0:T(8,128)(2,1)S(1)}, u32[]{:S(2)}, u32[]{:S(2)}) collective-permute-start(bf16[7,4,64,128]{3,2,1,0:T(8,128)(2,1)S(1)} %get-tuple-element.26), channel_id=1, source_target_pairs={{0,16},{16,0},{1,17},{17,1},{2,18},{18,2},{3,19},{19,3},{4,20},{20... | collective-permute-start | bytes 1376264 | tf_op jit(solution)/shard_map/ppermute | solution.py:22
  27.1 143.6 %all-gather.5.cloned.1.call-start = ((), (), s32[]{:S(2)}) async-start(), calls=%async_computation.3 | async-start | bytes 2293760 | tf_op jit(solution)/shard_map/all_gather | solution.py:273
  27.2 9.9 %collective-permute-start = (bf16[32,4096]{1,0:T(8,128)(2,1)}, bf16[32,4096]{1,0:T(8,128)(2,1)S(1)}, u32[]{:S(2)}, u32[]{:S(2)}) collective-permute-start(bf16[32,4096]{1,0:T(8,128)(2,1)} %param.8), channel_id=1, source_target_pairs={{0,12},{4,0},{8,4},{12,8},{1,13},{5,1},{9,5},{13,9},{2,14},{6,2},{... | collective-permute-start | bytes 786440 | tf_op jit(solution)/shard_map/ppermute | solution.py:18
  27.8 13.7 %collective-permute-start.1 = (bf16[32,4096]{1,0:T(8,128)(2,1)}, bf16[32,4096]{1,0:T(8,128)(2,1)S(1)}, u32[]{:S(2)}, u32[]{:S(2)}) collective-permute-start(bf16[32,4096]{1,0:T(8,128)(2,1)} %param.8), channel_id=1, source_target_pairs={{0,8},{4,12},{8,0},{12,4},{1,9},{5,13},{9,1},{13,5},{2,10},{6,14},... | collective-permute-start | bytes 786440 | tf_op jit(solution)/shard_map/ppermute | solution.py:18
  30.2 12.2 %collective-permute-start.2 = (bf16[32,4096]{1,0:T(8,128)(2,1)}, bf16[32,4096]{1,0:T(8,128)(2,1)S(1)}, u32[]{:S(2)}, u32[]{:S(2)}) collective-permute-start(bf16[32,4096]{1,0:T(8,128)(2,1)} %param.8), channel_id=1, source_target_pairs={{0,4},{4,8},{8,12},{12,0},{1,5},{5,9},{9,13},{13,1},{2,6},{6,10},{... | collective-permute-start | bytes 786440 | tf_op jit(solution)/shard_map/ppermute | solution.py:18
  32.0 14.3 %collective-permute-start.21 = (bf16[32,4096]{1,0:T(8,128)(2,1)}, bf16[32,4096]{1,0:T(8,128)(2,1)S(1)}, u32[]{:S(2)}, u32[]{:S(2)}) collective-permute-start(bf16[32,4096]{1,0:T(8,128)(2,1)} %param.9), channel_id=1, source_target_pairs={{0,18},{2,0},{16,2},{18,16},{1,19},{3,1},{17,3},{19,17},{4,22},{6,... | collective-permute-start | bytes 786440 | tf_op jit(solution)/shard_map/ppermute | solution.py:18
  35.4 11.7 %collective-permute-start.22 = (bf16[32,4096]{1,0:T(8,128)(2,1)}, bf16[32,4096]{1,0:T(8,128)(2,1)S(1)}, u32[]{:S(2)}, u32[]{:S(2)}) collective-permute-start(bf16[32,4096]{1,0:T(8,128)(2,1)} %param.9), channel_id=1, source_target_pairs={{0,16},{2,18},{16,0},{18,2},{1,17},{3,19},{17,1},{19,3},{4,20},{6,... | collective-permute-start | bytes 786440 | tf_op jit(solution)/shard_map/ppermute | solution.py:18
  37.1 11.7 %collective-permute-start.23 = (bf16[32,4096]{1,0:T(8,128)(2,1)S(1)}, bf16[32,4096]{1,0:T(8,128)(2,1)S(1)}, u32[]{:S(2)}, u32[]{:S(2)}) collective-permute-start(bf16[32,4096]{1,0:T(8,128)(2,1)S(1)} %copy-done.15), channel_id=1, source_target_pairs={{0,2},{2,16},{16,18},{18,0},{1,3},{3,17},{17,19},{19,1},{4,6},{6,2... | collective-permute-start | bytes 786440 | tf_op jit(solution)/shard_map/ppermute | solution.py:18
  43.2 35.6 %collective-permute-start.3 = (bf16[128,4096]{1,0:T(8,128)(2,1)}, bf16[128,4096]{1,0:T(8,128)(2,1)}, u32[]{:S(2)}, u32[]{:S(2)}) collective-permute-start(bf16[128,4096]{1,0:T(8,128)(2,1)} %get-tuple-element.47), channel_id=1, source_target_pairs={{0,18},{2,0},{16,2},{18,16},{1,19},{3,1},{17,3},{19,17},{4,22},{6,... | collective-permute-start | bytes 3145736 | tf_op jit(solution)/shard_map/ppermute | solution.py:18
  46.3 31.0 %collective-permute-start.4 = (bf16[128,4096]{1,0:T(8,128)(2,1)}, bf16[128,4096]{1,0:T(8,128)(2,1)}, u32[]{:S(2)}, u32[]{:S(2)}) collective-permute-start(bf16[128,4096]{1,0:T(8,128)(2,1)} %get-tuple-element.47), channel_id=1, source_target_pairs={{0,2},{2,16},{16,18},{18,0},{1,3},{3,17},{17,19},{19,1},{4,6},{6,2... | collective-permute-start | bytes 3145736 | tf_op jit(solution)/shard_map/ppermute | solution.py:18
  46.3 3.8 %copy-start.11 = (bf16[32,4096]{1,0:T(8,128)(2,1)}, bf16[32,4096]{1,0:T(8,128)(2,1)S(1)}, u32[]{:S(2)}) copy-start(bf16[32,4096]{1,0:T(8,128)(2,1)S(1)} %collective-permute-done.21) | copy-start | bytes 786436
  47.1 3.0 copy-start.9
  48.8 1.3 copy-start.8
  49.6 30.5 %collective-permute-start.25 = (bf16[128,4096]{1,0:T(8,128)(2,1)}, bf16[128,4096]{1,0:T(8,128)(2,1)S(1)}, u32[]{:S(2)}, u32[]{:S(2)}) collective-permute-start(bf16[128,4096]{1,0:T(8,128)(2,1)} %constant_dynamic-update-slice_fusion.17), channel_id=1, source_target_pairs={{0,4},{4,8},{8,12},{12,0},{1,5},{5,9},{9,13},{13,1},{2,6},{6,10},{... | collective-permute-start | bytes 3145736 | tf_op jit(solution)/shard_map/ppermute | solution.py:18
  50.1 33.3 %collective-permute-start.24 = (bf16[128,4096]{1,0:T(8,128)(2,1)}, bf16[128,4096]{1,0:T(8,128)(2,1)S(1)}, u32[]{:S(2)}, u32[]{:S(2)}) collective-permute-start(bf16[128,4096]{1,0:T(8,128)(2,1)} %constant_dynamic-update-slice_fusion.17), channel_id=1, source_target_pairs={{0,12},{4,0},{8,4},{12,8},{1,13},{5,1},{9,5},{13,9},{2,14},{6,2},{... | collective-permute-start | bytes 3145736 | tf_op jit(solution)/shard_map/ppermute | solution.py:18
  53.2 49.3 %copy-start.12 = (bf16[32,4096]{1,0:T(8,128)(2,1)S(1)}, bf16[32,4096]{1,0:T(8,128)(2,1)}, u32[]{:S(2)}) copy-start(bf16[32,4096]{1,0:T(8,128)(2,1)} %copy-done.11) | copy-start | bytes 786436
  53.2 52.1 %copy-start.10 = (bf16[32,4096]{1,0:T(8,128)(2,1)S(1)}, bf16[32,4096]{1,0:T(8,128)(2,1)}, u32[]{:S(2)}) copy-start(bf16[32,4096]{1,0:T(8,128)(2,1)} %copy-done.9) | copy-start | bytes 786436
  55.2 21.1 %collective-permute-start.13 = (bf16[7,2,64,128]{3,2,1,0:T(8,128)(2,1)}, bf16[7,2,64,128]{3,2,1,0:T(8,128)(2,1)S(1)}, u32[]{:S(2)}, u32[]{:S(2)}) collective-permute-start(bf16[7,2,64,128]{3,2,1,0:T(8,128)(2,1)} %copy.20), channel_id=1, source_target_pairs={{0,16},{16,0},{1,17},{17,1},{2,18},{18,2},{3,19},{19,3},{4,20},{20... | collective-permute-start | bytes 688136 | tf_op jit(solution)/shard_map/ppermute | solution.py:22
  77.1 136.7 %reduce-scatter.5.cloned.1.call-start = ((), (), s32[]{:S(2)}) async-start(), calls=%async_computation.5 | async-start | bytes 2293760 | tf_op jit(solution)/shard_map/reduce_scatter | solution.py:405
  77.2 45.6 %collective-permute-start.7 = (bf16[128,4096]{1,0:T(8,128)(2,1)}, bf16[128,4096]{1,0:T(8,128)(2,1)S(1)}, u32[]{:S(2)}, u32[]{:S(2)}) collective-permute-start(bf16[128,4096]{1,0:T(8,128)(2,1)} %get-tuple-element.47), channel_id=1, source_target_pairs={{0,1},{1,0},{2,3},{3,2},{4,5},{5,4},{6,7},{7,6},{8,9},{9,8},{10,11... | collective-permute-start | bytes 3145736 | tf_op jit(solution)/shard_map/ppermute | solution.py:22
  77.3 39.5 %collective-permute-start.28 = (bf16[128,4096]{1,0:T(8,128)(2,1)}, bf16[128,4096]{1,0:T(8,128)(2,1)S(1)}, u32[]{:S(2)}, u32[]{:S(2)}) collective-permute-start(bf16[128,4096]{1,0:T(8,128)(2,1)} %constant_dynamic-update-slice_fusion.17), channel_id=1, source_target_pairs={{0,1},{1,0},{2,3},{3,2},{4,5},{5,4},{6,7},{7,6},{8,9},{9,8},{10,11... | collective-permute-start | bytes 3145736 | tf_op jit(solution)/shard_map/ppermute | solution.py:22
  78.9 39.2 %collective-permute-start.5 = (bf16[64,4096]{1,0:T(8,128)(2,1)S(1)}, bf16[64,4096]{1,0:T(8,128)(2,1)S(1)}, u32[]{:S(2)}, u32[]{:S(2)}) collective-permute-start(bf16[64,4096]{1,0:T(8,128)(2,1)S(1)} %slice.238), channel_id=1, source_target_pairs={{0,2},{2,16},{16,18},{18,0},{1,3},{3,17},{17,19},{19,1},{4,6},{6,2... | collective-permute-start | bytes 1572872 | tf_op jit(solution)/shard_map/ppermute | solution.py:18
  80.1 39.1 %collective-permute-start.6 = (bf16[64,4096]{1,0:T(8,128)(2,1)S(1)}, bf16[64,4096]{1,0:T(8,128)(2,1)S(1)}, u32[]{:S(2)}, u32[]{:S(2)}) collective-permute-start(bf16[64,4096]{1,0:T(8,128)(2,1)S(1)} %slice.239), channel_id=1, source_target_pairs={{0,18},{2,0},{16,2},{18,16},{1,19},{3,1},{17,3},{19,17},{4,22},{6,... | collective-permute-start | bytes 1572872 | tf_op jit(solution)/shard_map/ppermute | solution.py:18
  83.4 14.7 %collective-permute-start.26 = (bf16[64,4096]{1,0:T(8,128)(2,1)S(1)}, bf16[64,4096]{1,0:T(8,128)(2,1)S(1)}, u32[]{:S(2)}, u32[]{:S(2)}) collective-permute-start(bf16[64,4096]{1,0:T(8,128)(2,1)S(1)} %slice.249), channel_id=1, source_target_pairs={{0,4},{4,8},{8,12},{12,0},{1,5},{5,9},{9,13},{13,1},{2,6},{6,10},{... | collective-permute-start | bytes 1572872 | tf_op jit(solution)/shard_map/ppermute | solution.py:18
  98.1 13.4 %collective-permute-start.27 = (bf16[64,4096]{1,0:T(8,128)(2,1)S(1)}, bf16[64,4096]{1,0:T(8,128)(2,1)S(1)}, u32[]{:S(2)}, u32[]{:S(2)}) collective-permute-start(bf16[64,4096]{1,0:T(8,128)(2,1)S(1)} %slice.256), channel_id=1, source_target_pairs={{0,12},{4,0},{8,4},{12,8},{1,13},{5,1},{9,5},{13,9},{2,14},{6,2},{... | collective-permute-start | bytes 1572872 | tf_op jit(solution)/shard_map/ppermute | solution.py:18
  111.5 13.6 %collective-permute-start.8 = (bf16[128,4096]{1,0:T(8,128)(2,1)}, bf16[128,4096]{1,0:T(8,128)(2,1)S(1)}, u32[]{:S(2)}, u32[]{:S(2)}) collective-permute-start(bf16[128,4096]{1,0:T(8,128)(2,1)} %collective-permute-done.3), channel_id=1, source_target_pairs={{0,1},{1,0},{2,3},{3,2},{4,5},{5,4},{6,7},{7,6},{8,9},{9,8},{10,11... | collective-permute-start | bytes 3145736 | tf_op jit(solution)/shard_map/ppermute | solution.py:22
  116.8 20.4 %collective-permute-start.11 = (bf16[128,4096]{1,0:T(8,128)(2,1)}, bf16[128,4096]{1,0:T(8,128)(2,1)S(1)}, u32[]{:S(2)}, u32[]{:S(2)}) collective-permute-start(bf16[128,4096]{1,0:T(8,128)(2,1)} %collective-permute-done.4), channel_id=1, source_target_pairs={{0,1},{1,0},{2,3},{3,2},{4,5},{5,4},{6,7},{7,6},{8,9},{9,8},{10,11... | collective-permute-start | bytes 3145736 | tf_op jit(solution)/shard_map/ppermute | solution.py:22
  118.0 5.8 %collective-permute-start.29 = (bf16[128,4096]{1,0:T(8,128)(2,1)S(1)}, bf16[128,4096]{1,0:T(8,128)(2,1)S(1)}, u32[]{:S(2)}, u32[]{:S(2)}) collective-permute-start(bf16[128,4096]{1,0:T(8,128)(2,1)S(1)} %collective-permute-done.24), channel_id=1, source_target_pairs={{0,1},{1,0},{2,3},{3,2},{4,5},{5,4},{6,7},{7,6},{8,9},{9,8},{10,11... | collective-permute-start | bytes 3145736 | tf_op jit(solution)/shard_map/ppermute | solution.py:22
  119.1 8.3 %collective-permute-start.31 = (bf16[128,4096]{1,0:T(8,128)(2,1)S(1)}, bf16[128,4096]{1,0:T(8,128)(2,1)S(1)}, u32[]{:S(2)}, u32[]{:S(2)}) collective-permute-start(bf16[128,4096]{1,0:T(8,128)(2,1)S(1)} %collective-permute-done.25), channel_id=1, source_target_pairs={{0,1},{1,0},{2,3},{3,2},{4,5},{5,4},{6,7},{7,6},{8,9},{9,8},{10,11... | collective-permute-start | bytes 3145736 | tf_op jit(solution)/shard_map/ppermute | solution.py:22
  122.8 11.9 %collective-permute-start.9 = (bf16[64,4096]{1,0:T(8,128)(2,1)S(1)}, bf16[64,4096]{1,0:T(8,128)(2,1)S(1)}, u32[]{:S(2)}, u32[]{:S(2)}) collective-permute-start(bf16[64,4096]{1,0:T(8,128)(2,1)S(1)} %collective-permute-done.5), channel_id=1, source_target_pairs={{0,1},{1,0},{2,3},{3,2},{4,5},{5,4},{6,7},{7,6},{8,9},{9,8},{10,11... | collective-permute-start | bytes 1572872 | tf_op jit(solution)/shard_map/ppermute | solution.py:22
  123.9 2.3 collective-permute-start.30
  125.1 10.4 %collective-permute-start.10 = (bf16[64,4096]{1,0:T(8,128)(2,1)S(1)}, bf16[64,4096]{1,0:T(8,128)(2,1)S(1)}, u32[]{:S(2)}, u32[]{:S(2)}) collective-permute-start(bf16[64,4096]{1,0:T(8,128)(2,1)S(1)} %collective-permute-done.6), channel_id=1, source_target_pairs={{0,1},{1,0},{2,3},{3,2},{4,5},{5,4},{6,7},{7,6},{8,9},{9,8},{10,11... | collective-permute-start | bytes 1572872 | tf_op jit(solution)/shard_map/ppermute | solution.py:22
  126.2 6.3 %collective-permute-start.32 = (bf16[64,4096]{1,0:T(8,128)(2,1)S(1)}, bf16[64,4096]{1,0:T(8,128)(2,1)S(1)}, u32[]{:S(2)}, u32[]{:S(2)}) collective-permute-start(bf16[64,4096]{1,0:T(8,128)(2,1)S(1)} %collective-permute-done.27), channel_id=1, source_target_pairs={{0,1},{1,0},{2,3},{3,2},{4,5},{5,4},{6,7},{7,6},{8,9},{9,8},{10,11... | collective-permute-start | bytes 1572872 | tf_op jit(solution)/shard_map/ppermute | solution.py:22
  139.7 17.7 %copy-start.2 = (s32[14,32]{1,0:T(8,128)S(1)}, s32[14,32]{1,0:T(8,128)}, u32[]{:S(2)}) copy-start(s32[14,32]{1,0:T(8,128)} %refs_1_.7) | copy-start | bytes 5380
  157.3 1.2 copy-start.5
  158.6 12.2 %copy-start.6 = (bf16[1024,512]{1,0:T(8,128)(2,1)S(1)}, bf16[1024,512]{1,0:T(8,128)(2,1)}, u32[]{:S(2)}) copy-start(bf16[1024,512]{1,0:T(8,128)(2,1)} %get-tuple-element.12.refs_2_.refs_3_) | copy-start | bytes 3145732
  170.7 147.9 %reduce-scatter.3.cloned.1.call-start = ((), (), s32[]{:S(2)}) async-start(), calls=%async_computation.4 | async-start | bytes 4587520 | tf_op jit(solution)/shard_map/reduce_scatter | solution.py:405
  170.7 1.5 copy-start.1
  187.3 54.8 %collective-permute-start.14 = (bf16[512,4096]{1,0:T(8,128)(2,1)}, bf16[512,4096]{1,0:T(8,128)(2,1)}, u32[]{:S(2)}, u32[]{:S(2)}) collective-permute-start(bf16[512,4096]{1,0:T(8,128)(2,1)} %slice.183), channel_id=1, source_target_pairs={{0,1},{1,0},{2,3},{3,2},{4,5},{5,4},{6,7},{7,6},{8,9},{9,8},{10,11... | collective-permute-start | bytes 12582920 | tf_op jit(solution)/shard_map/ppermute | solution.py:22
  208.6 16.0 %copy-start.3 = (s32[14,32]{1,0:T(8,128)S(1)}, s32[14,32]{1,0:T(8,128)}, u32[]{:S(2)}) copy-start(s32[14,32]{1,0:T(8,128)} %refs_1_.6) | copy-start | bytes 5380
  208.6 16.0 %copy-start.4 = (s32[14,32]{1,0:T(8,128)S(1)}, s32[14,32]{1,0:T(8,128)}, u32[]{:S(2)}) copy-start(s32[14,32]{1,0:T(8,128)} %refs_2_.3) | copy-start | bytes 5380
  208.6 16.0 %copy-start.7 = (bf16[1024,896]{1,0:T(8,128)(2,1)S(1)}, bf16[1024,896]{1,0:T(8,128)(2,1)}, u32[]{:S(2)}) copy-start(bf16[1024,896]{1,0:T(8,128)(2,1)} %get-tuple-element.18.refs_4_) | copy-start | bytes 5505028
  213.4 39.7 %collective-permute-start.33 = (bf16[4,4,32,4096]{3,2,1,0:T(8,128)(2,1)}, bf16[4,4,32,4096]{3,2,1,0:T(8,128)(2,1)}, u32[]{:S(2)}, u32[]{:S(2)}) collective-permute-start(bf16[4,4,32,4096]{3,2,1,0:T(8,128)(2,1)} %slice_bitcast_fusion), channel_id=1, source_target_pairs={{0,1},{1,0},{2,3},{3,2},{4,5},{5,4},{6,7},{7,6},{8,9},{9,8},{10,11... | collective-permute-start | bytes 12582920 | tf_op jit(solution)/shard_map/ppermute | solution.py:22
  215.0 25.3 %collective-permute-start.41 = (bf16[7,2,64,128]{3,2,1,0:T(8,128)(2,1)S(1)}, bf16[7,2,64,128]{3,2,1,0:T(8,128)(2,1)S(1)}, u32[]{:S(2)}, u32[]{:S(2)}) collective-permute-start(bf16[7,2,64,128]{3,2,1,0:T(8,128)(2,1)S(1)} %bitcast.60), channel_id=1, source_target_pairs={{0,16},{16,0},{1,17},{17,1},{2,18},{18,2},{3,19},{19,3},{4,20},{20... | collective-permute-start | bytes 688136 | tf_op jit(solution)/shard_map/ppermute | solution.py:22
  238.4 1.9 copy-start
  247.5 27.6 %collective-permute-start.17 = (bf16[128,4096]{1,0:T(8,128)(2,1)S(1)}, bf16[128,4096]{1,0:T(8,128)(2,1)S(1)}, u32[]{:S(2)}, u32[]{:S(2)}) collective-permute-start(bf16[128,4096]{1,0:T(8,128)(2,1)S(1)} %get-tuple-element.23), channel_id=1, source_target_pairs={{0,16},{2,18},{16,0},{18,2},{1,17},{3,19},{17,1},{19,3},{4,20},{6,... | collective-permute-start | bytes 3145736 | tf_op jit(solution)/shard_map/ppermute | solution.py:18
  251.1 44.7 %collective-permute-start.16 = (bf16[128,4096]{1,0:T(8,128)(2,1)S(1)}, bf16[128,4096]{1,0:T(8,128)(2,1)S(1)}, u32[]{:S(2)}, u32[]{:S(2)}) collective-permute-start(bf16[128,4096]{1,0:T(8,128)(2,1)S(1)} %get-tuple-element.24), channel_id=1, source_target_pairs={{0,18},{2,0},{16,2},{18,16},{1,19},{3,1},{17,3},{19,17},{4,22},{6,... | collective-permute-start | bytes 3145736 | tf_op jit(solution)/shard_map/ppermute | solution.py:18
  251.7 45.0 %collective-permute-start.15 = (bf16[128,4096]{1,0:T(8,128)(2,1)S(1)}, bf16[128,4096]{1,0:T(8,128)(2,1)S(1)}, u32[]{:S(2)}, u32[]{:S(2)}) collective-permute-start(bf16[128,4096]{1,0:T(8,128)(2,1)S(1)} %get-tuple-element.22), channel_id=1, source_target_pairs={{0,2},{2,16},{16,18},{18,0},{1,3},{3,17},{17,19},{19,1},{4,6},{6,2... | collective-permute-start | bytes 3145736 | tf_op jit(solution)/shard_map/ppermute | solution.py:18
  258.4 42.0 %collective-permute-start.36 = (bf16[4,32,4096]{2,1,0:T(8,128)(2,1)S(1)}, bf16[4,32,4096]{2,1,0:T(8,128)(2,1)S(1)}, u32[]{:S(2)}, u32[]{:S(2)}) collective-permute-start(bf16[4,32,4096]{2,1,0:T(8,128)(2,1)S(1)} %get-tuple-element.20), channel_id=1, source_target_pairs={{0,8},{4,12},{8,0},{12,4},{1,9},{5,13},{9,1},{13,5},{2,10},{6,14},... | collective-permute-start | bytes 3145736 | tf_op jit(solution)/shard_map/ppermute | solution.py:18
  261.4 47.2 %collective-permute-start.35 = (bf16[4,32,4096]{2,1,0:T(8,128)(2,1)S(1)}, bf16[4,32,4096]{2,1,0:T(8,128)(2,1)S(1)}, u32[]{:S(2)}, u32[]{:S(2)}) collective-permute-start(bf16[4,32,4096]{2,1,0:T(8,128)(2,1)S(1)} %get-tuple-element.21), channel_id=1, source_target_pairs={{0,12},{4,0},{8,4},{12,8},{1,13},{5,1},{9,5},{13,9},{2,14},{6,2},{... | collective-permute-start | bytes 3145736 | tf_op jit(solution)/shard_map/ppermute | solution.py:18
  275.2 33.5 %collective-permute-start.34 = (bf16[4,32,4096]{2,1,0:T(8,128)(2,1)S(1)}, bf16[4,32,4096]{2,1,0:T(8,128)(2,1)S(1)}, u32[]{:S(2)}, u32[]{:S(2)}) collective-permute-start(bf16[4,32,4096]{2,1,0:T(8,128)(2,1)S(1)} %get-tuple-element.19), channel_id=1, source_target_pairs={{0,4},{4,8},{8,12},{12,0},{1,5},{5,9},{9,13},{13,1},{2,6},{6,10},{... | collective-permute-start | bytes 3145736 | tf_op jit(solution)/shard_map/ppermute | solution.py:18
  297.4 16.8 %collective-permute-start.20 = (bf16[32,4096]{1,0:T(8,128)(2,1)S(1)}, bf16[32,4096]{1,0:T(8,128)(2,1)S(1)}, u32[]{:S(2)}, u32[]{:S(2)}) collective-permute-start(bf16[32,4096]{1,0:T(8,128)(2,1)S(1)} %get-tuple-element.31), channel_id=1, source_target_pairs={{0,8},{4,12},{8,0},{12,4},{1,9},{5,13},{9,1},{13,5},{2,10},{6,14},... | collective-permute-start | bytes 786440 | tf_op jit(solution)/shard_map/ppermute | solution.py:18
  300.4 17.3 %collective-permute-start.19 = (bf16[32,4096]{1,0:T(8,128)(2,1)S(1)}, bf16[32,4096]{1,0:T(8,128)(2,1)S(1)}, u32[]{:S(2)}, u32[]{:S(2)}) collective-permute-start(bf16[32,4096]{1,0:T(8,128)(2,1)S(1)} %get-tuple-element.32), channel_id=1, source_target_pairs={{0,12},{4,0},{8,4},{12,8},{1,13},{5,1},{9,5},{13,9},{2,14},{6,2},{... | collective-permute-start | bytes 786440 | tf_op jit(solution)/shard_map/ppermute | solution.py:18
  300.4 17.3 %collective-permute-start.18 = (bf16[32,4096]{1,0:T(8,128)(2,1)S(1)}, bf16[32,4096]{1,0:T(8,128)(2,1)S(1)}, u32[]{:S(2)}, u32[]{:S(2)}) collective-permute-start(bf16[32,4096]{1,0:T(8,128)(2,1)S(1)} %get-tuple-element.30), channel_id=1, source_target_pairs={{0,4},{4,8},{8,12},{12,0},{1,5},{5,9},{9,13},{13,1},{2,6},{6,10},{... | collective-permute-start | bytes 786440 | tf_op jit(solution)/shard_map/ppermute | solution.py:18
  309.5 11.3 %collective-permute-start.39 = (bf16[32,4096]{1,0:T(8,128)(2,1)S(1)}, bf16[32,4096]{1,0:T(8,128)(2,1)S(1)}, u32[]{:S(2)}, u32[]{:S(2)}) collective-permute-start(bf16[32,4096]{1,0:T(8,128)(2,1)S(1)} %get-tuple-element.28), channel_id=1, source_target_pairs={{0,16},{2,18},{16,0},{18,2},{1,17},{3,19},{17,1},{19,3},{4,20},{6,... | collective-permute-start | bytes 786440 | tf_op jit(solution)/shard_map/ppermute | solution.py:18
  310.4 13.9 %collective-permute-start.38 = (bf16[32,4096]{1,0:T(8,128)(2,1)S(1)}, bf16[32,4096]{1,0:T(8,128)(2,1)S(1)}, u32[]{:S(2)}, u32[]{:S(2)}) collective-permute-start(bf16[32,4096]{1,0:T(8,128)(2,1)S(1)} %get-tuple-element.29), channel_id=1, source_target_pairs={{0,18},{2,0},{16,2},{18,16},{1,19},{3,1},{17,3},{19,17},{4,22},{6,... | collective-permute-start | bytes 786440 | tf_op jit(solution)/shard_map/ppermute | solution.py:18
  314.3 11.1 %collective-permute-start.37 = (bf16[32,4096]{1,0:T(8,128)(2,1)S(1)}, bf16[32,4096]{1,0:T(8,128)(2,1)S(1)}, u32[]{:S(2)}, u32[]{:S(2)}) collective-permute-start(bf16[32,4096]{1,0:T(8,128)(2,1)S(1)} %get-tuple-element.27), channel_id=1, source_target_pairs={{0,2},{2,16},{16,18},{18,0},{1,3},{3,17},{17,19},{19,1},{4,6},{6,2... | collective-permute-start | bytes 786440 | tf_op jit(solution)/shard_map/ppermute | solution.py:18
  319.8 14.8 %collective-permute-start.40 = (bf16[7,4,64,128]{3,2,1,0:T(8,128)(2,1)S(1)}, bf16[7,4,64,128]{3,2,1,0:T(8,128)(2,1)S(1)}, u32[]{:S(2)}, u32[]{:S(2)}) collective-permute-start(bf16[7,4,64,128]{3,2,1,0:T(8,128)(2,1)S(1)} %bitcast.58), channel_id=1, source_target_pairs={{0,16},{16,0},{1,17},{17,1},{2,18},{18,2},{3,19},{19,3},{4,20},{20... | collective-permute-start | bytes 1376264 | tf_op jit(solution)/shard_map/ppermute | solution.py:22
Sparse Core Ops, SparseCore 0:
  27.3 43.6 all-gather.2
  77.3 26.9 all-gather.4
  170.8 25.0 reduce-scatter.4
  240.4 42.6 reduce-scatter.2

commit v2 on v0

v2 whole, which is shorter than its diff:
```python
import jax
import jax.numpy as jnp
from jax import lax
from jax.experimental import pallas as pl
from jax.experimental.pallas import tpu as pltpu
from jax.sharding import Mesh, PartitionSpec as P

BLK = 64
AXES = ("y", "zh", "x", "zl", "c")
Z = ("zh", "zl")
ZX = ("zh", "zl", "x")
RING = 4
BF = jnp.bfloat16
F32 = jnp.float32
MIB = 1024 * 1024


def shift(value, axis, step):
    return lax.ppermute(value, axis, [(i, (i + step) % RING) for i in range(RING)])


def swap(value, axis):
    return lax.ppermute(value, axis, [(0, 1), (1, 0)])


def gather_direct(own, axis):
    below = shift(own, axis, 1)
    above = shift(own, axis, -1)
    across = shift(own, axis, 2)
    return [own, above, across, below]


def add(first, second):
    return (first.astype(F32) + second.astype(F32)).astype(BF)


def left_half(shape):
    return lax.broadcasted_iota(jnp.int32, shape, len(shape) - 1) % (2 * BLK) < BLK


def flip(value):
    return pltpu.roll(value, BLK, 1)


def kernel_params(limit):
    return pltpu.CompilerParams(
        dimension_semantics=("arbitrary",), vmem_limit_bytes=limit * MIB
    )


def row_copies(pieces, buf, sems):
    rows = pieces[0].shape[0]
    return [
        pltpu.make_async_copy(piece, buf.at[pl.ds(n * rows, rows)], sems.at[n])
        for n, piece in enumerate(pieces)
    ]


def owner_row(place, core, z, x):
    return core * RING * RING + (place[1] + z) % RING * RING + (place[2] + x) % RING


def chunk_copies(pieces, buf, sems, place):
    per = pieces[0].shape[0] // RING
    copies = []
    for n, piece in enumerate(pieces):
        for x in range(RING):
            at = owner_row(place, n // RING, n % RING, x) * per
            copies.append(
                pltpu.make_async_copy(
                    piece.at[pl.ds(x * per, per)],
                    buf.at[pl.ds(pl.multiple_of(at, per), per)],
                    sems.at[n * RING + x],
                )
            )
    return copies


def tile_wait(copies, i):
    for t in range(len(copies) // 2):

        @pl.when(i == t)
        def _(t=t):
            copies[2 * t].wait()
            copies[2 * t + 1].wait()


class Tiles:
    def __init__(self, half_panels, kept_here, zh):
        self.half_panels, self.kept_here, self.zh = half_panels, kept_here, zh
        self.pairs = kept_here // 2
        self.per_panel = kept_here + self.pairs

    def at(self, group, p, k):
        return (group * self.half_panels + p) * self.per_panel + k

    def kept(self, group, k):
        return (group // 2) * (2 * self.kept_here) + (self.zh ^ (group % 2)) * self.kept_here + k

    def row(self, idx_ref, p, j):
        return pl.multiple_of(idx_ref[self.zh * self.half_panels + p, j] * BLK, BLK)


def build_input_weights(where, gate_idx, up_idx, tiles, w_ref):
    w_ref[...] = jnp.zeros_like(w_ref)
    mask = left_half((BLK, 2 * BLK))

    def put(step, carry):
        group, k = step // where.kept_here, step % where.kept_here
        j = where.kept(group, k)
        for p in range(where.half_panels):
            tile = tiles[where.at(group, p, k)]
            lanes = pl.ds(p * 2 * BLK, 2 * BLK)
            for idx_ref, left in ((gate_idx, True), (up_idx, False)):
                rows = pl.ds(where.row(idx_ref, p, j), BLK)
                old = w_ref[rows, lanes]
                w_ref[rows, lanes] = jnp.where(mask, tile, old) if left else jnp.where(mask, old, tile)
        return carry

    lax.fori_loop(0, 2 * RING * where.kept_here, put, 0)


def build_down_weights(where, down_idx, tiles, w_ref):
    w_ref[...] = jnp.zeros_like(w_ref)
    mask = left_half((BLK, 2 * BLK))

    def put(step, carry):
        group, m = step // where.pairs, step % where.pairs
        j = where.kept(group, 2 * m)
        for p in range(where.half_panels):
            tile = tiles[where.at(group, p, where.kept_here + m)]
            turned = flip(tile)
            lanes = pl.ds((p // 2) * 128, 128)
            for h in range(2):
                rows = pl.ds(where.row(down_idx, p, j + h), BLK)
                source = tile if h == p % 2 else turned
                old = w_ref[rows, lanes]
                if p % 2 == 0:
                    w_ref[rows, lanes] = jnp.where(mask, source, old)
                else:
                    w_ref[rows, lanes] = jnp.where(mask, old, source)
        return carry

    lax.fori_loop(0, 2 * RING * where.pairs, put, 0)


def back_rows(left, w_ref, out_ref, place, i):
    width = w_ref.shape[0]
    step = min(width, 1024)
    per = out_ref.shape[1]
    for start in range(0, width, step):
        part = lax.dot_general(
            left, w_ref[start : start + step, :], (((1,), (1,)), ((), ())),
            preferred_element_type=F32,
        ).astype(BF)
        for a in range(RING // 2):
            for b in range(RING):
                at = (a * RING + b) * per
                z = (place[1] + i * (RING // 2) + a) % RING
                x = (place[2] + b) % RING
                out_ref[z * RING + x, :, start : start + step] = part[at : at + per]


def forward_tile(half_panels, x_tile, w_ref, m_ref, h_ref, h2_ref):
    rows = x_tile.shape[0]
    both = jnp.dot(x_tile, w_ref[...], preferred_element_type=F32)
    mask = left_half((rows, 2 * BLK))
    per = m_ref.shape[3]
    spans = [(a, b, (a * RING + b) * per) for a in range(RING // 2) for b in range(RING)]
    previous = None
    for p in range(half_panels):
        lanes = slice(p * 2 * BLK, (p + 1) * 2 * BLK)
        here = both[:, lanes]
        turned = flip(here)
        gate = jnp.where(mask, here, turned)
        up = jnp.where(mask, turned, here)
        sigma = jax.nn.sigmoid(gate)
        silu = gate * sigma
        mult = jnp.where(mask, up * sigma * (1.0 + gate * (1.0 - sigma)), silu)
        for a, b, at in spans:
            m_ref[0, a, b, :, lanes] = mult[at : at + per]
        hidden = silu * up
        if p % 2 == 0:
            previous = hidden
        if p % 2 == 1 or p == half_panels - 1:
            merged = jnp.where(mask, previous, hidden if p % 2 == 1 else 0.0).astype(BF)
            out = slice((p // 2) * 128, (p // 2 + 1) * 128)
            h_ref[:, out] = merged
            for a, b, at in spans:
                h2_ref[0, b, a, :, out] = merged[at : at + per]


def forward_kernel(half_panels, kept_here, first, place, *refs):
    if first:
        gate_idx, up_idx, down_idx, tiles = refs[:4]
        pieces, refs = refs[4:8], refs[8:]
        m_ref, h2_ref, y_ref, w_other, wd_other = refs[:5]
    else:
        w_other, wd_other = refs[:2]
        pieces, refs = refs[2:6], refs[8:]
        m_ref, h2_ref, y_ref = refs[:3]
    w_ref, wd_ref, h_ref, buf, sems, w_sems = refs[-6:]
    i = pl.program_id(0)
    rows = buf.shape[0] // 2
    copies = row_copies(pieces, buf, sems)
    pairs = ((w_ref, w_other), (wd_ref, wd_other))
    if not first:
        pairs = [(b, a) for a, b in pairs]
    w_copies = [pltpu.make_async_copy(a, b, w_sems.at[n]) for n, (a, b) in enumerate(pairs)]

    @pl.when(i == 0)
    def _():
        if not first:
            for copy in w_copies:
                copy.start()
        for copy in copies:
            copy.start()
        if first:
            where = Tiles(half_panels, kept_here, place[0])
            build_input_weights(where, gate_idx, up_idx, tiles, w_ref)
            w_copies[0].start()
            build_down_weights(where, down_idx, tiles, wd_ref)
            w_copies[1].start()
        else:
            w_copies[0].wait()

    tile_wait(copies, i)
    x_tile = buf[pl.ds(pl.multiple_of(i * rows, rows), rows), :]
    forward_tile(half_panels, x_tile, w_ref, m_ref, h_ref, h2_ref)
    if not first:

        @pl.when(i == 0)
        def _():
            w_copies[1].wait()

    back_rows(h_ref[...], wd_ref, y_ref, place, i)
    if first:

        @pl.when(i == pl.num_programs(0) - 1)
        def _():
            for copy in w_copies:
                copy.wait()


def gradient_kernel(half_panels, kept_here, place, gate_idx, up_idx, down_idx, *refs):
    dy_pieces, x_pieces = refs[:8], refs[8:16]
    wd_ref, m_ref, h_ref, back_kept, back_away, out_ref, dy_buf, x_buf, g_ref, acc, dy_sems, x_sems, g_sems = refs[16:]
    i = pl.program_id(0)
    where = Tiles(half_panels, kept_here, place[0])
    rows = dy_buf.shape[0] // 4
    dy_copies = row_copies(dy_pieces, dy_buf, dy_sems)
    x_copies = chunk_copies(x_pieces, x_buf, x_sems, place)
    half_rows = back_kept.shape[0]
    g_copies = [
        pltpu.make_async_copy(g_ref.at[pl.ds(n * half_rows, half_rows)], out, g_sems.at[n])
        for n, out in enumerate((back_kept, back_away))
    ]
    hid = h_ref.shape[1]
    cols = dy_buf.shape[1] // 4
    mask = left_half((rows, 2 * BLK))
    small = left_half((BLK, 2 * BLK))

    @pl.when(i == 0)
    def _():
        for copy in dy_copies:
            copy.start()
        for copy in x_copies:
            copy.start()

    tile_wait(dy_copies, i)

    @pl.when(i < 4)
    def _():
        dy_tile = dy_buf[pl.ds(pl.multiple_of(i * rows, rows), rows), :]
        d_hidden = jnp.dot(dy_tile, wd_ref[...], preferred_element_type=F32)
        per = m_ref.shape[3]
        for p in range(half_panels):
            if p % 2 == 0:
                here = d_hidden[:, (p // 2) * 128 : (p // 2 + 1) * 128]
                turned = flip(here)
                spread = jnp.where(mask, here, turned)
            else:
                spread = jnp.where(mask, turned, here)
            lanes = slice(p * 2 * BLK, (p + 1) * 2 * BLK)
            for a in range(RING // 2):
                for b in range(RING):
                    at = (a * RING + b) * per
                    chunk = owner_row(place, i // 2, b, (i % 2) * (RING // 2) + a)
                    rows_at = pl.ds(pl.multiple_of(chunk * per, per), per)
                    g_ref[rows_at, lanes] = (
                        spread[at : at + per] * m_ref[0, b, a, :, lanes]
                    ).astype(BF)

    @pl.when((i >= 4) & (i < 8))
    def _():
        at = pl.multiple_of((i - 4) * cols, cols)
        part = lax.dot_general(
            dy_buf[:, pl.ds(at, cols)], h_ref[...], (((0,), (0,)), ((), ())),
            preferred_element_type=F32,
        )
        acc[pl.ds(at, cols), :hid] = part.astype(BF)

    @pl.when(i == 4)
    def _():
        for copy in g_copies:
            copy.start()

    @pl.when(i == 7)
    def _():
        for copy in x_copies:
            copy.wait()

        def take(step, carry):
            group, m = step // where.pairs, step % where.pairs
            j = where.kept(group, 2 * m)
            for p in range(half_panels):
                lanes = pl.ds((p // 2) * 128, 128)
                first = acc[pl.ds(where.row(down_idx, p, j), BLK), lanes]
                second = acc[pl.ds(where.row(down_idx, p, j + 1), BLK), lanes]
                if p % 2 == 0:
                    second = flip(second)
                else:
                    first = flip(first)
                out_ref[where.at(group, p, kept_here + m)] = jnp.where(small, first, second)
            return carry

        lax.fori_loop(0, 2 * RING * where.pairs, take, 0)

    @pl.when(i >= 8)
    def _():
        at = pl.multiple_of((i - 8) * cols, cols)
        part = lax.dot_general(
            x_buf[:, pl.ds(at, cols)], g_ref[...], (((0,), (0,)), ((), ())),
            preferred_element_type=F32,
        )
        acc[pl.ds(at, cols), :] = part.astype(BF)

    @pl.when(i == pl.num_programs(0) - 1)
    def _():
        def take(step, carry):
            group, k = step // kept_here, step % kept_here
            j = where.kept(group, k)
            for p in range(half_panels):
                lanes = pl.ds(p * 2 * BLK, 2 * BLK)
                first = acc[pl.ds(where.row(gate_idx, p, j), BLK), lanes]
                second = acc[pl.ds(where.row(up_idx, p, j), BLK), lanes]
                out_ref[where.at(group, p, k)] = jnp.where(small, first, second)
            return carry

        lax.fori_loop(0, 2 * RING * kept_here, take, 0)
        for copy in g_copies:
            copy.wait()


def cost(flops, nbytes):
    return pl.CostEstimate(flops=flops // 8, bytes_accessed=nbytes // 8, transcendentals=0)


def per_device(x_seq, dy_seq, gate_vals, gate_idx, up_vals, up_idx, down_vals, down_idx):
    panels, kept_here, square = gate_vals.shape
    per, width = x_seq.shape
    edge = BLK
    half = panels // 2
    pairs = kept_here // 2
    per_panel = kept_here + pairs
    zh, z_place = lax.axis_index("zh"), lax.axis_index(Z)
    place = jnp.stack([zh, z_place, lax.axis_index("x")]).astype(jnp.int32)
    shape = jax.ShapeDtypeStruct

    gate_blk = gate_vals.reshape(panels, kept_here, edge, edge)
    up_blk = up_vals.reshape(panels, kept_here, edge, edge)
    pair_gu = jnp.concatenate([gate_blk, up_blk], axis=3)
    down_blk = down_vals.reshape(panels, pairs, 2, edge, edge)
    pair_d = jnp.transpose(down_blk, (0, 1, 4, 2, 3)).reshape(panels, pairs, edge, 2 * edge)
    all_pairs = jnp.concatenate([pair_gu, pair_d], axis=1)
    own = lax.dynamic_slice_in_dim(all_pairs, zh * half, half, 0)
    other = swap(lax.dynamic_slice_in_dim(all_pairs, (1 - zh) * half, half, 0), "zh")

    dy_abs = lax.all_gather(dy_seq, Z, axis=0, tiled=True)
    x_row = jnp.concatenate(gather_direct(x_seq, "x"), axis=0)
    other, dy_abs, x_row = lax.optimization_barrier((other, dy_abs, x_row))
    both = jnp.stack([own, other]).reshape(-1, edge, 2 * edge)
    tiles = lax.all_gather(both, "y", axis=0, tiled=True)
    dy_row = jnp.roll(dy_abs, -z_place * per, axis=0)
    x_own = gather_direct(x_row, Z)
    dy_below, dy_above = shift(dy_row, "x", 1), shift(dy_row, "x", -1)
    dy_own = [dy_row, dy_above, shift(dy_row, "x", 2), dy_below]
    x_own, dy_own = lax.optimization_barrier((x_own, dy_own))
    x_core = [swap(v, "c") for v in x_own]

    tokens = 2 * RING * RING * per
    rows = tokens // 4
    hid = -(-half * edge // 128) * 128
    two = half * 2 * edge
    pair = RING // 2
    once = pl.Buffered(1)
    full = lambda *dims: pl.BlockSpec(dims, lambda i: (0,) * len(dims), pipeline_mode=once)
    out_full = lambda *dims: pl.BlockSpec(dims, lambda i: (0,) * len(dims))
    smem = pl.BlockSpec(memory_space=pltpu.SMEM)
    hbm = pl.BlockSpec(memory_space=pl.ANY)
    ordered = lambda last: (2, RING, RING, per, last)
    gu_flops = 2 * tokens * width * two
    d_flops = 2 * tokens * width * hid
    chunks = (RING * RING, per, width)

    def part(fn, *extra):
        def body(*refs):
            fn(*extra, *refs)

        return body

    def forward(core, first, inputs, name):
        specs = [smem] * 4 + [full(*tiles.shape)] + [hbm] * 4 if first else [smem] + [hbm] * 8
        extra_out = [shape((width, two), BF), shape((width, hid), BF)] if first else []
        return pl.pallas_call(
            part(forward_kernel, half, kept_here, first),
            grid=(2,),
            in_specs=specs,
            out_specs=[
                pl.BlockSpec((1, pair, RING, per, two), lambda i: (core, i, 0, 0, 0)),
                pl.BlockSpec((1, RING, pair, per, hid), lambda i: (core, 0, i, 0, 0)),
                out_full(*chunks),
            ] + [hbm] * len(extra_out),
            out_shape=[shape(ordered(two), F32), shape(ordered(hid), BF), shape(chunks, BF)] + extra_out,
            scratch_shapes=[
                pltpu.VMEM((width, two), BF),
                pltpu.VMEM((width, hid), BF),
                pltpu.VMEM((rows, hid), BF),
                pltpu.VMEM((tokens // 2, width), BF),
                pltpu.SemaphoreType.DMA((4,)),
                pltpu.SemaphoreType.DMA((2,)),
            ],
            input_output_aliases={} if first else {7: 0, 8: 1},
            compiler_params=kernel_params(56),
            cost_estimate=cost((gu_flops + d_flops) // 2, 24 * MIB),
            name=name,
        )(place, *inputs)

    mult, hidden, y_away, w_gu, w_d = forward(
        1, True, (gate_idx, up_idx, down_idx, tiles, *x_core), "forward_away"
    )
    dy_core = [swap(v, "c") for v in dy_own]
    y_recv = swap(y_away, "c")
    mult, hidden, y_kept = forward(0, False, (w_gu, w_d, *x_own, mult, hidden), "forward_kept")
    y_chip = add(y_kept, y_recv)
    mult, y_chip = lax.optimization_barrier((mult, y_chip))
    y_parts = lax.all_to_all(y_chip, ZX, 0, 0, tiled=True)

    steps = 12
    x_tile = lambda i: jnp.minimum(i, 3)
    back_kept, back_away, terms = pl.pallas_call(
        part(gradient_kernel, half, kept_here),
        grid=(steps,),
        in_specs=[smem] * 4
        + [hbm] * 16
        + [
            full(width, hid),
            pl.BlockSpec(
                (1, RING, pair, per, two), lambda i: (x_tile(i) // 2, 0, x_tile(i) % 2, 0, 0)
            ),
            full(tokens, hid),
        ],
        out_specs=[hbm, hbm, out_full(*tiles.shape)],
        out_shape=[shape((tokens // 2, two), BF)] * 2 + [shape(tiles.shape, BF)],
        scratch_shapes=[
            pltpu.VMEM((tokens, width), BF),
            pltpu.VMEM((tokens, width), BF),
            pltpu.VMEM((tokens, two), BF),
            pltpu.VMEM((width, two), BF),
            pltpu.SemaphoreType.DMA((8,)),
            pltpu.SemaphoreType.DMA((32,)),
            pltpu.SemaphoreType.DMA((2,)),
        ],
        compiler_params=kernel_params(60),
        cost_estimate=cost(gu_flops + 2 * d_flops, 40 * MIB),
        name="gradients",
    )(
        place, gate_idx, up_idx, down_idx, *dy_own, *dy_core, *x_own, *x_core,
        w_d, mult, hidden.reshape(tokens, hid),
    )

    def project(left):
        return lax.dot_general(left, w_gu, (((1,), (1,)), ((), ())), preferred_element_type=F32)

    back_away, y_parts = lax.optimization_barrier((back_away, y_parts))
    dx_away = project(back_away).astype(BF)
    dx_recv = swap(dx_away, "c")
    back_kept, dx_away = lax.optimization_barrier((back_kept, dx_away))
    dx_kept, dx_recv = lax.optimization_barrier((project(back_kept).astype(BF), dx_recv))
    dx_chip = add(dx_kept, dx_recv).reshape(chunks)
    dx_parts = lax.all_to_all(dx_chip, ZX, 0, 0, tiled=True)
    y_seq = jnp.sum(y_parts.astype(F32), axis=0).astype(BF)
    dx_seq = jnp.sum(dx_parts.astype(F32), axis=0).astype(BF)

    summed = lax.psum_scatter(terms, "y", scatter_dimension=0, tiled=True)
    summed = summed.reshape(2, half, per_panel, edge, 2 * edge)
    other = swap(summed[1], "zh")
    low = jnp.where(zh == 0, summed[0], other)
    high = jnp.where(zh == 0, other, summed[0])
    grads = jnp.concatenate([low, high], axis=0)
    gu_grads = grads[:, :kept_here]
    d_gate_vals = gu_grads[..., :edge].reshape(panels, kept_here, square)
    d_up_vals = gu_grads[..., edge:].reshape(panels, kept_here, square)
    d_grads = grads[:, kept_here:].reshape(panels, pairs, edge, 2, edge)
    d_down_vals = jnp.transpose(d_grads, (0, 1, 3, 4, 2)).reshape(panels, kept_here, square)
    return (y_seq, dx_seq, d_gate_vals, d_up_vals, d_down_vals)


def solution(mesh):
    grid = Mesh(mesh.devices.reshape(4, 2, 4, 2, 2), AXES)
    row, col = ("y", "zh"), ("x", "zl", "c")
    tokens = P(row + col, None)
    vals = P(col, row, None)
    idx = P(col, None)
    return jax.shard_map(
        per_device,
        mesh=grid,
        in_specs=(tokens, tokens, vals, idx, vals, idx, vals, idx),
        out_specs=(tokens, tokens, vals, vals, vals),
        check_vma=False,
    )
```

time: 1910 us -> 335 us (0.18); the launches traced: 1890 us -> 335 us
  waiting for transfers between devices: 679 us -> 164 us
  other arithmetic: 506 us -> 21.6 us
  local copies, waits for them, and re-layouts: 349 us -> 12.7 us
  matrix products: 306 us -> 14 us
  Pallas kernels: 0 us -> 68.8 us
    unnamed x9 -> x3, waiting for transfers between devices: 431 us -> 0.71 us
    scatter-add x42 -> x0, other arithmetic: 427 us -> none  [the longest x28 285 us: input_panel(): total = total.at[gate_ids].add(gate_contrib).at[up_ids].add(up_contrib)]
    dot_general x126 -> x2, matrix products: 306 us -> 14 us  [project(): lax.dot_general(left, w_gu, (((1,), (1,)), ((), ())), preferred_element_t...]
    gather x70 -> x0, local copies, waits for them, and re-layouts: 202 us -> none  [the longest x14 40.4 us: forward_panel(): up_in = jnp.take(x_blocks, up_ids, axis=0)]
    all_gather x5 -> x2, waiting for transfers between devices: 183 us -> 0.01 us  [the longest x1 0.01 us: per_device(): dy_abs = lax.all_gather(dy_seq, Z, axis=0, tiled=True)]
    ppermute x0 -> x21, waiting for transfers between devices: none -> 134 us  [the longest x12 79.3 us: swap(): return lax.ppermute(value, axis, [(0, 1), (1, 0)])]
    pallas_call x0 -> x3, Pallas kernels: none -> 68.8 us  [the longest x1 35.2 us: per_device(): pl.pallas_call(part(gradient_kernel, half, kept_here), grid=(steps,), in_...]
    reduce_scatter x2 -> x1, waiting for transfers between devices: 55.4 us -> 12.5 us  [per_device(): summed = lax.psum_scatter(terms, 'y', scatter_dimension=0, tiled=True)]
  transfers between devices with their start and end apart: 11 -> 26, of which waited for: 8 -> 18; matrix products, arithmetic and copies ran while one was open for 43% -> 11% of each run, Pallas kernels for 0% -> 15%
where the time goes in v2:
time: 335 us
  waiting for transfers between devices  164 us (49%)
  Pallas kernels  68.8 us (21%)
  starting transfers between devices  39.5 us (12%)
  other arithmetic  21.6 us (6%)
  between operations  14.1 us (4%)
  matrix products  14 us (4%)
  local copies, waits for them, and re-layouts  12.7 us (4%)
    ppermute x12, waiting for transfers between devices, swap(): return lax.ppermute(value, axis, [(0, 1), (1, 0)])  79.3 us
    ppermute x9, waiting for transfers between devices, shift(): lax.ppermute(value, axis, [(i, (i + step) % RING) for i in range(RING)])  55.1 us
    pallas_call x1, Pallas kernels, per_device(): pl.pallas_call(part(gradient_kernel, half, kept_here), grid=(steps,), in_...  35.2 us
    pallas_call x2, Pallas kernels, forward(): pl.pallas_call(part(forward_kernel, half, kept_here, first), grid=(2,), i...  33.6 us
    all_to_all x1, waiting for transfers between devices, per_device(): y_parts = lax.all_to_all(y_chip, ZX, 0, 0, tiled=True)  16.3 us
    dot_general x2, matrix products, project(): lax.dot_general(left, w_gu, (((1,), (1,)), ((), ())), preferred_element_t...  14 us
    ppermute x9, starting transfers between devices, shift(): lax.ppermute(value, axis, [(i, (i + step) % RING) for i in range(RING)])  13.9 us
    reduce_scatter x1, waiting for transfers between devices, per_device(): summed = lax.psum_scatter(terms, 'y', scatter_dimension=0, tiled=True)  12.5 us
  transfers between devices with their start and end apart: 26, of which 18 were waited for; matrix products, arithmetic and copies ran while one was open for 11% of the time, Pallas kernels for 15%

profile of v2, /device:TPU:26, one launch (start us, length us, event | category | flops | bytes accessed | tf_op | source)
XLA Modules:
  0.0 334.6 jit_solution(10130587741740848280)
XLA Ops:
  7.2 0.7 all-gather.3.cloned.1.call-update
  8.0 0.6 collective-permute-start.1
  8.6 2.4 collective-permute-start.2
  11.0 1.8 collective-permute-start.3
  12.8 1.9 reshape.50
  14.7 0.3 copy.19
  15.0 1.9 reshape.48
  16.9 0.7 reshape.49
  17.7 0.5 pad_maximum_fusion
  18.2 0.1 dynamic-slice_bitcast_fusion
  18.3 4.0 %collective-permute-start = (bf16[7,6,64,128]{3,2,1,0:T(8,128)(2,1)S(1)}, bf16[7,6,64,128]{3,2,1,0:T(8,128)(2,1)S(1)}, u32[]{:S(2)}, u32[]{:S(2)}) collective-permute-start(bf16[7,6,64,128]{3,2,1,0:T(8,128)(2,1)S(1)} %get-tuple-element.70), channel_id=1, source_target_pairs={{0,16},{16,0},{1,17},{17,1},{2,18},{18,2},{3,19},{19,3},{4,20},{20... | collective-permute-start | bytes 2064392 | tf_op jit(solution)/shard_map/ppermute | solution.py:23
  22.3 0.7 collective-permute-done.2
  22.9 0.9 collective-permute-done.3
  23.8 1.2 pad_maximum_fusion.2.refs_3_.refs_12_
  25.0 20.3 %collective-permute-done = bf16[7,6,64,128]{3,2,1,0:T(8,128)(2,1)S(1)} collective-permute-done((bf16[7,6,64,128]{3,2,1,0:T(8,128)(2,1)S(1)}, bf16[7,6,64,128]{3,2,1,0:T(8,128)(2,1)S(1)}, u32[]{:S(2)}, u32[]{:S(2)}) %collective-permute-start) | collective-permute-done | bytes 688160 | tf_op jit(solution)/shard_map/ppermute | solution.py:23
  45.3 1.2 pad_maximum_fusion.1
  46.6 0.4 copy-done.14
  47.0 0.6 fusion.refs_4_
  47.6 0.3 collective-permute-start.7
  47.9 1.5 collective-permute-start.8
  49.4 2.3 collective-permute-start.9
  51.7 3.4 %collective-permute-start.4 = (bf16[128,4096]{1,0:T(8,128)(2,1)S(1)}, bf16[128,4096]{1,0:T(8,128)(2,1)S(1)}, u32[]{:S(2)}, u32[]{:S(2)}) collective-permute-start(bf16[128,4096]{1,0:T(8,128)(2,1)S(1)} %pad_maximum_fusion.2.refs_3_.refs_12_), channel_id=1, source_target_pairs={{0,18},{2,0},{16,2},{18,16},{1,19},{3,1},{17,3},{19,17},{4,22},{6,... | collective-permute-start | bytes 3145736 | tf_op jit(solution)/shard_map/ppermute | solution.py:19
  55.1 18.0 %collective-permute-done.7.refs_5_ = bf16[128,4096]{1,0:T(8,128)(2,1)S(1)} collective-permute-done((bf16[128,4096]{1,0:T(8,128)(2,1)S(1)}, bf16[128,4096]{1,0:T(8,128)(2,1)S(1)}, u32[]{:S(2)}, u32[]{:S(2)}) %collective-permute-start.7) | collective-permute-done | bytes 1048608 | tf_op jit(solution)/shard_map/ppermute | solution.py:19
  73.1 1.6 collective-permute-start.6
  74.6 19.2 %collective-permute-done.8.refs_6_ = bf16[128,4096]{1,0:T(8,128)(2,1)S(1)} collective-permute-done((bf16[128,4096]{1,0:T(8,128)(2,1)S(1)}, bf16[128,4096]{1,0:T(8,128)(2,1)S(1)}, u32[]{:S(2)}, u32[]{:S(2)}) %collective-permute-start.8) | collective-permute-done | bytes 1048608 | tf_op jit(solution)/shard_map/ppermute | solution.py:19
  93.8 1.6 collective-permute-done.9.refs_7_
  95.4 1.9 collective-permute-done.4.refs_4_.refs_13_
  97.4 12.8 %collective-permute-done.6.refs_6_.refs_15_ = bf16[128,4096]{1,0:T(8,128)(2,1)} collective-permute-done((bf16[128,4096]{1,0:T(8,128)(2,1)S(1)}, bf16[128,4096]{1,0:T(8,128)(2,1)}, u32[]{:S(2)}, u32[]{:S(2)}) %collective-permute-start.6) | collective-permute-done | bytes 1048608 | tf_op jit(solution)/shard_map/ppermute | solution.py:19
  110.2 0.5 collective-permute-start.15
  110.8 0.4 collective-permute-start.17
  111.3 0.6 pad_add_fusion.refs_0_
  111.8 1.2 collective-permute-done.14.refs_5_.refs_16_
  113.0 3.0 collective-permute-done.15.refs_6_.refs_17_
  116.0 1.5 collective-permute-done.16.refs_7_.refs_18_
  117.5 19.3 %forward_away.1 = (f32[2,4,4,32,896]{4,3,2,1,0:T(8,128)}, bf16[2,4,4,32,512]{4,3,2,1,0:T(8,128)(2,1)}, bf16[16,32,4096]{2,1,0:T(8,128)(2,1)}, bf16[4096,896]{1,0:T(8,128)(2,1)}, bf16[4096,512]{1,0:T(8,128)(2,1)}) custom-call(s32[3]{0:T(128)} %pad_add_fusion.refs_0_, s32[14,32]{1,0:T(8,128)} %refs_1_.3, s32[14,32]{1,0:T(8,128)} %refs_2_.3, s32[14,32]{1,0:T(8,128)} %refs_3_.3, ...), custom_call_target="tpu_custom_call" | custom-call | flops 738197504 | bytes 3145728 | tf_op jit(solution)/shard_map/forward_away/pallas_call | solution.py:415
  136.9 0.2 collective-permute-start.18
  137.1 14.3 %forward_kept.1 = (f32[2,4,4,32,896]{4,3,2,1,0:T(8,128)}, bf16[2,4,4,32,512]{4,3,2,1,0:T(8,128)(2,1)}, bf16[16,32,4096]{2,1,0:T(8,128)(2,1)}) custom-call(s32[3]{0:T(128)} %pad_add_fusion.refs_0_, bf16[4096,896]{1,0:T(8,128)(2,1)} %get-tuple-element.46.refs_1_, ...), custom_call_target="tpu_custom_call", output_to_operand_aliasing={{0}: (7, {}), {1}: (8, {})} | custom-call | flops 738197504 | bytes 3145728 | tf_op jit(solution)/shard_map/forward_kept/pallas_call | solution.py:415
  151.4 6.0 %add_convert_fusion.1 = bf16[16,32,4096]{2,1,0:T(8,128)(2,1)} fusion(bf16[16,32,4096]{2,1,0:T(8,128)(2,1)S(1)} %collective-permute-done.18, bf16[16,32,4096]{2,1,0:T(8,128)(2,1)} %get-tuple-element.50), kind=kLoop, calls=%fused_computation.1 | loop fusion | flops 8388608 | bytes 12582912 | tf_op jit(solution)/shard_map/convert_element_type | solution.py:34
  157.4 6.7 %all-to-all-start = ((bf16[16,32,4096]{2,1,0:T(8,128)(2,1)}), bf16[16,32,4096]{2,1,0:T(8,128)(2,1)}, u32[]{:S(2)}, u32[]{:S(2)}) async-start(bf16[16,32,4096]{2,1,0:T(8,128)(2,1)} %add_convert_fusion.1), calls=%async_computation | async-start | bytes 8388608 | tf_op jit(solution)/shard_map/all_to_all | solution.py:447
  164.2 0.5 collective-permute-start.11
  164.8 0.4 collective-permute-start.13
  165.2 1.6 collective-permute-done.10.refs_8_
  166.9 3.0 collective-permute-done.11.refs_9_
  169.9 1.5 collective-permute-done.12.refs_10_
  171.4 0.9 copy-done.12
  172.3 0.4 copy-done.13
  172.7 35.2 %gradients.1 = (bf16[512,896]{1,0:T(8,128)(2,1)}, bf16[512,896]{1,0:T(8,128)(2,1)}, bf16[336,64,128]{2,1,0:T(8,128)(2,1)}) custom-call(s32[3]{0:T(128)} %pad_add_fusion.refs_0_, s32[14,32]{1,0:T(8,128)} %refs_1_.3, s32[14,32]{1,0:T(8,128)} %refs_2_.3, s32[14,32]{1,0:T(8,128)} %refs_3_.3, bf16[128,4096]{1,0:T(8,128)(2,1)} %copy-done.3, ...), custom_call_target="tpu_custom_call" | custom-call | flops 2013265920 | bytes 5242880 | tf_op jit(solution)/shard_map/gradients/pallas_call | solution.py:451
  207.9 16.3 %all-to-all-done = bf16[16,32,4096]{2,1,0:T(8,128)(2,1)} async-done(((bf16[16,32,4096]{2,1,0:T(8,128)(2,1)}), bf16[16,32,4096]{2,1,0:T(8,128)(2,1)}, u32[]{:S(2)}, u32[]{:S(2)}) %all-to-all-start) | async-done | bytes 4194336 | tf_op jit(solution)/shard_map/all_to_all | solution.py:447
  224.2 8.0 %convolution_convert_fusion.1 = bf16[512,4096]{1,0:T(8,128)(2,1)S(1)} fusion(bf16[512,896]{1,0:T(8,128)(2,1)} %get-tuple-element.58, bf16[4096,896]{1,0:T(8,128)(2,1)} %get-tuple-element.46.refs_1_), kind=kOutput, calls=%fused_computation.3 | convolution fusion | flops 3760193536 | bytes 12451840 | tf_op jit(solution)/shard_map/dot_general | solution.py:483
  232.4 6.0 %convolution_convert_fusion = bf16[512,4096]{1,0:T(8,128)(2,1)S(1)} fusion(bf16[512,896]{1,0:T(8,128)(2,1)} %get-tuple-element.59, bf16[4096,896]{1,0:T(8,128)(2,1)S(1)} %bitcast.29), kind=kOutput, calls=%fused_computation.2 | convolution fusion | flops 3760193536 | bytes 12451840 | tf_op jit(solution)/shard_map/dot_general | solution.py:483
  238.3 1.1 collective-permute-done.19
  239.5 3.6 %add_convert_fusion = bf16[512,4096]{1,0:T(8,128)(2,1)} fusion(bf16[512,4096]{1,0:T(8,128)(2,1)S(1)} %collective-permute-done.19, bf16[512,4096]{1,0:T(8,128)(2,1)S(1)} %convolution_convert_fusion), kind=kLoop, calls=%fused_computation | loop fusion | flops 8388608 | bytes 12582912 | tf_op jit(solution)/shard_map/convert_element_type | solution.py:34
  243.1 9.0 %all-to-all-start.1 = ((bf16[16,32,4096]{2,1,0:T(8,128)(2,1)}), bf16[16,32,4096]{2,1,0:T(8,128)(2,1)}, u32[]{:S(2)}, u32[]{:S(2)}) async-start(bf16[16,32,4096]{2,1,0:T(8,128)(2,1)} %bitcast.27), calls=%async_computation.1 | async-start | bytes 8388608 | tf_op jit(solution)/shard_map/all_to_all | solution.py:491
  252.1 12.5 %reduce-scatter.2.cloned.1.call-done = bf16[84,64,128]{2,1,0:T(8,128)(2,1)} async-done(((bf16[336,64,128]{2,1,0:T(8,128)(2,1)}), bf16[84,64,128]{2,1,0:T(8,128)(2,1)}) %reduce-scatter.2.cloned.1.call-update) | async-done | bytes 1376272 | tf_op jit(solution)/shard_map/reduce_scatter | solution.py:495
  264.6 1.4 fusion.3
  266.0 3.5 %collective-permute-start.20 = (bf16[7,6,64,128]{3,2,1,0:T(8,128)(2,1)S(1)}, bf16[7,6,64,128]{3,2,1,0:T(8,128)(2,1)S(1)}, u32[]{:S(2)}, u32[]{:S(2)}) collective-permute-start(bf16[7,6,64,128]{3,2,1,0:T(8,128)(2,1)S(1)} %bitcast.36), channel_id=1, source_target_pairs={{0,16},{16,0},{1,17},{17,1},{2,18},{18,2},{3,19},{19,3},{4,20},{20... | collective-permute-start | bytes 2064392 | tf_op jit(solution)/shard_map/ppermute | solution.py:23
  269.5 3.7 %reduce_sum.24 = bf16[32,4096]{1,0:T(8,128)(2,1)} reduce(bf16[16,32,4096]{2,1,0:T(8,128)(2,1)} %all-to-all-done, bf16[]{:T(256)} %constant.49.clone.1), dimensions={0}, to_apply=%region_0.1 | reduce | flops 1966080 | bytes 4456450 | tf_op jit(solution)/shard_map/reduce_sum | solution.py:492
  273.2 46.1 %collective-permute-done.20 = bf16[7,6,64,128]{3,2,1,0:T(8,128)(2,1)S(1)} collective-permute-done((bf16[7,6,64,128]{3,2,1,0:T(8,128)(2,1)S(1)}, bf16[7,6,64,128]{3,2,1,0:T(8,128)(2,1)S(1)}, u32[]{:S(2)}, u32[]{:S(2)}) %collective-permute-start.20) | collective-permute-done | bytes 688160 | tf_op jit(solution)/shard_map/ppermute | solution.py:23
  319.4 0.4 copy.20
  319.9 1.4 reshape.58
  321.3 0.3 fusion.1
  321.6 1.4 reshape.55
  323.0 1.4 reshape.56
  324.4 3.7 %reduce_sum.25 = bf16[32,4096]{1,0:T(8,128)(2,1)} reduce(bf16[16,32,4096]{2,1,0:T(8,128)(2,1)} %all-to-all-done.1, bf16[]{:T(256)} %constant.49.clone.1), dimensions={0}, to_apply=%region_1.2 | reduce | flops 1966080 | bytes 4456450 | tf_op jit(solution)/shard_map/reduce_sum | solution.py:493
  (57 shorter events, 0.7 us)
Async XLA Ops:
  7.2 9.8 %copy-start.15 = (bf16[14,4,4096]{2,1,0:T(4,128)(2,1)S(1)}, bf16[14,4,4096]{2,1,0:T(4,128)(2,1)}, u32[]{:S(2)}) copy-start(bf16[14,4,4096]{2,1,0:T(4,128)(2,1)} %param.12) | copy-start | bytes 1376260
  7.2 38.1 %all-gather.3.cloned.1.call-start = ((), (), s32[]{:S(2)}) async-start(), calls=%async_computation.3 | async-start | bytes 1310720 | tf_op jit(solution)/shard_map/all_gather | solution.py:379
  7.9 109.6 %all-gather.5.cloned.1.call-start = ((), (), s32[]{:S(2)}) async-start(), calls=%async_computation.4 | async-start | bytes 6881280 | tf_op jit(solution)/shard_map/all_gather | solution.py:383
  8.0 14.3 %collective-permute-start.1 = (bf16[32,4096]{1,0:T(8,128)(2,1)}, bf16[32,4096]{1,0:T(8,128)(2,1)}, u32[]{:S(2)}, u32[]{:S(2)}) collective-permute-start(bf16[32,4096]{1,0:T(8,128)(2,1)} %param.8), channel_id=1, source_target_pairs={{0,12},{4,0},{8,4},{12,8},{1,13},{5,1},{9,5},{13,9},{2,14},{6,2},{... | collective-permute-start | bytes 786440 | tf_op jit(solution)/shard_map/ppermute | solution.py:19
  8.6 14.4 %collective-permute-start.2 = (bf16[32,4096]{1,0:T(8,128)(2,1)}, bf16[32,4096]{1,0:T(8,128)(2,1)}, u32[]{:S(2)}, u32[]{:S(2)}) collective-permute-start(bf16[32,4096]{1,0:T(8,128)(2,1)} %param.8), channel_id=1, source_target_pairs={{0,8},{4,12},{8,0},{12,4},{1,9},{5,13},{9,1},{13,5},{2,10},{6,14},... | collective-permute-start | bytes 786440 | tf_op jit(solution)/shard_map/ppermute | solution.py:19
  11.0 12.9 %collective-permute-start.3 = (bf16[32,4096]{1,0:T(8,128)(2,1)}, bf16[32,4096]{1,0:T(8,128)(2,1)}, u32[]{:S(2)}, u32[]{:S(2)}) collective-permute-start(bf16[32,4096]{1,0:T(8,128)(2,1)} %param.8), channel_id=1, source_target_pairs={{0,4},{4,8},{8,12},{12,0},{1,5},{5,9},{9,13},{13,1},{2,6},{6,10},{... | collective-permute-start | bytes 786440 | tf_op jit(solution)/shard_map/ppermute | solution.py:19
  17.7 6.2 %copy-start.16 = (bf16[32,4096]{1,0:T(8,128)(2,1)S(1)}, bf16[32,4096]{1,0:T(8,128)(2,1)}, u32[]{:S(2)}) copy-start(bf16[32,4096]{1,0:T(8,128)(2,1)} %param.8) | copy-start | bytes 786436
  18.3 27.0 %collective-permute-start = (bf16[7,6,64,128]{3,2,1,0:T(8,128)(2,1)S(1)}, bf16[7,6,64,128]{3,2,1,0:T(8,128)(2,1)S(1)}, u32[]{:S(2)}, u32[]{:S(2)}) collective-permute-start(bf16[7,6,64,128]{3,2,1,0:T(8,128)(2,1)S(1)} %get-tuple-element.70), channel_id=1, source_target_pairs={{0,16},{16,0},{1,17},{17,1},{2,18},{18,2},{3,19},{19,3},{4,20},{20... | collective-permute-start | bytes 2064392 | tf_op jit(solution)/shard_map/ppermute | solution.py:23
  25.0 111.8 %copy-start = (bf16[128,4096]{1,0:T(8,128)(2,1)}, bf16[128,4096]{1,0:T(8,128)(2,1)S(1)}, u32[]{:S(2)}) copy-start(bf16[128,4096]{1,0:T(8,128)(2,1)S(1)} %pad_maximum_fusion.2.refs_3_.refs_12_) | copy-start | bytes 3145732
  45.3 1.7 copy-start.14
  47.6 62.7 %copy-start.3 = (bf16[128,4096]{1,0:T(8,128)(2,1)}, bf16[128,4096]{1,0:T(8,128)(2,1)S(1)}, u32[]{:S(2)}) copy-start(bf16[128,4096]{1,0:T(8,128)(2,1)S(1)} %fusion.refs_4_) | copy-start | bytes 3145732
  47.6 25.5 %collective-permute-start.7 = (bf16[128,4096]{1,0:T(8,128)(2,1)S(1)}, bf16[128,4096]{1,0:T(8,128)(2,1)S(1)}, u32[]{:S(2)}, u32[]{:S(2)}) collective-permute-start(bf16[128,4096]{1,0:T(8,128)(2,1)S(1)} %fusion.refs_4_), channel_id=1, source_target_pairs={{0,12},{4,0},{8,4},{12,8},{1,13},{5,1},{9,5},{13,9},{2,14},{6,2},{... | collective-permute-start | bytes 3145736 | tf_op jit(solution)/shard_map/ppermute | solution.py:19
  47.9 45.9 %collective-permute-start.8 = (bf16[128,4096]{1,0:T(8,128)(2,1)S(1)}, bf16[128,4096]{1,0:T(8,128)(2,1)S(1)}, u32[]{:S(2)}, u32[]{:S(2)}) collective-permute-start(bf16[128,4096]{1,0:T(8,128)(2,1)S(1)} %fusion.refs_4_), channel_id=1, source_target_pairs={{0,8},{4,12},{8,0},{12,4},{1,9},{5,13},{9,1},{13,5},{2,10},{6,14},... | collective-permute-start | bytes 3145736 | tf_op jit(solution)/shard_map/ppermute | solution.py:19
  49.4 46.1 %collective-permute-start.9 = (bf16[128,4096]{1,0:T(8,128)(2,1)S(1)}, bf16[128,4096]{1,0:T(8,128)(2,1)S(1)}, u32[]{:S(2)}, u32[]{:S(2)}) collective-permute-start(bf16[128,4096]{1,0:T(8,128)(2,1)S(1)} %fusion.refs_4_), channel_id=1, source_target_pairs={{0,4},{4,8},{8,12},{12,0},{1,5},{5,9},{9,13},{13,1},{2,6},{6,10},{... | collective-permute-start | bytes 3145736 | tf_op jit(solution)/shard_map/ppermute | solution.py:19
  51.7 45.7 %collective-permute-start.4 = (bf16[128,4096]{1,0:T(8,128)(2,1)S(1)}, bf16[128,4096]{1,0:T(8,128)(2,1)S(1)}, u32[]{:S(2)}, u32[]{:S(2)}) collective-permute-start(bf16[128,4096]{1,0:T(8,128)(2,1)S(1)} %pad_maximum_fusion.2.refs_3_.refs_12_), channel_id=1, source_target_pairs={{0,18},{2,0},{16,2},{18,16},{1,19},{3,1},{17,3},{19,17},{4,22},{6,... | collective-permute-start | bytes 3145736 | tf_op jit(solution)/shard_map/ppermute | solution.py:19
  55.1 42.3 %collective-permute-start.5 = (bf16[128,4096]{1,0:T(8,128)(2,1)S(1)}, bf16[128,4096]{1,0:T(8,128)(2,1)S(1)}, u32[]{:S(2)}, u32[]{:S(2)}) collective-permute-start(bf16[128,4096]{1,0:T(8,128)(2,1)S(1)} %pad_maximum_fusion.2.refs_3_.refs_12_), channel_id=1, source_target_pairs={{0,16},{2,18},{16,0},{18,2},{1,17},{3,19},{17,1},{19,3},{4,20},{6,... | collective-permute-start | bytes 3145736 | tf_op jit(solution)/shard_map/ppermute | solution.py:19
  73.1 37.7 %copy-start.5 = (bf16[128,4096]{1,0:T(8,128)(2,1)}, bf16[128,4096]{1,0:T(8,128)(2,1)S(1)}, u32[]{:S(2)}) copy-start(bf16[128,4096]{1,0:T(8,128)(2,1)S(1)} %collective-permute-done.7.refs_5_) | copy-start | bytes 3145732
  73.1 37.2 %collective-permute-start.6 = (bf16[128,4096]{1,0:T(8,128)(2,1)S(1)}, bf16[128,4096]{1,0:T(8,128)(2,1)}, u32[]{:S(2)}, u32[]{:S(2)}) collective-permute-start(bf16[128,4096]{1,0:T(8,128)(2,1)S(1)} %pad_maximum_fusion.2.refs_3_.refs_12_), channel_id=1, source_target_pairs={{0,2},{2,16},{16,18},{18,0},{1,3},{3,17},{17,19},{19,1},{4,6},{6,2... | collective-permute-start | bytes 3145736 | tf_op jit(solution)/shard_map/ppermute | solution.py:19
  93.8 17.0 %copy-start.7 = (bf16[128,4096]{1,0:T(8,128)(2,1)}, bf16[128,4096]{1,0:T(8,128)(2,1)S(1)}, u32[]{:S(2)}) copy-start(bf16[128,4096]{1,0:T(8,128)(2,1)S(1)} %collective-permute-done.8.refs_6_) | copy-start | bytes 3145732
  95.4 15.4 %copy-start.9 = (bf16[128,4096]{1,0:T(8,128)(2,1)}, bf16[128,4096]{1,0:T(8,128)(2,1)S(1)}, u32[]{:S(2)}) copy-start(bf16[128,4096]{1,0:T(8,128)(2,1)S(1)} %collective-permute-done.9.refs_7_) | copy-start | bytes 3145732
  97.4 39.5 %copy-start.1 = (bf16[128,4096]{1,0:T(8,128)(2,1)}, bf16[128,4096]{1,0:T(8,128)(2,1)S(1)}, u32[]{:S(2)}) copy-start(bf16[128,4096]{1,0:T(8,128)(2,1)S(1)} %collective-permute-done.4.refs_4_.refs_13_) | copy-start | bytes 3145732
  97.4 39.5 %copy-start.2 = (bf16[128,4096]{1,0:T(8,128)(2,1)}, bf16[128,4096]{1,0:T(8,128)(2,1)S(1)}, u32[]{:S(2)}) copy-start(bf16[128,4096]{1,0:T(8,128)(2,1)S(1)} %collective-permute-done.5.refs_5_.refs_14_) | copy-start | bytes 3145732
  110.2 2.8 collective-permute-start.14
  110.2 5.8 %collective-permute-start.15 = (bf16[128,4096]{1,0:T(8,128)(2,1)S(1)}, bf16[128,4096]{1,0:T(8,128)(2,1)}, u32[]{:S(2)}, u32[]{:S(2)}) collective-permute-start(bf16[128,4096]{1,0:T(8,128)(2,1)S(1)} %collective-permute-done.4.refs_4_.refs_13_), channel_id=1, source_target_pairs={{0,1},{1,0},{2,3},{3,2},{4,5},{5,4},{6,7},{7,6},{8,9},{9,8},{10,11... | collective-permute-start | bytes 3145736 | tf_op jit(solution)/shard_map/ppermute | solution.py:23
  110.7 6.8 %collective-permute-start.16 = (bf16[128,4096]{1,0:T(8,128)(2,1)S(1)}, bf16[128,4096]{1,0:T(8,128)(2,1)}, u32[]{:S(2)}, u32[]{:S(2)}) collective-permute-start(bf16[128,4096]{1,0:T(8,128)(2,1)S(1)} %collective-permute-done.5.refs_5_.refs_14_), channel_id=1, source_target_pairs={{0,1},{1,0},{2,3},{3,2},{4,5},{5,4},{6,7},{7,6},{8,9},{9,8},{10,11... | collective-permute-start | bytes 3145736 | tf_op jit(solution)/shard_map/ppermute | solution.py:23
  110.8 6.7 %collective-permute-start.17 = (bf16[128,4096]{1,0:T(8,128)(2,1)}, bf16[128,4096]{1,0:T(8,128)(2,1)}, u32[]{:S(2)}, u32[]{:S(2)}) collective-permute-start(bf16[128,4096]{1,0:T(8,128)(2,1)} %collective-permute-done.6.refs_6_.refs_15_), channel_id=1, source_target_pairs={{0,1},{1,0},{2,3},{3,2},{4,5},{5,4},{6,7},{7,6},{8,9},{9,8},{10,11... | collective-permute-start | bytes 3145736 | tf_op jit(solution)/shard_map/ppermute | solution.py:23
  136.9 14.6 %collective-permute-start.18 = (bf16[16,32,4096]{2,1,0:T(8,128)(2,1)}, bf16[16,32,4096]{2,1,0:T(8,128)(2,1)S(1)}, u32[]{:S(2)}, u32[]{:S(2)}) collective-permute-start(bf16[16,32,4096]{2,1,0:T(8,128)(2,1)} %get-tuple-element.51), channel_id=1, source_target_pairs={{0,1},{1,0},{2,3},{3,2},{4,5},{5,4},{6,7},{7,6},{8,9},{9,8},{10,11... | collective-permute-start | bytes 12582920 | tf_op jit(solution)/shard_map/ppermute | solution.py:23
  157.4 6.7 %copy-start.4 = (bf16[128,4096]{1,0:T(8,128)(2,1)S(1)}, bf16[128,4096]{1,0:T(8,128)(2,1)}, u32[]{:S(2)}) copy-start(bf16[128,4096]{1,0:T(8,128)(2,1)} %copy-done.3) | copy-start | bytes 3145732
  157.4 6.8 %copy-start.6 = (bf16[128,4096]{1,0:T(8,128)(2,1)S(1)}, bf16[128,4096]{1,0:T(8,128)(2,1)}, u32[]{:S(2)}) copy-start(bf16[128,4096]{1,0:T(8,128)(2,1)} %copy-done.5) | copy-start | bytes 3145732
  157.4 7.3 %copy-start.8 = (bf16[128,4096]{1,0:T(8,128)(2,1)S(1)}, bf16[128,4096]{1,0:T(8,128)(2,1)}, u32[]{:S(2)}) copy-start(bf16[128,4096]{1,0:T(8,128)(2,1)} %copy-done.7) | copy-start | bytes 3145732
  157.4 66.8 %all-to-all-start = ((bf16[16,32,4096]{2,1,0:T(8,128)(2,1)}), bf16[16,32,4096]{2,1,0:T(8,128)(2,1)}, u32[]{:S(2)}, u32[]{:S(2)}) async-start(bf16[16,32,4096]{2,1,0:T(8,128)(2,1)} %add_convert_fusion.1), calls=%async_computation | async-start | bytes 8388608 | tf_op jit(solution)/shard_map/all_to_all | solution.py:447
  164.1 100.5 %reduce-scatter.2.cloned.1.call-start = ((), (), s32[]{:S(2)}) async-start(), calls=%async_computation.5 | async-start | bytes 6881280 | tf_op jit(solution)/shard_map/reduce_scatter | solution.py:495
  164.1 2.7 collective-permute-start.10
  164.2 5.6 %collective-permute-start.11 = (bf16[128,4096]{1,0:T(8,128)(2,1)S(1)}, bf16[128,4096]{1,0:T(8,128)(2,1)S(1)}, u32[]{:S(2)}, u32[]{:S(2)}) collective-permute-start(bf16[128,4096]{1,0:T(8,128)(2,1)S(1)} %copy-done.6), channel_id=1, source_target_pairs={{0,1},{1,0},{2,3},{3,2},{4,5},{5,4},{6,7},{7,6},{8,9},{9,8},{10,11... | collective-permute-start | bytes 3145736 | tf_op jit(solution)/shard_map/ppermute | solution.py:23
  164.7 6.6 %collective-permute-start.12 = (bf16[128,4096]{1,0:T(8,128)(2,1)S(1)}, bf16[128,4096]{1,0:T(8,128)(2,1)S(1)}, u32[]{:S(2)}, u32[]{:S(2)}) collective-permute-start(bf16[128,4096]{1,0:T(8,128)(2,1)S(1)} %copy-done.8), channel_id=1, source_target_pairs={{0,1},{1,0},{2,3},{3,2},{4,5},{5,4},{6,7},{7,6},{8,9},{9,8},{10,11... | collective-permute-start | bytes 3145736 | tf_op jit(solution)/shard_map/ppermute | solution.py:23
  164.8 6.6 %collective-permute-start.13 = (bf16[128,4096]{1,0:T(8,128)(2,1)}, bf16[128,4096]{1,0:T(8,128)(2,1)S(1)}, u32[]{:S(2)}, u32[]{:S(2)}) collective-permute-start(bf16[128,4096]{1,0:T(8,128)(2,1)} %copy-done.9), channel_id=1, source_target_pairs={{0,1},{1,0},{2,3},{3,2},{4,5},{5,4},{6,7},{7,6},{8,9},{9,8},{10,11... | collective-permute-start | bytes 3145736 | tf_op jit(solution)/shard_map/ppermute | solution.py:23
  166.9 4.5 %copy-start.10 = (bf16[128,4096]{1,0:T(8,128)(2,1)}, bf16[128,4096]{1,0:T(8,128)(2,1)S(1)}, u32[]{:S(2)}) copy-start(bf16[128,4096]{1,0:T(8,128)(2,1)S(1)} %collective-permute-done.10.refs_8_) | copy-start | bytes 3145732
  169.9 1.5 copy-start.11
  171.4 0.9 copy-start.12
  171.4 1.3 copy-start.13
  207.9 24.5 %slice-start = ((s8[7340032]{0:T(1024)(128)(4,1)}), s8[3145728]{0:T(1024)(128)(4,1)S(1)}, s32[]{:S(2)}) async-start(s8[7340032]{0:T(1024)(128)(4,1)} %bitcast.28), calls=%async_computation.6 | async-start | bytes 6291456
  224.2 8.2 %slice-start.1 = ((s8[7340032]{0:T(1024)(128)(4,1)}), s8[4194304]{0:T(1024)(128)(4,1)S(1)}, s32[]{:S(2)}) async-start(s8[7340032]{0:T(1024)(128)(4,1)} %bitcast.28), calls=%async_computation.7 | async-start | bytes 8388608
  232.3 7.2 %collective-permute-start.19 = (bf16[512,4096]{1,0:T(8,128)(2,1)S(1)}, bf16[512,4096]{1,0:T(8,128)(2,1)S(1)}, u32[]{:S(2)}, u32[]{:S(2)}) collective-permute-start(bf16[512,4096]{1,0:T(8,128)(2,1)S(1)} %convolution_convert_fusion.1), channel_id=1, source_target_pairs={{0,1},{1,0},{2,3},{3,2},{4,5},{5,4},{6,7},{7,6},{8,9},{9,8},{10,11... | collective-permute-start | bytes 12582920 | tf_op jit(solution)/shard_map/ppermute | solution.py:23
  243.1 81.3 %all-to-all-start.1 = ((bf16[16,32,4096]{2,1,0:T(8,128)(2,1)}), bf16[16,32,4096]{2,1,0:T(8,128)(2,1)}, u32[]{:S(2)}, u32[]{:S(2)}) async-start(bf16[16,32,4096]{2,1,0:T(8,128)(2,1)} %bitcast.27), calls=%async_computation.1 | async-start | bytes 8388608 | tf_op jit(solution)/shard_map/all_to_all | solution.py:491
  266.0 53.3 %collective-permute-start.20 = (bf16[7,6,64,128]{3,2,1,0:T(8,128)(2,1)S(1)}, bf16[7,6,64,128]{3,2,1,0:T(8,128)(2,1)S(1)}, u32[]{:S(2)}, u32[]{:S(2)}) collective-permute-start(bf16[7,6,64,128]{3,2,1,0:T(8,128)(2,1)S(1)} %bitcast.36), channel_id=1, source_target_pairs={{0,16},{16,0},{1,17},{17,1},{2,18},{18,2},{3,19},{19,3},{4,20},{20... | collective-permute-start | bytes 2064392 | tf_op jit(solution)/shard_map/ppermute | solution.py:23
Sparse Core Ops, SparseCore 0:
  9.7 33.2 all-gather.2
  46.7 58.2 all-gather.4
  208.0 56.5 reduce-scatter.1

commit v3 on v2

--- a/solution.py
+++ b/solution.py
@@ -28,6 +28,15 @@
     above = shift(own, axis, -1)
     across = shift(own, axis, 2)
     return [own, above, across, below]
+
+
+def scatter_direct(chunks, axis):
+    from_below = shift(chunks[1], axis, 1)
+    from_above = shift(chunks[3], axis, -1)
+    from_across = shift(chunks[2], axis, 2)
+    total = chunks[0].astype(F32) + from_below.astype(F32)
+    total = total + from_above.astype(F32) + from_across.astype(F32)
+    return total.astype(BF)
 
 
 def add(first, second):
@@ -76,6 +85,16 @@
     return copies
 
 
+def ring_copies(pieces, buf, sems, place):
+    per = pieces[0].shape[2]
+    copies = []
+    for n in range(2 * RING * RING):
+        core, x, z = n // (RING * RING), n // RING % RING, n % RING
+        source = pieces[core].at[(place[2] + x) % RING, (place[1] + z) % RING]
+        copies.append(pltpu.make_async_copy(source, buf.at[pl.ds(n * per, per)], sems.at[n]))
+    return copies
+
+
 def tile_wait(copies, i):
     for t in range(len(copies) // 2):
 
@@ -101,20 +120,25 @@
         return pl.multiple_of(idx_ref[self.zh * self.half_panels + p, j] * BLK, BLK)
 
 
+def put_blocks(w_ref, places):
+    mask = left_half((BLK, 2 * BLK))
+    old = [w_ref[rows, lanes] for rows, lanes, _, _ in places]
+    for before, (rows, lanes, tile, left) in zip(old, places):
+        w_ref[rows, lanes] = jnp.where(mask, tile, before) if left else jnp.where(mask, before, tile)
+
+
 def build_input_weights(where, gate_idx, up_idx, tiles, w_ref):
     w_ref[...] = jnp.zeros_like(w_ref)
-    mask = left_half((BLK, 2 * BLK))
 
     def put(step, carry):
         group, k = step // where.kept_here, step % where.kept_here
         j = where.kept(group, k)
-        for p in range(where.half_panels):
-            tile = tiles[where.at(group, p, k)]
-            lanes = pl.ds(p * 2 * BLK, 2 * BLK)
-            for idx_ref, left in ((gate_idx, True), (up_idx, False)):
-                rows = pl.ds(where.row(idx_ref, p, j), BLK)
-                old = w_ref[rows, lanes]
-                w_ref[rows, lanes] = jnp.where(mask, tile, old) if left else jnp.where(mask, old, tile)
+        block = [tiles[where.at(group, p, k)] for p in range(where.half_panels)]
+        for idx_ref, left in ((gate_idx, True), (up_idx, False)):
+            put_blocks(w_ref, [
+                (pl.ds(where.row(idx_ref, p, j), BLK), pl.ds(p * 2 * BLK, 2 * BLK), block[p], left)
+                for p in range(where.half_panels)
+            ])
         return carry
 
     lax.fori_loop(0, 2 * RING * where.kept_here, put, 0)
@@ -122,29 +146,25 @@
 
 def build_down_weights(where, down_idx, tiles, w_ref):
     w_ref[...] = jnp.zeros_like(w_ref)
-    mask = left_half((BLK, 2 * BLK))
 
     def put(step, carry):
         group, m = step // where.pairs, step % where.pairs
         j = where.kept(group, 2 * m)
-        for p in range(where.half_panels):
-            tile = tiles[where.at(group, p, where.kept_here + m)]
-            turned = flip(tile)
-            lanes = pl.ds((p // 2) * 128, 128)
-            for h in range(2):
-                rows = pl.ds(where.row(down_idx, p, j + h), BLK)
-                source = tile if h == p % 2 else turned
-                old = w_ref[rows, lanes]
-                if p % 2 == 0:
-                    w_ref[rows, lanes] = jnp.where(mask, source, old)
-                else:
-                    w_ref[rows, lanes] = jnp.where(mask, old, source)
+        for parity in range(2):
+            places = []
+            for p in range(parity, where.half_panels, 2):
+                tile = tiles[where.at(group, p, where.kept_here + m)]
+                for h in range(2):
+                    rows = pl.ds(where.row(down_idx, p, j + h), BLK)
+                    source = tile if h == parity else flip(tile)
+                    places.append((rows, pl.ds((p // 2) * 128, 128), source, parity == 0))
+            put_blocks(w_ref, places)
         return carry
 
     lax.fori_loop(0, 2 * RING * where.pairs, put, 0)
 
 
-def back_rows(left, w_ref, out_ref, place, i):
+def back_rows(left, w_ref, out_ref, i):
     width = w_ref.shape[0]
     step = min(width, 1024)
     per = out_ref.shape[1]
@@ -156,9 +176,8 @@
         for a in range(RING // 2):
             for b in range(RING):
                 at = (a * RING + b) * per
-                z = (place[1] + i * (RING // 2) + a) % RING
-                x = (place[2] + b) % RING
-                out_ref[z * RING + x, :, start : start + step] = part[at : at + per]
+                chunk = (i * (RING // 2) + a) * RING + b
+                out_ref[chunk, :, start : start + step] = part[at : at + per]
 
 
 def forward_tile(half_panels, x_tile, w_ref, m_ref, h_ref, h2_ref):
@@ -233,7 +252,7 @@
         def _():
             w_copies[1].wait()
 
-    back_rows(h_ref[...], wd_ref, y_ref, place, i)
+    back_rows(h_ref[...], wd_ref, y_ref, i)
     if first:
 
         @pl.when(i == pl.num_programs(0) - 1)
@@ -243,12 +262,12 @@
 
 
 def gradient_kernel(half_panels, kept_here, place, gate_idx, up_idx, down_idx, *refs):
-    dy_pieces, x_pieces = refs[:8], refs[8:16]
-    wd_ref, m_ref, h_ref, back_kept, back_away, out_ref, dy_buf, x_buf, g_ref, acc, dy_sems, x_sems, g_sems = refs[16:]
+    dy_pieces, x_pieces = refs[:2], refs[2:10]
+    wd_ref, m_ref, h_ref, back_kept, back_away, out_ref, dy_buf, x_buf, g_ref, acc, dy_sems, x_sems, g_sems = refs[10:]
     i = pl.program_id(0)
     where = Tiles(half_panels, kept_here, place[0])
     rows = dy_buf.shape[0] // 4
-    dy_copies = row_copies(dy_pieces, dy_buf, dy_sems)
+    dy_copies = ring_copies(dy_pieces, dy_buf, dy_sems, place)
     x_copies = chunk_copies(x_pieces, x_buf, x_sems, place)
     half_rows = back_kept.shape[0]
     g_copies = [
@@ -267,7 +286,12 @@
         for copy in x_copies:
             copy.start()
 
-    tile_wait(dy_copies, i)
+    for t in range(4):
+
+        @pl.when(i == t)
+        def _(t=t):
+            for copy in dy_copies[8 * t : 8 * t + 8]:
+                copy.wait()
 
     @pl.when(i < 4)
     def _():
@@ -376,17 +400,20 @@
     own = lax.dynamic_slice_in_dim(all_pairs, zh * half, half, 0)
     other = swap(lax.dynamic_slice_in_dim(all_pairs, (1 - zh) * half, half, 0), "zh")
 
-    dy_abs = lax.all_gather(dy_seq, Z, axis=0, tiled=True)
+    def gather_all(value, axis):
+        wide = jnp.broadcast_to(value[None], (RING, *value.shape))
+        return lax.all_to_all(wide, axis, 0, 0, tiled=True)
+
+    dy_row = gather_all(dy_seq, Z)
     x_row = jnp.concatenate(gather_direct(x_seq, "x"), axis=0)
-    other, dy_abs, x_row = lax.optimization_barrier((other, dy_abs, x_row))
+    other, x_row, dy_row = lax.optimization_barrier((other, x_row, dy_row))
     both = jnp.stack([own, other]).reshape(-1, edge, 2 * edge)
     tiles = lax.all_gather(both, "y", axis=0, tiled=True)
-    dy_row = jnp.roll(dy_abs, -z_place * per, axis=0)
+    dy_own = gather_all(dy_row, "x")
     x_own = gather_direct(x_row, Z)
-    dy_below, dy_above = shift(dy_row, "x", 1), shift(dy_row, "x", -1)
-    dy_own = [dy_row, dy_above, shift(dy_row, "x", 2), dy_below]
-    x_own, dy_own = lax.optimization_barrier((x_own, dy_own))
     x_core = [swap(v, "c") for v in x_own]
+    x_core, dy_own = lax.optimization_barrier((x_core, dy_own))
+    dy_core = swap(dy_own, "c")
 
     tokens = 2 * RING * RING * per
     rows = tokens // 4
@@ -439,12 +466,13 @@
     mult, hidden, y_away, w_gu, w_d = forward(
         1, True, (gate_idx, up_idx, down_idx, tiles, *x_core), "forward_away"
     )
-    dy_core = [swap(v, "c") for v in dy_own]
     y_recv = swap(y_away, "c")
     mult, hidden, y_kept = forward(0, False, (w_gu, w_d, *x_own, mult, hidden), "forward_kept")
-    y_chip = add(y_kept, y_recv)
-    mult, y_chip = lax.optimization_barrier((mult, y_chip))
-    y_parts = lax.all_to_all(y_chip, ZX, 0, 0, tiled=True)
+    y_kept, dy_core = lax.optimization_barrier((y_kept, dy_core))
+    dy_pieces = [v.reshape(RING, RING, per, width) for v in (dy_own, dy_core)]
+    y_sum = [add(y_kept[n * RING : n * RING + RING], y_recv[n * RING : n * RING + RING]) for n in range(RING)]
+    mult, y_sum = lax.optimization_barrier((mult, y_sum))
+    y_z = scatter_direct(y_sum, Z)
 
     steps = 12
     x_tile = lambda i: jnp.minimum(i, 3)
@@ -452,7 +480,7 @@
         part(gradient_kernel, half, kept_here),
         grid=(steps,),
         in_specs=[smem] * 4
-        + [hbm] * 16
+        + [hbm] * 10
         + [
             full(width, hid),
             pl.BlockSpec(
@@ -467,7 +495,7 @@
             pltpu.VMEM((tokens, width), BF),
             pltpu.VMEM((tokens, two), BF),
             pltpu.VMEM((width, two), BF),
-            pltpu.SemaphoreType.DMA((8,)),
+            pltpu.SemaphoreType.DMA((32,)),
             pltpu.SemaphoreType.DMA((32,)),
             pltpu.SemaphoreType.DMA((2,)),
         ],
@@ -475,21 +503,22 @@
         cost_estimate=cost(gu_flops + 2 * d_flops, 40 * MIB),
         name="gradients",
     )(
-        place, gate_idx, up_idx, down_idx, *dy_own, *dy_core, *x_own, *x_core,
+        place, gate_idx, up_idx, down_idx, *dy_pieces, *x_own, *x_core,
         w_d, mult, hidden.reshape(tokens, hid),
     )
 
     def project(left):
         return lax.dot_general(left, w_gu, (((1,), (1,)), ((), ())), preferred_element_type=F32)
 
-    back_away, y_parts = lax.optimization_barrier((back_away, y_parts))
+    back_away, y_z = lax.optimization_barrier((back_away, y_z))
+    y_seq = scatter_direct([y_z[n] for n in range(RING)], "x")
     dx_away = project(back_away).astype(BF)
     dx_recv = swap(dx_away, "c")
     back_kept, dx_away = lax.optimization_barrier((back_kept, dx_away))
     dx_kept, dx_recv = lax.optimization_barrier((project(back_kept).astype(BF), dx_recv))
     dx_chip = add(dx_kept, dx_recv).reshape(chunks)
+    dx_chip, y_seq = lax.optimization_barrier((dx_chip, y_seq))
     dx_parts = lax.all_to_all(dx_chip, ZX, 0, 0, tiled=True)
-    y_seq = jnp.sum(y_parts.astype(F32), axis=0).astype(BF)
     dx_seq = jnp.sum(dx_parts.astype(F32), axis=0).astype(BF)
 
     summed = lax.psum_scatter(terms, "y", scatter_dimension=0, tiled=True)

time: 335 us -> 315 us (0.940)
  waiting for transfers between devices: 164 us -> 143 us
    ppermute x12 -> x9, waiting for transfers between devices: 79.3 us -> 28.7 us  [swap(): return lax.ppermute(value, axis, [(0, 1), (1, 0)])]
    all_to_all x1, waiting for transfers between devices: 0.01 us -> 45.7 us  [per_device(): dx_parts = lax.all_to_all(dx_chip, ZX, 0, 0, tiled=True)]
    all_to_all x1 -> x2, waiting for transfers between devices: 16.3 us -> 0.01 us  [gather_all(): return lax.all_to_all(wide, axis, 0, 0, tiled=True)]
    ppermute x9 -> x12, waiting for transfers between devices: 55.1 us -> 61 us  [shift(): lax.ppermute(value, axis, [(i, (i + step) % RING) for i in range(RING)])]
    reduce_scatter x1, waiting for transfers between devices: 12.5 us -> 7.35 us  [per_device(): summed = lax.psum_scatter(terms, 'y', scatter_dimension=0, tiled=True)]
    broadcast_in_dim x0 -> x2, local copies, waits for them, and re-layouts: none -> 4.61 us  [gather_all(): wide = jnp.broadcast_to(value[None], (RING, *value.shape))]
    all_to_all x1 -> x2, starting transfers between devices: 6.66 us -> 10.5 us  [gather_all(): return lax.all_to_all(wide, axis, 0, 0, tiled=True)]
    reduce_sum x1 -> x0, other arithmetic: 3.72 us -> none  [per_device(): y_seq = jnp.sum(y_parts.astype(F32), axis=0).astype(BF)]
  transfers between devices with their start and end apart: 26 -> 26, of which waited for: 18 -> 12; matrix products, arithmetic and copies ran while one was open for 11% -> 12% of each run, Pallas kernels for 15% -> 22%
where the time goes in v3:
time: 315 us; the launch traced here: 313 us
  waiting for transfers between devices  143 us (45%)
  Pallas kernels  68.1 us (22%)
  starting transfers between devices  40.7 us (13%)
  other arithmetic  18.8 us (6%)
  local copies, waits for them, and re-layouts  14.4 us (5%)
  between operations  14.3 us (5%)
  matrix products  14.2 us (5%)
    ppermute x12, waiting for transfers between devices, shift(): lax.ppermute(value, axis, [(i, (i + step) % RING) for i in range(RING)])  61 us
    all_to_all x1, waiting for transfers between devices, per_device(): dx_parts = lax.all_to_all(dx_chip, ZX, 0, 0, tiled=True)  45.7 us
    pallas_call x1, Pallas kernels, per_device(): pl.pallas_call(part(gradient_kernel, half, kept_here), grid=(steps,), in_...  35.3 us
    pallas_call x2, Pallas kernels, forward(): pl.pallas_call(part(forward_kernel, half, kept_here, first), grid=(2,), i...  32.8 us
    ppermute x9, waiting for transfers between devices, swap(): return lax.ppermute(value, axis, [(0, 1), (1, 0)])  28.7 us
    ppermute x12, starting transfers between devices, shift(): lax.ppermute(value, axis, [(i, (i + step) % RING) for i in range(RING)])  15.3 us
    dot_general x2, matrix products, project(): lax.dot_general(left, w_gu, (((1,), (1,)), ((), ())), preferred_element_t...  14.2 us
    all_to_all x2, starting transfers between devices, gather_all(): return lax.all_to_all(wide, axis, 0, 0, tiled=True)  10.5 us
  transfers between devices with their start and end apart: 26, of which 12 were waited for; matrix products, arithmetic and copies ran while one was open for 12% of the time, Pallas kernels for 22%

profile of v3, /device:TPU:26, one launch (start us, length us, event | category | flops | bytes accessed | tf_op | source)
XLA Modules:
  0.0 313.3 jit_solution(14675304757021172751)
XLA Ops:
  7.2 0.6 collective-permute-start.1
  7.8 2.4 collective-permute-start.2
  10.2 1.8 collective-permute-start.3
  12.0 2.1 broadcast_in_dim.4
  14.1 5.4 %all-to-all-start = ((bf16[4,32,4096]{2,1,0:T(8,128)(2,1)}), bf16[4,32,4096]{2,1,0:T(8,128)(2,1)S(1)}, u32[]{:S(2)}, u32[]{:S(2)}) async-start(bf16[4,32,4096]{2,1,0:T(8,128)(2,1)} %broadcast_in_dim.4), calls=%async_computation | async-start | bytes 2097152 | tf_op jit(solution)/shard_map/all_to_all | solution.py:405
  19.5 0.7 reshape.54
  20.2 0.3 copy.19
  20.6 0.7 reshape.52
  21.3 1.9 reshape.53
  23.2 0.5 pad_maximum_fusion
  23.7 0.0 copy-start.5
  23.7 0.1 dynamic-slice_bitcast_fusion
  23.9 3.6 %collective-permute-start = (bf16[7,6,64,128]{3,2,1,0:T(8,128)(2,1)S(1)}, bf16[7,6,64,128]{3,2,1,0:T(8,128)(2,1)S(1)}, u32[]{:S(2)}, u32[]{:S(2)}) collective-permute-start(bf16[7,6,64,128]{3,2,1,0:T(8,128)(2,1)S(1)} %get-tuple-element.82), channel_id=1, source_target_pairs={{0,16},{16,0},{1,17},{17,1},{2,18},{18,2},{3,19},{19,3},{4,20},{20... | collective-permute-start | bytes 2064392 | tf_op jit(solution)/shard_map/ppermute | solution.py:23
  27.5 0.0 collective-permute-done.1
  27.5 1.2 pad_maximum_fusion.2.refs_3_.refs_6_
  28.7 19.8 %collective-permute-done = bf16[7,6,64,128]{3,2,1,0:T(8,128)(2,1)S(1)} collective-permute-done((bf16[7,6,64,128]{3,2,1,0:T(8,128)(2,1)S(1)}, bf16[7,6,64,128]{3,2,1,0:T(8,128)(2,1)S(1)}, u32[]{:S(2)}, u32[]{:S(2)}) %collective-permute-start) | collective-permute-done | bytes 688160 | tf_op jit(solution)/shard_map/ppermute | solution.py:23
  48.5 1.2 pad_maximum_fusion.1
  49.7 0.0 all-gather.2.cloned.1.call-update
  49.8 2.6 broadcast_in_dim.5
  52.3 5.0 %all-to-all-start.1 = ((bf16[4,4,32,4096]{3,2,1,0:T(8,128)(2,1)}), bf16[4,4,32,4096]{3,2,1,0:T(8,128)(2,1)}, u32[]{:S(2)}, u32[]{:S(2)}) async-start(bf16[4,4,32,4096]{3,2,1,0:T(8,128)(2,1)} %broadcast_in_dim.5), calls=%async_computation.1 | async-start | bytes 8388608 | tf_op jit(solution)/shard_map/all_to_all | solution.py:405
  57.3 0.6 collective-permute-start.9
  57.9 2.7 collective-permute-start.5
  60.6 43.2 %collective-permute-done.9.refs_6_.refs_9_ = bf16[128,4096]{1,0:T(8,128)(2,1)S(1)} collective-permute-done((bf16[128,4096]{1,0:T(8,128)(2,1)S(1)}, bf16[128,4096]{1,0:T(8,128)(2,1)S(1)}, u32[]{:S(2)}, u32[]{:S(2)}) %collective-permute-start.9) | collective-permute-done | bytes 1048608 | tf_op jit(solution)/shard_map/ppermute | solution.py:19
  103.8 0.5 collective-permute-start.6
  104.3 0.1 collective-permute-start.8
  104.4 0.6 pad_add_fusion.refs_0_
  105.0 1.6 collective-permute-done.10.refs_8_.refs_13_
  106.6 3.0 collective-permute-done.6.refs_6_.refs_11_
  109.6 0.2 collective-permute-done.8.refs_7_.refs_12_
  109.8 0.1 collective-permute-start.11
  110.0 18.6 %forward_away.1 = (f32[2,4,4,32,896]{4,3,2,1,0:T(8,128)}, bf16[2,4,4,32,512]{4,3,2,1,0:T(8,128)(2,1)}, bf16[16,32,4096]{2,1,0:T(8,128)(2,1)}, bf16[4096,896]{1,0:T(8,128)(2,1)}, bf16[4096,512]{1,0:T(8,128)(2,1)}) custom-call(s32[3]{0:T(128)} %pad_add_fusion.refs_0_, s32[14,32]{1,0:T(8,128)} %refs_1_.3, s32[14,32]{1,0:T(8,128)} %refs_2_.3, s32[14,32]{1,0:T(8,128)} %refs_3_.3, ...), custom_call_target="tpu_custom_call" | custom-call | flops 738197504 | bytes 3145728 | tf_op jit(solution)/shard_map/forward_away/pallas_call | solution.py:442
  128.6 0.4 collective-permute-start.12
  129.1 14.2 %forward_kept.1 = (f32[2,4,4,32,896]{4,3,2,1,0:T(8,128)}, bf16[2,4,4,32,512]{4,3,2,1,0:T(8,128)(2,1)}, bf16[16,32,4096]{2,1,0:T(8,128)(2,1)}) custom-call(s32[3]{0:T(128)} %pad_add_fusion.refs_0_, bf16[4096,896]{1,0:T(8,128)(2,1)} %get-tuple-element.46.refs_1_, ...), custom_call_target="tpu_custom_call", output_to_operand_aliasing={{0}: (7, {}), {1}: (8, {})} | custom-call | flops 738197504 | bytes 3145728 | tf_op jit(solution)/shard_map/forward_kept/pallas_call | solution.py:442
  143.3 4.1 %add_convert_fusion.2 = (bf16[4,32,4096]{2,1,0:T(8,128)(2,1)}, bf16[4,32,4096]{2,1,0:T(8,128)(2,1)S(1)}, bf16[4,32,4096]{2,1,0:T(8,128)(2,1)}, bf16[4,32,4096]{2,1,0:T(8,128)(2,1)S(1)}) fusion(bf16[16,32,4096]{2,1,0:T(8,128)(2,1)S(1)} %collective-permute-done.12, bf16[16,32,4096]{2,1,0:T(8,128)(2,1)} %get-tuple-element.53), kind=kLoop, calls=%fused_computation.4 | loop fusion | flops 8388608 | bytes 12582912 | tf_op jit(solution)/shard_map/convert_element_type | solution.py:43
  147.4 3.2 %collective-permute-start.14 = (bf16[4,32,4096]{2,1,0:T(8,128)(2,1)}, bf16[4,32,4096]{2,1,0:T(8,128)(2,1)}, u32[]{:S(2)}, u32[]{:S(2)}) collective-permute-start(bf16[4,32,4096]{2,1,0:T(8,128)(2,1)} %get-tuple-element.61), channel_id=1, source_target_pairs={{0,18},{2,0},{16,2},{18,16},{1,19},{3,1},{17,3},{19,17},{4,22},{6,... | collective-permute-start | bytes 3145736 | tf_op jit(solution)/shard_map/ppermute | solution.py:19
  150.6 0.0 collective-permute-start.15
  150.6 35.3 %gradients.1 = (bf16[512,896]{1,0:T(8,128)(2,1)}, bf16[512,896]{1,0:T(8,128)(2,1)}, bf16[336,64,128]{2,1,0:T(8,128)(2,1)}) custom-call(s32[3]{0:T(128)} %pad_add_fusion.refs_0_, s32[14,32]{1,0:T(8,128)} %refs_1_.3, s32[14,32]{1,0:T(8,128)} %refs_2_.3, s32[14,32]{1,0:T(8,128)} %refs_3_.3, bf16[4,4,32,4096]{3,2,1,0:T(8,128)(2,1)} %all-to-all-done.1.refs_4_, ...), custom_call_target="tpu_custom_call" | custom-call | flops 2013265920 | bytes 5242880 | tf_op jit(solution)/shard_map/gradients/pallas_call | solution.py:479
  185.9 0.0 reduce-scatter.2.cloned.1.call-update
  186.0 10.5 %collective-permute-done.13 = bf16[4,32,4096]{2,1,0:T(8,128)(2,1)S(1)} collective-permute-done((bf16[4,32,4096]{2,1,0:T(8,128)(2,1)}, bf16[4,32,4096]{2,1,0:T(8,128)(2,1)S(1)}, u32[]{:S(2)}, u32[]{:S(2)}) %collective-permute-start.13) | collective-permute-done | bytes 1048608 | tf_op jit(solution)/shard_map/ppermute | solution.py:19
  196.5 2.6 add_convert_fusion.1
  199.2 9.4 %convolution_convert_fusion.1 = bf16[512,4096]{1,0:T(8,128)(2,1)} fusion(bf16[512,896]{1,0:T(8,128)(2,1)S(1)} %copy-done.7, bf16[4096,896]{1,0:T(8,128)(2,1)} %get-tuple-element.46.refs_1_), kind=kOutput, calls=%fused_computation.2 | convolution fusion | flops 3760193536 | bytes 12451840 | tf_op jit(solution)/shard_map/dot_general | solution.py:511
  208.5 0.1 slice_bitcast_fusion.2
  208.6 1.4 collective-permute-start.17
  210.0 0.7 collective-permute-start.18
  210.7 1.9 collective-permute-start.19
  212.7 4.8 %convolution_convert_fusion = bf16[512,4096]{1,0:T(8,128)(2,1)S(1)} fusion(bf16[512,896]{1,0:T(8,128)(2,1)S(1)} %copy-done.6, bf16[4096,896]{1,0:T(8,128)(2,1)S(1)} %bitcast.38), kind=kOutput, calls=%fused_computation.1 | convolution fusion | flops 3760193536 | bytes 12451840 | tf_op jit(solution)/shard_map/dot_general | solution.py:511
  217.4 0.3 collective-permute-done.17
  217.8 0.7 collective-permute-done.18
  218.5 6.1 %collective-permute-done.19 = bf16[32,4096]{1,0:T(8,128)(2,1)S(1)} collective-permute-done((bf16[32,4096]{1,0:T(8,128)(2,1)S(1)}, bf16[32,4096]{1,0:T(8,128)(2,1)S(1)}, u32[]{:S(2)}, u32[]{:S(2)}) %collective-permute-start.19) | collective-permute-done | bytes 262176 | tf_op jit(solution)/shard_map/ppermute | solution.py:19
  224.7 0.8 fusion.4
  225.5 3.6 %add_convert_fusion = bf16[512,4096]{1,0:T(8,128)(2,1)} fusion(bf16[512,4096]{1,0:T(8,128)(2,1)S(1)} %collective-permute-done.16, bf16[512,4096]{1,0:T(8,128)(2,1)S(1)} %convolution_convert_fusion), kind=kLoop, calls=%fused_computation | loop fusion | flops 8388608 | bytes 12582912 | tf_op jit(solution)/shard_map/convert_element_type | solution.py:43
  229.1 6.6 %all-to-all-start.2 = ((bf16[16,32,4096]{2,1,0:T(8,128)(2,1)}), bf16[16,32,4096]{2,1,0:T(8,128)(2,1)}, u32[]{:S(2)}, u32[]{:S(2)}) async-start(bf16[16,32,4096]{2,1,0:T(8,128)(2,1)} %bitcast.36), calls=%async_computation.2 | async-start | bytes 8388608 | tf_op jit(solution)/shard_map/all_to_all | solution.py:521
  235.7 7.3 %reduce-scatter.2.cloned.1.call-done = bf16[84,64,128]{2,1,0:T(8,128)(2,1)} async-done(((bf16[336,64,128]{2,1,0:T(8,128)(2,1)}), bf16[84,64,128]{2,1,0:T(8,128)(2,1)}) %reduce-scatter.2.cloned.1.call-update) | async-done | bytes 1376272 | tf_op jit(solution)/shard_map/reduce_scatter | solution.py:524
  243.0 1.4 fusion.5
  244.4 3.5 %collective-permute-start.20 = (bf16[7,6,64,128]{3,2,1,0:T(8,128)(2,1)S(1)}, bf16[7,6,64,128]{3,2,1,0:T(8,128)(2,1)S(1)}, u32[]{:S(2)}, u32[]{:S(2)}) collective-permute-start(bf16[7,6,64,128]{3,2,1,0:T(8,128)(2,1)S(1)} %bitcast.45), channel_id=1, source_target_pairs={{0,16},{16,0},{1,17},{17,1},{2,18},{18,2},{3,19},{19,3},{4,20},{20... | collective-permute-start | bytes 2064392 | tf_op jit(solution)/shard_map/ppermute | solution.py:23
  247.9 45.7 %all-to-all-done.2 = bf16[16,32,4096]{2,1,0:T(8,128)(2,1)} async-done(((bf16[16,32,4096]{2,1,0:T(8,128)(2,1)}), bf16[16,32,4096]{2,1,0:T(8,128)(2,1)}, u32[]{:S(2)}, u32[]{:S(2)}) %all-to-all-start.2) | async-done | bytes 4194336 | tf_op jit(solution)/shard_map/all_to_all | solution.py:521
  293.6 3.7 %reduce_sum.12 = bf16[32,4096]{1,0:T(8,128)(2,1)} reduce(bf16[16,32,4096]{2,1,0:T(8,128)(2,1)} %all-to-all-done.2, bf16[]{:T(256)} %constant.25.clone.1), dimensions={0}, to_apply=%region_0.0 | reduce | flops 1966080 | bytes 4456450 | tf_op jit(solution)/shard_map/reduce_sum | solution.py:522
  297.3 4.1 %collective-permute-done.20 = bf16[7,6,64,128]{3,2,1,0:T(8,128)(2,1)S(1)} collective-permute-done((bf16[7,6,64,128]{3,2,1,0:T(8,128)(2,1)S(1)}, bf16[7,6,64,128]{3,2,1,0:T(8,128)(2,1)S(1)}, u32[]{:S(2)}, u32[]{:S(2)}) %collective-permute-start.20) | collective-permute-done | bytes 688160 | tf_op jit(solution)/shard_map/ppermute | solution.py:23
  301.4 0.1 broadcast_select_fusion
  301.5 0.3 fusion
  301.9 0.4 copy.20
  302.3 1.4 reshape.62
  303.7 1.4 reshape.59
  305.1 1.4 reshape.60
  (41 shorter events, 0.1 us)
Async XLA Ops:
  7.2 12.3 %copy-start.3 = (bf16[14,4,4096]{2,1,0:T(4,128)(2,1)S(1)}, bf16[14,4,4096]{2,1,0:T(4,128)(2,1)}, u32[]{:S(2)}) copy-start(bf16[14,4,4096]{2,1,0:T(4,128)(2,1)} %param.14) | copy-start | bytes 1376260
  7.2 20.3 %collective-permute-start.1 = (bf16[32,4096]{1,0:T(8,128)(2,1)}, bf16[32,4096]{1,0:T(8,128)(2,1)}, u32[]{:S(2)}, u32[]{:S(2)}) collective-permute-start(bf16[32,4096]{1,0:T(8,128)(2,1)} %param.8), channel_id=1, source_target_pairs={{0,12},{4,0},{8,4},{12,8},{1,13},{5,1},{9,5},{13,9},{2,14},{6,2},{... | collective-permute-start | bytes 786440 | tf_op jit(solution)/shard_map/ppermute | solution.py:19
  7.8 19.7 %collective-permute-start.2 = (bf16[32,4096]{1,0:T(8,128)(2,1)}, bf16[32,4096]{1,0:T(8,128)(2,1)}, u32[]{:S(2)}, u32[]{:S(2)}) collective-permute-start(bf16[32,4096]{1,0:T(8,128)(2,1)} %param.8), channel_id=1, source_target_pairs={{0,8},{4,12},{8,0},{12,4},{1,9},{5,13},{9,1},{13,5},{2,10},{6,14},... | collective-permute-start | bytes 786440 | tf_op jit(solution)/shard_map/ppermute | solution.py:19
  10.2 17.3 %collective-permute-start.3 = (bf16[32,4096]{1,0:T(8,128)(2,1)}, bf16[32,4096]{1,0:T(8,128)(2,1)}, u32[]{:S(2)}, u32[]{:S(2)}) collective-permute-start(bf16[32,4096]{1,0:T(8,128)(2,1)} %param.8), channel_id=1, source_target_pairs={{0,4},{4,8},{8,12},{12,0},{1,5},{5,9},{9,13},{13,1},{2,6},{6,10},{... | collective-permute-start | bytes 786440 | tf_op jit(solution)/shard_map/ppermute | solution.py:19
  14.1 6.5 %copy-start.4 = (bf16[14,4,4096]{2,1,0:T(4,128)(2,1)S(1)}, bf16[14,4,4096]{2,1,0:T(4,128)(2,1)}, u32[]{:S(2)}) copy-start(bf16[14,4,4096]{2,1,0:T(4,128)(2,1)} %param.10) | copy-start | bytes 1376260
  14.1 34.4 %all-to-all-start = ((bf16[4,32,4096]{2,1,0:T(8,128)(2,1)}), bf16[4,32,4096]{2,1,0:T(8,128)(2,1)S(1)}, u32[]{:S(2)}, u32[]{:S(2)}) async-start(bf16[4,32,4096]{2,1,0:T(8,128)(2,1)} %broadcast_in_dim.4), calls=%async_computation | async-start | bytes 2097152 | tf_op jit(solution)/shard_map/all_to_all | solution.py:405
  19.5 90.5 %all-gather.2.cloned.1.call-start = ((), (), s32[]{:S(2)}) async-start(), calls=%async_computation.4 | async-start | bytes 6881280 | tf_op jit(solution)/shard_map/all_gather | solution.py:411
  23.7 3.8 %copy-start.5 = (bf16[32,4096]{1,0:T(8,128)(2,1)S(1)}, bf16[32,4096]{1,0:T(8,128)(2,1)}, u32[]{:S(2)}) copy-start(bf16[32,4096]{1,0:T(8,128)(2,1)} %param.8) | copy-start | bytes 786436
  23.9 24.6 %collective-permute-start = (bf16[7,6,64,128]{3,2,1,0:T(8,128)(2,1)S(1)}, bf16[7,6,64,128]{3,2,1,0:T(8,128)(2,1)S(1)}, u32[]{:S(2)}, u32[]{:S(2)}) collective-permute-start(bf16[7,6,64,128]{3,2,1,0:T(8,128)(2,1)S(1)} %get-tuple-element.82), channel_id=1, source_target_pairs={{0,16},{16,0},{1,17},{17,1},{2,18},{18,2},{3,19},{19,3},{4,20},{20... | collective-permute-start | bytes 2064392 | tf_op jit(solution)/shard_map/ppermute | solution.py:23
  28.7 31.9 %copy-start = (bf16[128,4096]{1,0:T(8,128)(2,1)}, bf16[128,4096]{1,0:T(8,128)(2,1)S(1)}, u32[]{:S(2)}) copy-start(bf16[128,4096]{1,0:T(8,128)(2,1)S(1)} %pad_maximum_fusion.2.refs_3_.refs_6_) | copy-start | bytes 3145732
  52.3 57.5 %all-to-all-start.1 = ((bf16[4,4,32,4096]{3,2,1,0:T(8,128)(2,1)}), bf16[4,4,32,4096]{3,2,1,0:T(8,128)(2,1)}, u32[]{:S(2)}, u32[]{:S(2)}) async-start(bf16[4,4,32,4096]{3,2,1,0:T(8,128)(2,1)} %broadcast_in_dim.5), calls=%async_computation.1 | async-start | bytes 8388608 | tf_op jit(solution)/shard_map/all_to_all | solution.py:405
  57.3 185.7 %reduce-scatter.2.cloned.1.call-start = ((), (), s32[]{:S(2)}) async-start(), calls=%async_computation.5 | async-start | bytes 6881280 | tf_op jit(solution)/shard_map/reduce_scatter | solution.py:524
  57.3 46.5 %collective-permute-start.9 = (bf16[128,4096]{1,0:T(8,128)(2,1)S(1)}, bf16[128,4096]{1,0:T(8,128)(2,1)S(1)}, u32[]{:S(2)}, u32[]{:S(2)}) collective-permute-start(bf16[128,4096]{1,0:T(8,128)(2,1)S(1)} %pad_maximum_fusion.2.refs_3_.refs_6_), channel_id=1, source_target_pairs={{0,2},{2,16},{16,18},{18,0},{1,3},{3,17},{17,19},{19,1},{4,6},{6,2... | collective-permute-start | bytes 3145736 | tf_op jit(solution)/shard_map/ppermute | solution.py:19
  57.9 45.9 %collective-permute-start.5 = (bf16[128,4096]{1,0:T(8,128)(2,1)S(1)}, bf16[128,4096]{1,0:T(8,128)(2,1)S(1)}, u32[]{:S(2)}, u32[]{:S(2)}) collective-permute-start(bf16[128,4096]{1,0:T(8,128)(2,1)S(1)} %pad_maximum_fusion.2.refs_3_.refs_6_), channel_id=1, source_target_pairs={{0,18},{2,0},{16,2},{18,16},{1,19},{3,1},{17,3},{19,17},{4,22},{6,... | collective-permute-start | bytes 3145736 | tf_op jit(solution)/shard_map/ppermute | solution.py:19
  60.6 43.8 %collective-permute-start.7 = (bf16[128,4096]{1,0:T(8,128)(2,1)S(1)}, bf16[128,4096]{1,0:T(8,128)(2,1)}, u32[]{:S(2)}, u32[]{:S(2)}) collective-permute-start(bf16[128,4096]{1,0:T(8,128)(2,1)S(1)} %pad_maximum_fusion.2.refs_3_.refs_6_), channel_id=1, source_target_pairs={{0,16},{2,18},{16,0},{18,2},{1,17},{3,19},{17,1},{19,3},{4,20},{6,... | collective-permute-start | bytes 3145736 | tf_op jit(solution)/shard_map/ppermute | solution.py:19
  60.6 44.5 %collective-permute-start.4 = (bf16[128,4096]{1,0:T(8,128)(2,1)S(1)}, bf16[128,4096]{1,0:T(8,128)(2,1)}, u32[]{:S(2)}, u32[]{:S(2)}) collective-permute-start(bf16[128,4096]{1,0:T(8,128)(2,1)S(1)} %pad_maximum_fusion.2.refs_3_.refs_6_), channel_id=1, source_target_pairs={{0,1},{1,0},{2,3},{3,2},{4,5},{5,4},{6,7},{7,6},{8,9},{9,8},{10,11... | collective-permute-start | bytes 3145736 | tf_op jit(solution)/shard_map/ppermute | solution.py:23
  103.8 24.8 %copy-start.1 = (bf16[128,4096]{1,0:T(8,128)(2,1)}, bf16[128,4096]{1,0:T(8,128)(2,1)S(1)}, u32[]{:S(2)}) copy-start(bf16[128,4096]{1,0:T(8,128)(2,1)S(1)} %collective-permute-done.9.refs_6_.refs_9_) | copy-start | bytes 3145732
  103.8 2.8 collective-permute-start.10
  103.8 24.8 %copy-start.2 = (bf16[128,4096]{1,0:T(8,128)(2,1)}, bf16[128,4096]{1,0:T(8,128)(2,1)S(1)}, u32[]{:S(2)}) copy-start(bf16[128,4096]{1,0:T(8,128)(2,1)S(1)} %collective-permute-done.5.refs_4_.refs_7_) | copy-start | bytes 3145732
  103.8 5.8 %collective-permute-start.6 = (bf16[128,4096]{1,0:T(8,128)(2,1)S(1)}, bf16[128,4096]{1,0:T(8,128)(2,1)}, u32[]{:S(2)}, u32[]{:S(2)}) collective-permute-start(bf16[128,4096]{1,0:T(8,128)(2,1)S(1)} %collective-permute-done.5.refs_4_.refs_7_), channel_id=1, source_target_pairs={{0,1},{1,0},{2,3},{3,2},{4,5},{5,4},{6,7},{7,6},{8,9},{9,8},{10,11... | collective-permute-start | bytes 3145736 | tf_op jit(solution)/shard_map/ppermute | solution.py:23
  104.3 5.5 %collective-permute-start.8 = (bf16[128,4096]{1,0:T(8,128)(2,1)}, bf16[128,4096]{1,0:T(8,128)(2,1)}, u32[]{:S(2)}, u32[]{:S(2)}) collective-permute-start(bf16[128,4096]{1,0:T(8,128)(2,1)} %collective-permute-done.7.refs_5_.refs_8_), channel_id=1, source_target_pairs={{0,1},{1,0},{2,3},{3,2},{4,5},{5,4},{6,7},{7,6},{8,9},{9,8},{10,11... | collective-permute-start | bytes 3145736 | tf_op jit(solution)/shard_map/ppermute | solution.py:23
  109.8 33.5 %collective-permute-start.11 = (bf16[4,4,32,4096]{3,2,1,0:T(8,128)(2,1)}, bf16[4,4,32,4096]{3,2,1,0:T(8,128)(2,1)}, u32[]{:S(2)}, u32[]{:S(2)}) collective-permute-start(bf16[4,4,32,4096]{3,2,1,0:T(8,128)(2,1)} %all-to-all-done.1.refs_4_), channel_id=1, source_target_pairs={{0,1},{1,0},{2,3},{3,2},{4,5},{5,4},{6,7},{7,6},{8,9},{9,8},{10,11... | collective-permute-start | bytes 12582920 | tf_op jit(solution)/shard_map/ppermute | solution.py:23
  128.6 14.7 %collective-permute-start.12 = (bf16[16,32,4096]{2,1,0:T(8,128)(2,1)}, bf16[16,32,4096]{2,1,0:T(8,128)(2,1)S(1)}, u32[]{:S(2)}, u32[]{:S(2)}) collective-permute-start(bf16[16,32,4096]{2,1,0:T(8,128)(2,1)} %get-tuple-element.54), channel_id=1, source_target_pairs={{0,1},{1,0},{2,3},{3,2},{4,5},{5,4},{6,7},{7,6},{8,9},{9,8},{10,11... | collective-permute-start | bytes 12582920 | tf_op jit(solution)/shard_map/ppermute | solution.py:23
  147.4 49.1 %collective-permute-start.13 = (bf16[4,32,4096]{2,1,0:T(8,128)(2,1)}, bf16[4,32,4096]{2,1,0:T(8,128)(2,1)S(1)}, u32[]{:S(2)}, u32[]{:S(2)}) collective-permute-start(bf16[4,32,4096]{2,1,0:T(8,128)(2,1)} %get-tuple-element.60), channel_id=1, source_target_pairs={{0,2},{2,16},{16,18},{18,0},{1,3},{3,17},{17,19},{19,1},{4,6},{6,2... | collective-permute-start | bytes 3145736 | tf_op jit(solution)/shard_map/ppermute | solution.py:19
  147.4 49.1 %collective-permute-start.14 = (bf16[4,32,4096]{2,1,0:T(8,128)(2,1)}, bf16[4,32,4096]{2,1,0:T(8,128)(2,1)}, u32[]{:S(2)}, u32[]{:S(2)}) collective-permute-start(bf16[4,32,4096]{2,1,0:T(8,128)(2,1)} %get-tuple-element.61), channel_id=1, source_target_pairs={{0,18},{2,0},{16,2},{18,16},{1,19},{3,1},{17,3},{19,17},{4,22},{6,... | collective-permute-start | bytes 3145736 | tf_op jit(solution)/shard_map/ppermute | solution.py:19
  150.6 45.9 %collective-permute-start.15 = (bf16[4,32,4096]{2,1,0:T(8,128)(2,1)S(1)}, bf16[4,32,4096]{2,1,0:T(8,128)(2,1)}, u32[]{:S(2)}, u32[]{:S(2)}) collective-permute-start(bf16[4,32,4096]{2,1,0:T(8,128)(2,1)S(1)} %get-tuple-element.62), channel_id=1, source_target_pairs={{0,16},{2,18},{16,0},{18,2},{1,17},{3,19},{17,1},{19,3},{4,20},{6,... | collective-permute-start | bytes 3145736 | tf_op jit(solution)/shard_map/ppermute | solution.py:19
  186.0 13.2 %copy-start.7 = (bf16[512,896]{1,0:T(8,128)(2,1)S(1)}, bf16[512,896]{1,0:T(8,128)(2,1)}, u32[]{:S(2)}) copy-start(bf16[512,896]{1,0:T(8,128)(2,1)} %get-tuple-element.63) | copy-start | bytes 2752516
  196.5 16.1 %slice-start = ((s8[7340032]{0:T(1024)(128)(4,1)}), s8[4194304]{0:T(1024)(128)(4,1)S(1)}, s32[]{:S(2)}) async-start(s8[7340032]{0:T(1024)(128)(4,1)} %bitcast.37), calls=%async_computation.6 | async-start | bytes 8388608
  199.1 13.5 %slice-start.1 = ((s8[7340032]{0:T(1024)(128)(4,1)}), s8[3145728]{0:T(1024)(128)(4,1)S(1)}, s32[]{:S(2)}) async-start(s8[7340032]{0:T(1024)(128)(4,1)} %bitcast.37), calls=%async_computation.7 | async-start | bytes 6291456
  199.2 13.5 %copy-start.6 = (bf16[512,896]{1,0:T(8,128)(2,1)S(1)}, bf16[512,896]{1,0:T(8,128)(2,1)}, u32[]{:S(2)}) copy-start(bf16[512,896]{1,0:T(8,128)(2,1)} %get-tuple-element.64) | copy-start | bytes 2752516
  208.5 17.0 %collective-permute-start.16 = (bf16[512,4096]{1,0:T(8,128)(2,1)}, bf16[512,4096]{1,0:T(8,128)(2,1)S(1)}, u32[]{:S(2)}, u32[]{:S(2)}) collective-permute-start(bf16[512,4096]{1,0:T(8,128)(2,1)} %convolution_convert_fusion.1), channel_id=1, source_target_pairs={{0,1},{1,0},{2,3},{3,2},{4,5},{5,4},{6,7},{7,6},{8,9},{9,8},{10,11... | collective-permute-start | bytes 12582920 | tf_op jit(solution)/shard_map/ppermute | solution.py:23
  208.6 9.2 %collective-permute-start.17 = (bf16[32,4096]{1,0:T(8,128)(2,1)S(1)}, bf16[32,4096]{1,0:T(8,128)(2,1)S(1)}, u32[]{:S(2)}, u32[]{:S(2)}) collective-permute-start(bf16[32,4096]{1,0:T(8,128)(2,1)S(1)} %get-tuple-element.83), channel_id=1, source_target_pairs={{0,4},{4,8},{8,12},{12,0},{1,5},{5,9},{9,13},{13,1},{2,6},{6,10},{... | collective-permute-start | bytes 786440 | tf_op jit(solution)/shard_map/ppermute | solution.py:19
  210.0 8.5 %collective-permute-start.18 = (bf16[32,4096]{1,0:T(8,128)(2,1)S(1)}, bf16[32,4096]{1,0:T(8,128)(2,1)S(1)}, u32[]{:S(2)}, u32[]{:S(2)}) collective-permute-start(bf16[32,4096]{1,0:T(8,128)(2,1)S(1)} %get-tuple-element.85), channel_id=1, source_target_pairs={{0,12},{4,0},{8,4},{12,8},{1,13},{5,1},{9,5},{13,9},{2,14},{6,2},{... | collective-permute-start | bytes 786440 | tf_op jit(solution)/shard_map/ppermute | solution.py:19
  210.7 14.0 %collective-permute-start.19 = (bf16[32,4096]{1,0:T(8,128)(2,1)S(1)}, bf16[32,4096]{1,0:T(8,128)(2,1)S(1)}, u32[]{:S(2)}, u32[]{:S(2)}) collective-permute-start(bf16[32,4096]{1,0:T(8,128)(2,1)S(1)} %get-tuple-element.84), channel_id=1, source_target_pairs={{0,8},{4,12},{8,0},{12,4},{1,9},{5,13},{9,1},{13,5},{2,10},{6,14},... | collective-permute-start | bytes 786440 | tf_op jit(solution)/shard_map/ppermute | solution.py:19
  229.1 64.5 %all-to-all-start.2 = ((bf16[16,32,4096]{2,1,0:T(8,128)(2,1)}), bf16[16,32,4096]{2,1,0:T(8,128)(2,1)}, u32[]{:S(2)}, u32[]{:S(2)}) async-start(bf16[16,32,4096]{2,1,0:T(8,128)(2,1)} %bitcast.36), calls=%async_computation.2 | async-start | bytes 8388608 | tf_op jit(solution)/shard_map/all_to_all | solution.py:521
  244.4 57.0 %collective-permute-start.20 = (bf16[7,6,64,128]{3,2,1,0:T(8,128)(2,1)S(1)}, bf16[7,6,64,128]{3,2,1,0:T(8,128)(2,1)S(1)}, u32[]{:S(2)}, u32[]{:S(2)}) collective-permute-start(bf16[7,6,64,128]{3,2,1,0:T(8,128)(2,1)S(1)} %bitcast.45), channel_id=1, source_target_pairs={{0,16},{16,0},{1,17},{17,1},{2,18},{18,2},{3,19},{19,3},{4,20},{20... | collective-permute-start | bytes 2064392 | tf_op jit(solution)/shard_map/ppermute | solution.py:23
Sparse Core Ops, SparseCore 0:
  49.9 55.9 all-gather.1
  186.1 56.8 reduce-scatter.1

commit v4 on v3

--- a/solution.py
+++ b/solution.py
@@ -65,33 +65,34 @@
     ]
 
 
-def owner_row(place, core, z, x):
-    return core * RING * RING + (place[1] + z) % RING * RING + (place[2] + x) % RING
+def z_copies(piece, buf, sems, place):
+    rows = piece.shape[1]
+    return [
+        pltpu.make_async_copy(
+            piece.at[(place[1] + n) % RING], buf.at[pl.ds(n * rows, rows)], sems.at[n]
+        )
+        for n in range(RING)
+    ]
+
+
+def owner_row(core, z, x):
+    return core * RING * RING + z % RING * RING + x % RING
 
 
 def chunk_copies(pieces, buf, sems, place):
-    per = pieces[0].shape[0] // RING
+    per = pieces[0].shape[1] // RING
     copies = []
-    for n, piece in enumerate(pieces):
-        for x in range(RING):
-            at = owner_row(place, n // RING, n % RING, x) * per
-            copies.append(
-                pltpu.make_async_copy(
-                    piece.at[pl.ds(x * per, per)],
-                    buf.at[pl.ds(pl.multiple_of(at, per), per)],
-                    sems.at[n * RING + x],
+    for core, piece in enumerate(pieces):
+        for z in range(RING):
+            for x in range(RING):
+                at = owner_row(core, z, place[2] + x) * per
+                copies.append(
+                    pltpu.make_async_copy(
+                        piece.at[z, pl.ds(x * per, per)],
+                        buf.at[pl.ds(pl.multiple_of(at, per), per)],
+                        sems.at[len(copies)],
+                    )
                 )
-            )
-    return copies
-
-
-def ring_copies(pieces, buf, sems, place):
-    per = pieces[0].shape[2]
-    copies = []
-    for n in range(2 * RING * RING):
-        core, x, z = n // (RING * RING), n // RING % RING, n % RING
-        source = pieces[core].at[(place[2] + x) % RING, (place[1] + z) % RING]
-        copies.append(pltpu.make_async_copy(source, buf.at[pl.ds(n * per, per)], sems.at[n]))
     return copies
 
 
@@ -212,16 +213,16 @@
 def forward_kernel(half_panels, kept_here, first, place, *refs):
     if first:
         gate_idx, up_idx, down_idx, tiles = refs[:4]
-        pieces, refs = refs[4:8], refs[8:]
+        piece, refs = refs[4], refs[5:]
         m_ref, h2_ref, y_ref, w_other, wd_other = refs[:5]
     else:
         w_other, wd_other = refs[:2]
-        pieces, refs = refs[2:6], refs[8:]
+        piece, refs = refs[2], refs[5:]
         m_ref, h2_ref, y_ref = refs[:3]
     w_ref, wd_ref, h_ref, buf, sems, w_sems = refs[-6:]
     i = pl.program_id(0)
     rows = buf.shape[0] // 2
-    copies = row_copies(pieces, buf, sems)
+    copies = z_copies(piece, buf, sems, place)
     pairs = ((w_ref, w_other), (wd_ref, wd_other))
     if not first:
         pairs = [(b, a) for a, b in pairs]
@@ -262,18 +263,18 @@
 
 
 def gradient_kernel(half_panels, kept_here, place, gate_idx, up_idx, down_idx, *refs):
-    dy_pieces, x_pieces = refs[:2], refs[2:10]
-    wd_ref, m_ref, h_ref, back_kept, back_away, out_ref, dy_buf, x_buf, g_ref, acc, dy_sems, x_sems, g_sems = refs[10:]
+    dy_pieces, x_pieces, refs = refs[:8], refs[8:10], refs[10:]
+    wd_ref, m_ref, h_ref, w_gu, back_kept, dx_away, out_ref = refs[:7]
+    dy_buf, x_buf, g_ref, acc, w_ref, dy_sems, x_sems, g_sems = refs[7:]
     i = pl.program_id(0)
     where = Tiles(half_panels, kept_here, place[0])
     rows = dy_buf.shape[0] // 4
-    dy_copies = ring_copies(dy_pieces, dy_buf, dy_sems, place)
+    dy_copies = row_copies(dy_pieces, dy_buf, dy_sems)
+    w_copy = pltpu.make_async_copy(w_gu, w_ref, g_sems.at[2])
     x_copies = chunk_copies(x_pieces, x_buf, x_sems, place)
     half_rows = back_kept.shape[0]
-    g_copies = [
-        pltpu.make_async_copy(g_ref.at[pl.ds(n * half_rows, half_rows)], out, g_sems.at[n])
-        for n, out in enumerate((back_kept, back_away))
-    ]
+    g_copy = pltpu.make_async_copy(g_ref.at[pl.ds(0, half_rows)], back_kept, g_sems.at[0])
+    dx_copy = pltpu.make_async_copy(dy_buf.at[pl.ds(0, half_rows)], dx_away, g_sems.at[1])
     hid = h_ref.shape[1]
     cols = dy_buf.shape[1] // 4
     mask = left_half((rows, 2 * BLK))
@@ -285,13 +286,9 @@
             copy.start()
         for copy in x_copies:
             copy.start()
-
-    for t in range(4):
-
-        @pl.when(i == t)
-        def _(t=t):
-            for copy in dy_copies[8 * t : 8 * t + 8]:
-                copy.wait()
+        w_copy.start()
+
+    tile_wait(dy_copies, i)
 
     @pl.when(i < 4)
     def _():
@@ -309,7 +306,7 @@
             for a in range(RING // 2):
                 for b in range(RING):
                     at = (a * RING + b) * per
-                    chunk = owner_row(place, i // 2, b, (i % 2) * (RING // 2) + a)
+                    chunk = owner_row(i // 2, place[1] + b, place[2] + (i % 2) * (RING // 2) + a)
                     rows_at = pl.ds(pl.multiple_of(chunk * per, per), per)
                     g_ref[rows_at, lanes] = (
                         spread[at : at + per] * m_ref[0, b, a, :, lanes]
@@ -326,14 +323,10 @@
 
     @pl.when(i == 4)
     def _():
-        for copy in g_copies:
-            copy.start()
+        g_copy.start()
 
     @pl.when(i == 7)
     def _():
-        for copy in x_copies:
-            copy.wait()
-
         def take(step, carry):
             group, m = step // where.pairs, step % where.pairs
             j = where.kept(group, 2 * m)
@@ -350,9 +343,28 @@
 
         lax.fori_loop(0, 2 * RING * where.pairs, take, 0)
 
-    @pl.when(i >= 8)
+    @pl.when(i == 8)
+    def _():
+        w_copy.wait()
+
+    @pl.when((i >= 8) & (i < 12))
     def _():
         at = pl.multiple_of((i - 8) * cols, cols)
+        part = lax.dot_general(
+            g_ref[half_rows:, :], w_ref[pl.ds(at, cols), :], (((1,), (1,)), ((), ())),
+            preferred_element_type=F32,
+        )
+        dy_buf[:half_rows, pl.ds(at, cols)] = part.astype(BF)
+
+    @pl.when(i == 12)
+    def _():
+        dx_copy.start()
+        for copy in x_copies:
+            copy.wait()
+
+    @pl.when(i >= 12)
+    def _():
+        at = pl.multiple_of((i - 12) * cols, cols)
         part = lax.dot_general(
             x_buf[:, pl.ds(at, cols)], g_ref[...], (((0,), (0,)), ((), ())),
             preferred_element_type=F32,
@@ -372,8 +384,8 @@
             return carry
 
         lax.fori_loop(0, 2 * RING * kept_here, take, 0)
-        for copy in g_copies:
-            copy.wait()
+        g_copy.wait()
+        dx_copy.wait()
 
 
 def cost(flops, nbytes):
@@ -391,29 +403,35 @@
     place = jnp.stack([zh, z_place, lax.axis_index("x")]).astype(jnp.int32)
     shape = jax.ShapeDtypeStruct
 
-    gate_blk = gate_vals.reshape(panels, kept_here, edge, edge)
-    up_blk = up_vals.reshape(panels, kept_here, edge, edge)
-    pair_gu = jnp.concatenate([gate_blk, up_blk], axis=3)
-    down_blk = down_vals.reshape(panels, pairs, 2, edge, edge)
-    pair_d = jnp.transpose(down_blk, (0, 1, 4, 2, 3)).reshape(panels, pairs, edge, 2 * edge)
-    all_pairs = jnp.concatenate([pair_gu, pair_d], axis=1)
-    own = lax.dynamic_slice_in_dim(all_pairs, zh * half, half, 0)
-    other = swap(lax.dynamic_slice_in_dim(all_pairs, (1 - zh) * half, half, 0), "zh")
-
-    def gather_all(value, axis):
-        wide = jnp.broadcast_to(value[None], (RING, *value.shape))
-        return lax.all_to_all(wide, axis, 0, 0, tiled=True)
-
-    dy_row = gather_all(dy_seq, Z)
+    def block_pairs(values):
+        gate, up, down = (
+            values[:, n * kept_here : (n + 1) * kept_here].reshape(half, kept_here, edge, edge)
+            for n in range(3)
+        )
+        down = down.reshape(half, pairs, 2, edge, edge)
+        down = jnp.transpose(down, (0, 1, 4, 2, 3)).reshape(half, pairs, edge, 2 * edge)
+        return jnp.concatenate([jnp.concatenate([gate, up], axis=3), down], axis=1)
+
+    def panel_half(which):
+        return jnp.concatenate(
+            [lax.dynamic_slice_in_dim(v, which * half, half, 0) for v in (gate_vals, up_vals, down_vals)],
+            axis=1,
+        )
+
+    other = swap(panel_half(1 - zh), "zh")
+    own = block_pairs(panel_half(zh))
+
     x_row = jnp.concatenate(gather_direct(x_seq, "x"), axis=0)
-    other, x_row, dy_row = lax.optimization_barrier((other, x_row, dy_row))
-    both = jnp.stack([own, other]).reshape(-1, edge, 2 * edge)
+    other, x_row, own = lax.optimization_barrier((other, x_row, own))
+    both = jnp.stack([own, block_pairs(other)]).reshape(-1, edge, 2 * edge)
     tiles = lax.all_gather(both, "y", axis=0, tiled=True)
-    dy_own = gather_all(dy_row, "x")
-    x_own = gather_direct(x_row, Z)
-    x_core = [swap(v, "c") for v in x_own]
-    x_core, dy_own = lax.optimization_barrier((x_core, dy_own))
-    dy_core = swap(dy_own, "c")
+    dy_seq, other = lax.optimization_barrier((dy_seq, other))
+    wide = jnp.broadcast_to(x_row[None], (RING, *x_row.shape))
+    x_own = lax.all_to_all(wide, Z, 0, 0, tiled=True)
+    dy_row = jnp.concatenate(gather_direct(dy_seq, Z), axis=0)
+    dy_own = gather_direct(dy_row, "x")
+    x_own, dy_own = lax.optimization_barrier((x_own, dy_own))
+    x_core = swap(x_own, "c")
 
     tokens = 2 * RING * RING * per
     rows = tokens // 4
@@ -437,7 +455,7 @@
         return body
 
     def forward(core, first, inputs, name):
-        specs = [smem] * 4 + [full(*tiles.shape)] + [hbm] * 4 if first else [smem] + [hbm] * 8
+        specs = [smem] * 4 + [full(*tiles.shape), hbm] if first else [smem] + [hbm] * 5
         extra_out = [shape((width, two), BF), shape((width, hid), BF)] if first else []
         return pl.pallas_call(
             part(forward_kernel, half, kept_here, first),
@@ -457,26 +475,26 @@
                 pltpu.SemaphoreType.DMA((4,)),
                 pltpu.SemaphoreType.DMA((2,)),
             ],
-            input_output_aliases={} if first else {7: 0, 8: 1},
+            input_output_aliases={} if first else {4: 0, 5: 1},
             compiler_params=kernel_params(56),
             cost_estimate=cost((gu_flops + d_flops) // 2, 24 * MIB),
             name=name,
         )(place, *inputs)
 
     mult, hidden, y_away, w_gu, w_d = forward(
-        1, True, (gate_idx, up_idx, down_idx, tiles, *x_core), "forward_away"
+        1, True, (gate_idx, up_idx, down_idx, tiles, x_core), "forward_away"
     )
+    dy_core = [swap(v, "c") for v in dy_own]
     y_recv = swap(y_away, "c")
-    mult, hidden, y_kept = forward(0, False, (w_gu, w_d, *x_own, mult, hidden), "forward_kept")
+    mult, hidden, y_kept = forward(0, False, (w_gu, w_d, x_own, mult, hidden), "forward_kept")
     y_kept, dy_core = lax.optimization_barrier((y_kept, dy_core))
-    dy_pieces = [v.reshape(RING, RING, per, width) for v in (dy_own, dy_core)]
     y_sum = [add(y_kept[n * RING : n * RING + RING], y_recv[n * RING : n * RING + RING]) for n in range(RING)]
     mult, y_sum = lax.optimization_barrier((mult, y_sum))
     y_z = scatter_direct(y_sum, Z)
 
-    steps = 12
+    steps = 16
     x_tile = lambda i: jnp.minimum(i, 3)
-    back_kept, back_away, terms = pl.pallas_call(
+    back_kept, dx_away, terms = pl.pallas_call(
         part(gradient_kernel, half, kept_here),
         grid=(steps,),
         in_specs=[smem] * 4
@@ -487,40 +505,42 @@
                 (1, RING, pair, per, two), lambda i: (x_tile(i) // 2, 0, x_tile(i) % 2, 0, 0)
             ),
             full(tokens, hid),
+            hbm,
         ],
         out_specs=[hbm, hbm, out_full(*tiles.shape)],
-        out_shape=[shape((tokens // 2, two), BF)] * 2 + [shape(tiles.shape, BF)],
+        out_shape=[
+            shape((tokens // 2, two), BF),
+            shape((tokens // 2, width), BF),
+            shape(tiles.shape, BF),
+        ],
         scratch_shapes=[
             pltpu.VMEM((tokens, width), BF),
             pltpu.VMEM((tokens, width), BF),
             pltpu.VMEM((tokens, two), BF),
             pltpu.VMEM((width, two), BF),
+            pltpu.VMEM((width, two), BF),
+            pltpu.SemaphoreType.DMA((8,)),
             pltpu.SemaphoreType.DMA((32,)),
-            pltpu.SemaphoreType.DMA((32,)),
-            pltpu.SemaphoreType.DMA((2,)),
+            pltpu.SemaphoreType.DMA((3,)),
         ],
         compiler_params=kernel_params(60),
         cost_estimate=cost(gu_flops + 2 * d_flops, 40 * MIB),
         name="gradients",
     )(
-        place, gate_idx, up_idx, down_idx, *dy_pieces, *x_own, *x_core,
-        w_d, mult, hidden.reshape(tokens, hid),
+        place, gate_idx, up_idx, down_idx, *dy_own, *dy_core, x_own, x_core,
+        w_d, mult, hidden.reshape(tokens, hid), w_gu,
     )
 
     def project(left):
         return lax.dot_general(left, w_gu, (((1,), (1,)), ((), ())), preferred_element_type=F32)
 
-    back_away, y_z = lax.optimization_barrier((back_away, y_z))
-    y_seq = scatter_direct([y_z[n] for n in range(RING)], "x")
-    dx_away = project(back_away).astype(BF)
+    back_kept, dx_away, terms, y_z = lax.optimization_barrier((back_kept, dx_away, terms, y_z))
     dx_recv = swap(dx_away, "c")
-    back_kept, dx_away = lax.optimization_barrier((back_kept, dx_away))
     dx_kept, dx_recv = lax.optimization_barrier((project(back_kept).astype(BF), dx_recv))
     dx_chip = add(dx_kept, dx_recv).reshape(chunks)
-    dx_chip, y_seq = lax.optimization_barrier((dx_chip, y_seq))
+    y_z, dx_chip = lax.optimization_barrier((y_z, dx_chip))
     dx_parts = lax.all_to_all(dx_chip, ZX, 0, 0, tiled=True)
-    dx_seq = jnp.sum(dx_parts.astype(F32), axis=0).astype(BF)
-
+    y_seq = scatter_direct([y_z[n] for n in range(RING)], "x")
     summed = lax.psum_scatter(terms, "y", scatter_dimension=0, tiled=True)
     summed = summed.reshape(2, half, per_panel, edge, 2 * edge)
     other = swap(summed[1], "zh")
@@ -532,6 +552,10 @@
     d_up_vals = gu_grads[..., edge:].reshape(panels, kept_here, square)
     d_grads = grads[:, kept_here:].reshape(panels, pairs, edge, 2, edge)
     d_down_vals = jnp.transpose(d_grads, (0, 1, 3, 4, 2)).reshape(panels, kept_here, square)
+    dx_parts, d_gate_vals, d_up_vals, d_down_vals, y_seq = lax.optimization_barrier(
+        (dx_parts, d_gate_vals, d_up_vals, d_down_vals, y_seq)
+    )
+    dx_seq = jnp.sum(dx_parts.astype(F32), axis=0).astype(BF)
     return (y_seq, dx_seq, d_gate_vals, d_up_vals, d_down_vals)
 
 

time: 315 us -> 363 us (1.15)
  waiting for transfers between devices: 143 us -> 184 us
  Pallas kernels: 68.1 us -> 75.7 us
  matrix products: 14.2 us -> 7.84 us
    ppermute x12 -> x15, waiting for transfers between devices: 61 us -> 129 us  [shift(): lax.ppermute(value, axis, [(i, (i + step) % RING) for i in range(RING)])]
    all_to_all x1, waiting for transfers between devices: 45.7 us -> 0.01 us  [per_device(): dx_parts = lax.all_to_all(dx_chip, ZX, 0, 0, tiled=True)]
    reduce_scatter x1, waiting for transfers between devices: 7.35 us -> 32.8 us  [per_device(): summed = lax.psum_scatter(terms, 'y', scatter_dimension=0, tiled=True)]
    pallas_call x1, Pallas kernels: 35.3 us -> 42.9 us  [per_device(): pl.pallas_call(part(gradient_kernel, half, kept_here), grid=(steps,), in_...]
    ppermute x9, waiting for transfers between devices: 28.7 us -> 21.7 us  [swap(): return lax.ppermute(value, axis, [(0, 1), (1, 0)])]
    dot_general x2 -> x1, matrix products: 14.2 us -> 7.84 us  [project(): lax.dot_general(left, w_gu, (((1,), (1,)), ((), ())), preferred_element_t...]
    ppermute x12 -> x15, starting transfers between devices: 15.3 us -> 21.2 us  [shift(): lax.ppermute(value, axis, [(i, (i + step) % RING) for i in range(RING)])]
    all_to_all x2 -> x1, starting transfers between devices: 10.5 us -> 4.97 us  [per_device(): x_own = lax.all_to_all(wide, Z, 0, 0, tiled=True)]
  transfers between devices with their start and end apart: 26 -> 28, of which waited for: 12 -> 14; matrix products, arithmetic and copies ran while one was open for 12% -> 8% of each run, Pallas kernels for 22% -> 16%
where the time goes in v4:
time: 363 us; the launch traced here: 360 us
  waiting for transfers between devices  184 us (51%)
  Pallas kernels  75.7 us (21%)
  starting transfers between devices  42.3 us (12%)
  other arithmetic  18.7 us (5%)
  local copies, waits for them, and re-layouts  17.1 us (5%)
  between operations  14.4 us (4%)
  matrix products  7.84 us (2%)
    ppermute x15, waiting for transfers between devices, shift(): lax.ppermute(value, axis, [(i, (i + step) % RING) for i in range(RING)])  129 us
    pallas_call x1, Pallas kernels, per_device(): pl.pallas_call(part(gradient_kernel, half, kept_here), grid=(steps,), in_...  42.9 us
    pallas_call x2, Pallas kernels, forward(): pl.pallas_call(part(forward_kernel, half, kept_here, first), grid=(2,), i...  32.8 us
    reduce_scatter x1, waiting for transfers between devices, per_device(): summed = lax.psum_scatter(terms, 'y', scatter_dimension=0, tiled=True)  32.8 us
    ppermute x9, waiting for transfers between devices, swap(): return lax.ppermute(value, axis, [(0, 1), (1, 0)])  21.7 us
    ppermute x15, starting transfers between devices, shift(): lax.ppermute(value, axis, [(i, (i + step) % RING) for i in range(RING)])  21.2 us
    ppermute x9, starting transfers between devices, swap(): return lax.ppermute(value, axis, [(0, 1), (1, 0)])  8.76 us
    dot_general x1, matrix products, project(): lax.dot_general(left, w_gu, (((1,), (1,)), ((), ())), preferred_element_t...  7.84 us
  transfers between devices with their start and end apart: 28, of which 14 were waited for; matrix products, arithmetic and copies ran while one was open for 8% of the time, Pallas kernels for 16%

profile of v4, /device:TPU:26, one launch (start us, length us, event | category | flops | bytes accessed | tf_op | source)
XLA Modules:
  0.0 359.7 jit_solution(969217151752516230)
XLA Ops:
  7.2 0.6 collective-permute-start.1
  7.8 2.4 collective-permute-start.2
  10.2 1.8 collective-permute-start.3
  12.0 1.2 constant_dynamic-slice_fusion.2
  13.3 1.7 constant_dynamic-slice_fusion
  15.0 0.4 pad_maximum_fusion.2
  15.4 4.0 %collective-permute-start = (bf16[7,12,4096]{2,1,0:T(8,128)(2,1)S(1)}, bf16[7,12,4096]{2,1,0:T(8,128)(2,1)}, u32[]{:S(2)}, u32[]{:S(2)}) collective-permute-start(bf16[7,12,4096]{2,1,0:T(8,128)(2,1)S(1)} %pad_maximum_fusion.2), channel_id=1, source_target_pairs={{0,16},{16,0},{1,17},{17,1},{2,18},{18,2},{3,19},{19,3},{4,20},{20... | collective-permute-start | bytes 2064392 | tf_op jit(solution)/shard_map/ppermute | solution.py:23
  19.3 0.4 reshape_reshape.6
  20.0 0.4 reshape.58
  20.4 0.4 reshape.57
  21.1 1.1 collective-permute-done.2
  22.2 0.9 collective-permute-done.3
  23.1 1.1 pad_maximum_fusion.1
  24.2 14.7 %collective-permute-done = bf16[7,12,4096]{2,1,0:T(8,128)(2,1)} collective-permute-done((bf16[7,12,4096]{2,1,0:T(8,128)(2,1)S(1)}, bf16[7,12,4096]{2,1,0:T(8,128)(2,1)}, u32[]{:S(2)}, u32[]{:S(2)}) %collective-permute-start) | collective-permute-done | bytes 688160 | tf_op jit(solution)/shard_map/ppermute | solution.py:23
  38.9 1.6 fusion.6
  40.5 0.4 reshape_reshape.7
  41.2 0.4 reshape.60
  41.6 0.4 reshape.61
  42.3 1.2 pad_maximum_fusion
  43.5 2.6 broadcast_in_dim.2
  46.1 5.0 %all-to-all-start = ((bf16[4,128,4096]{2,1,0:T(8,128)(2,1)}), bf16[4,128,4096]{2,1,0:T(8,128)(2,1)}, u32[]{:S(2)}, u32[]{:S(2)}) async-start(bf16[4,128,4096]{2,1,0:T(8,128)(2,1)} %broadcast_in_dim.2), calls=%async_computation | async-start | bytes 8388608 | tf_op jit(solution)/shard_map/all_to_all | solution.py:430
  51.1 3.5 collective-permute-start.4
  54.6 0.5 collective-permute-start.5
  55.1 0.9 collective-permute-start.6
  56.0 49.5 %collective-permute-done.4 = bf16[32,4096]{1,0:T(8,128)(2,1)S(1)} collective-permute-done((bf16[32,4096]{1,0:T(8,128)(2,1)S(1)}, bf16[32,4096]{1,0:T(8,128)(2,1)S(1)}, u32[]{:S(2)}, u32[]{:S(2)}) %collective-permute-start.4) | collective-permute-done | bytes 262176 | tf_op jit(solution)/shard_map/ppermute | solution.py:19
  105.5 1.5 collective-permute-done.5
  107.0 2.8 collective-permute-done.6
  109.8 0.3 collective-permute-start.7
  110.1 1.8 collective-permute-start.8
  111.9 2.0 collective-permute-start.9
  113.9 21.5 %collective-permute-done.7.refs_5_ = bf16[128,4096]{1,0:T(8,128)(2,1)S(1)} collective-permute-done((bf16[128,4096]{1,0:T(8,128)(2,1)S(1)}, bf16[128,4096]{1,0:T(8,128)(2,1)S(1)}, u32[]{:S(2)}, u32[]{:S(2)}) %collective-permute-start.7) | collective-permute-done | bytes 1048608 | tf_op jit(solution)/shard_map/ppermute | solution.py:19
  135.4 19.7 %collective-permute-done.8.refs_6_ = bf16[128,4096]{1,0:T(8,128)(2,1)S(1)} collective-permute-done((bf16[128,4096]{1,0:T(8,128)(2,1)S(1)}, bf16[128,4096]{1,0:T(8,128)(2,1)S(1)}, u32[]{:S(2)}, u32[]{:S(2)}) %collective-permute-start.8) | collective-permute-done | bytes 1048608 | tf_op jit(solution)/shard_map/ppermute | solution.py:19
  155.1 1.7 collective-permute-done.9.refs_7_
  156.8 0.6 pad_add_fusion.refs_0_
  157.3 6.9 %collective-permute-done.10.refs_5_.refs_13_ = bf16[4,128,4096]{2,1,0:T(8,128)(2,1)} collective-permute-done((bf16[4,128,4096]{2,1,0:T(8,128)(2,1)}, bf16[4,128,4096]{2,1,0:T(8,128)(2,1)}, u32[]{:S(2)}, u32[]{:S(2)}) %collective-permute-start.10) | collective-permute-done | bytes 4194336 | tf_op jit(solution)/shard_map/ppermute | solution.py:23
  164.3 18.6 %forward_away.1 = (f32[2,4,4,32,896]{4,3,2,1,0:T(8,128)}, bf16[2,4,4,32,512]{4,3,2,1,0:T(8,128)(2,1)}, bf16[16,32,4096]{2,1,0:T(8,128)(2,1)}, bf16[4096,896]{1,0:T(8,128)(2,1)}, bf16[4096,512]{1,0:T(8,128)(2,1)}) custom-call(s32[3]{0:T(128)} %pad_add_fusion.refs_0_, s32[14,32]{1,0:T(8,128)} %refs_1_.3, s32[14,32]{1,0:T(8,128)} %refs_2_.3, s32[14,32]{1,0:T(8,128)} %refs_3_.3, ...), custom_call_target="tpu_custom_call" | custom-call | flops 738197504 | bytes 3145728 | tf_op jit(solution)/shard_map/forward_away/pallas_call | solution.py:460
  183.1 0.4 collective-permute-start.11
  183.6 0.4 collective-permute-start.13
  184.1 14.2 %forward_kept.1 = (f32[2,4,4,32,896]{4,3,2,1,0:T(8,128)}, bf16[2,4,4,32,512]{4,3,2,1,0:T(8,128)(2,1)}, bf16[16,32,4096]{2,1,0:T(8,128)(2,1)}) custom-call(s32[3]{0:T(128)} %pad_add_fusion.refs_0_, bf16[4096,896]{1,0:T(8,128)(2,1)} %get-tuple-element.57.refs_1_.refs_17_, ...), custom_call_target="tpu_custom_call", output_to_operand_aliasing={{0}: (4, {}), {1}: (5, {})} | custom-call | flops 738197504 | bytes 3145728 | tf_op jit(solution)/shard_map/forward_kept/pallas_call | solution.py:460
  198.4 4.1 %add_convert_fusion.2 = (bf16[4,32,4096]{2,1,0:T(8,128)(2,1)}, bf16[4,32,4096]{2,1,0:T(8,128)(2,1)S(1)}, bf16[4,32,4096]{2,1,0:T(8,128)(2,1)}, bf16[4,32,4096]{2,1,0:T(8,128)(2,1)S(1)}) fusion(bf16[16,32,4096]{2,1,0:T(8,128)(2,1)S(1)} %collective-permute-done.15, bf16[16,32,4096]{2,1,0:T(8,128)(2,1)} %get-tuple-element.67), kind=kLoop, calls=%fused_computation.3 | loop fusion | flops 8388608 | bytes 12582912 | tf_op jit(solution)/shard_map/convert_element_type | solution.py:43
  202.5 1.0 collective-permute-start.16
  203.4 2.3 collective-permute-start.17
  205.7 42.9 %gradients.1 = (bf16[512,896]{1,0:T(8,128)(2,1)}, bf16[512,4096]{1,0:T(8,128)(2,1)}, bf16[336,64,128]{2,1,0:T(8,128)(2,1)}) custom-call(s32[3]{0:T(128)} %pad_add_fusion.refs_0_, s32[14,32]{1,0:T(8,128)} %refs_1_.3, s32[14,32]{1,0:T(8,128)} %refs_2_.3, s32[14,32]{1,0:T(8,128)} %refs_3_.3, bf16[128,4096]{1,0:T(8,128)(2,1)} %copy-done, ...), custom_call_target="tpu_custom_call" | custom-call | flops 2013265920 | bytes 5242880 | tf_op jit(solution)/shard_map/gradients/pallas_call | solution.py:497
  248.6 3.2 collective-permute-done.16
  251.8 2.2 add_convert_fusion.1
  254.1 1.1 copy-done.5
  255.2 7.8 %convolution_convert_fusion = bf16[512,4096]{1,0:T(8,128)(2,1)S(1)} fusion(bf16[512,896]{1,0:T(8,128)(2,1)S(1)} %copy-done.5, bf16[4096,896]{1,0:T(8,128)(2,1)} %get-tuple-element.57.refs_1_.refs_17_), kind=kOutput, calls=%fused_computation.1 | convolution fusion | flops 3760193536 | bytes 12451840 | tf_op jit(solution)/shard_map/dot_general | solution.py:535
  263.0 3.6 add_convert_fusion
  266.6 7.3 %all-to-all-start.1 = ((bf16[16,32,4096]{2,1,0:T(8,128)(2,1)}), bf16[16,32,4096]{2,1,0:T(8,128)(2,1)}, u32[]{:S(2)}, u32[]{:S(2)}) async-start(bf16[16,32,4096]{2,1,0:T(8,128)(2,1)} %bitcast.37), calls=%async_computation.1 | async-start | bytes 8388608 | tf_op jit(solution)/shard_map/all_to_all | solution.py:542
  273.9 1.5 collective-permute-start.21
  275.4 0.6 collective-permute-start.22
  276.0 2.1 collective-permute-start.23
  278.1 32.8 %reduce-scatter.2.cloned.1.call-done = bf16[84,64,128]{2,1,0:T(8,128)(2,1)} async-done(((bf16[336,64,128]{2,1,0:T(8,128)(2,1)}), bf16[84,64,128]{2,1,0:T(8,128)(2,1)}) %reduce-scatter.2.cloned.1.call-update) | async-done | bytes 1376272 | tf_op jit(solution)/shard_map/reduce_scatter | solution.py:544
  310.9 1.4 fusion.5
  312.3 3.5 collective-permute-start.20
  315.7 24.5 %collective-permute-done.21 = bf16[32,4096]{1,0:T(8,128)(2,1)S(1)} collective-permute-done((bf16[32,4096]{1,0:T(8,128)(2,1)S(1)}, bf16[32,4096]{1,0:T(8,128)(2,1)S(1)}, u32[]{:S(2)}, u32[]{:S(2)}) %collective-permute-start.21) | collective-permute-done | bytes 262176 | tf_op jit(solution)/shard_map/ppermute | solution.py:19
  340.2 3.0 collective-permute-done.23
  343.2 0.8 fusion.4
  344.2 0.4 copy.24
  344.6 1.4 reshape.69
  346.0 0.3 fusion
  346.4 1.4 reshape.66
  347.8 1.4 reshape.67
  349.1 3.7 %reduce_sum.12 = bf16[32,4096]{1,0:T(8,128)(2,1)} reduce(bf16[16,32,4096]{2,1,0:T(8,128)(2,1)} %all-to-all-done.1, bf16[]{:T(256)} %constant.25.clone.1), dimensions={0}, to_apply=%region_1.2 | reduce | flops 1966080 | bytes 4456450 | tf_op jit(solution)/shard_map/reduce_sum | solution.py:558
  (46 shorter events, 2.0 us)
Async XLA Ops:
  7.2 157.1 %all-gather.2.cloned.1.call-start = ((), (), s32[]{:S(2)}) async-start(), calls=%async_computation.3 | async-start | bytes 6881280 | tf_op jit(solution)/shard_map/all_gather | solution.py:427
  7.2 13.8 %collective-permute-start.1 = (bf16[32,4096]{1,0:T(8,128)(2,1)}, bf16[32,4096]{1,0:T(8,128)(2,1)S(1)}, u32[]{:S(2)}, u32[]{:S(2)}) collective-permute-start(bf16[32,4096]{1,0:T(8,128)(2,1)} %param.8), channel_id=1, source_target_pairs={{0,12},{4,0},{8,4},{12,8},{1,13},{5,1},{9,5},{13,9},{2,14},{6,2},{... | collective-permute-start | bytes 786440 | tf_op jit(solution)/shard_map/ppermute | solution.py:19
  7.8 14.4 %collective-permute-start.2 = (bf16[32,4096]{1,0:T(8,128)(2,1)}, bf16[32,4096]{1,0:T(8,128)(2,1)}, u32[]{:S(2)}, u32[]{:S(2)}) collective-permute-start(bf16[32,4096]{1,0:T(8,128)(2,1)} %param.8), channel_id=1, source_target_pairs={{0,8},{4,12},{8,0},{12,4},{1,9},{5,13},{9,1},{13,5},{2,10},{6,14},... | collective-permute-start | bytes 786440 | tf_op jit(solution)/shard_map/ppermute | solution.py:19
  10.2 12.9 %collective-permute-start.3 = (bf16[32,4096]{1,0:T(8,128)(2,1)}, bf16[32,4096]{1,0:T(8,128)(2,1)}, u32[]{:S(2)}, u32[]{:S(2)}) collective-permute-start(bf16[32,4096]{1,0:T(8,128)(2,1)} %param.8), channel_id=1, source_target_pairs={{0,4},{4,8},{8,12},{12,0},{1,5},{5,9},{9,13},{13,1},{2,6},{6,10},{... | collective-permute-start | bytes 786440 | tf_op jit(solution)/shard_map/ppermute | solution.py:19
  15.4 23.6 %collective-permute-start = (bf16[7,12,4096]{2,1,0:T(8,128)(2,1)S(1)}, bf16[7,12,4096]{2,1,0:T(8,128)(2,1)}, u32[]{:S(2)}, u32[]{:S(2)}) collective-permute-start(bf16[7,12,4096]{2,1,0:T(8,128)(2,1)S(1)} %pad_maximum_fusion.2), channel_id=1, source_target_pairs={{0,16},{16,0},{1,17},{17,1},{2,18},{18,2},{3,19},{19,3},{4,20},{20... | collective-permute-start | bytes 2064392 | tf_op jit(solution)/shard_map/ppermute | solution.py:23
  19.7 3.4 copy-start.4
  46.1 5.0 %copy-start.3 = (bf16[32,4096]{1,0:T(8,128)(2,1)S(1)}, bf16[32,4096]{1,0:T(8,128)(2,1)}, u32[]{:S(2)}) copy-start(bf16[32,4096]{1,0:T(8,128)(2,1)} %param.9) | copy-start | bytes 786436
  46.1 110.7 %all-to-all-start = ((bf16[4,128,4096]{2,1,0:T(8,128)(2,1)}), bf16[4,128,4096]{2,1,0:T(8,128)(2,1)}, u32[]{:S(2)}, u32[]{:S(2)}) async-start(bf16[4,128,4096]{2,1,0:T(8,128)(2,1)} %broadcast_in_dim.2), calls=%async_computation | async-start | bytes 8388608 | tf_op jit(solution)/shard_map/all_to_all | solution.py:430
  51.1 259.8 %reduce-scatter.2.cloned.1.call-start = ((), (), s32[]{:S(2)}) async-start(), calls=%async_computation.4 | async-start | bytes 6881280 | tf_op jit(solution)/shard_map/reduce_scatter | solution.py:544
  51.1 54.3 %collective-permute-start.4 = (bf16[32,4096]{1,0:T(8,128)(2,1)S(1)}, bf16[32,4096]{1,0:T(8,128)(2,1)S(1)}, u32[]{:S(2)}, u32[]{:S(2)}) collective-permute-start(bf16[32,4096]{1,0:T(8,128)(2,1)S(1)} %copy-done.3), channel_id=1, source_target_pairs={{0,18},{2,0},{16,2},{18,16},{1,19},{3,1},{17,3},{19,17},{4,22},{6,... | collective-permute-start | bytes 786440 | tf_op jit(solution)/shard_map/ppermute | solution.py:19
  54.6 52.4 %collective-permute-start.5 = (bf16[32,4096]{1,0:T(8,128)(2,1)S(1)}, bf16[32,4096]{1,0:T(8,128)(2,1)S(1)}, u32[]{:S(2)}, u32[]{:S(2)}) collective-permute-start(bf16[32,4096]{1,0:T(8,128)(2,1)S(1)} %copy-done.3), channel_id=1, source_target_pairs={{0,16},{2,18},{16,0},{18,2},{1,17},{3,19},{17,1},{19,3},{4,20},{6,... | collective-permute-start | bytes 786440 | tf_op jit(solution)/shard_map/ppermute | solution.py:19
  55.1 54.6 %collective-permute-start.6 = (bf16[32,4096]{1,0:T(8,128)(2,1)S(1)}, bf16[32,4096]{1,0:T(8,128)(2,1)S(1)}, u32[]{:S(2)}, u32[]{:S(2)}) collective-permute-start(bf16[32,4096]{1,0:T(8,128)(2,1)S(1)} %copy-done.3), channel_id=1, source_target_pairs={{0,2},{2,16},{16,18},{18,0},{1,3},{3,17},{17,19},{19,1},{4,6},{6,2... | collective-permute-start | bytes 786440 | tf_op jit(solution)/shard_map/ppermute | solution.py:19
  109.8 73.3 %copy-start = (bf16[128,4096]{1,0:T(8,128)(2,1)}, bf16[128,4096]{1,0:T(8,128)(2,1)S(1)}, u32[]{:S(2)}) copy-start(bf16[128,4096]{1,0:T(8,128)(2,1)S(1)} %constant_dynamic-update-slice_fusion.refs_4_) | copy-start | bytes 3145732
  109.8 25.6 %collective-permute-start.7 = (bf16[128,4096]{1,0:T(8,128)(2,1)S(1)}, bf16[128,4096]{1,0:T(8,128)(2,1)S(1)}, u32[]{:S(2)}, u32[]{:S(2)}) collective-permute-start(bf16[128,4096]{1,0:T(8,128)(2,1)S(1)} %constant_dynamic-update-slice_fusion.refs_4_), channel_id=1, source_target_pairs={{0,12},{4,0},{8,4},{12,8},{1,13},{5,1},{9,5},{13,9},{2,14},{6,2},{... | collective-permute-start | bytes 3145736 | tf_op jit(solution)/shard_map/ppermute | solution.py:19
  110.1 45.0 %collective-permute-start.8 = (bf16[128,4096]{1,0:T(8,128)(2,1)S(1)}, bf16[128,4096]{1,0:T(8,128)(2,1)S(1)}, u32[]{:S(2)}, u32[]{:S(2)}) collective-permute-start(bf16[128,4096]{1,0:T(8,128)(2,1)S(1)} %constant_dynamic-update-slice_fusion.refs_4_), channel_id=1, source_target_pairs={{0,8},{4,12},{8,0},{12,4},{1,9},{5,13},{9,1},{13,5},{2,10},{6,14},... | collective-permute-start | bytes 3145736 | tf_op jit(solution)/shard_map/ppermute | solution.py:19
  111.9 44.9 %collective-permute-start.9 = (bf16[128,4096]{1,0:T(8,128)(2,1)S(1)}, bf16[128,4096]{1,0:T(8,128)(2,1)}, u32[]{:S(2)}, u32[]{:S(2)}) collective-permute-start(bf16[128,4096]{1,0:T(8,128)(2,1)S(1)} %constant_dynamic-update-slice_fusion.refs_4_), channel_id=1, source_target_pairs={{0,4},{4,8},{8,12},{12,0},{1,5},{5,9},{9,13},{13,1},{2,6},{6,10},{... | collective-permute-start | bytes 3145736 | tf_op jit(solution)/shard_map/ppermute | solution.py:19
  135.4 48.1 %copy-start.1 = (bf16[128,4096]{1,0:T(8,128)(2,1)}, bf16[128,4096]{1,0:T(8,128)(2,1)S(1)}, u32[]{:S(2)}) copy-start(bf16[128,4096]{1,0:T(8,128)(2,1)S(1)} %collective-permute-done.7.refs_5_) | copy-start | bytes 3145732
  155.1 28.5 %copy-start.2 = (bf16[128,4096]{1,0:T(8,128)(2,1)}, bf16[128,4096]{1,0:T(8,128)(2,1)S(1)}, u32[]{:S(2)}) copy-start(bf16[128,4096]{1,0:T(8,128)(2,1)S(1)} %collective-permute-done.8.refs_6_) | copy-start | bytes 3145732
  156.7 7.5 %collective-permute-start.10 = (bf16[4,128,4096]{2,1,0:T(8,128)(2,1)}, bf16[4,128,4096]{2,1,0:T(8,128)(2,1)}, u32[]{:S(2)}, u32[]{:S(2)}) collective-permute-start(bf16[4,128,4096]{2,1,0:T(8,128)(2,1)} %all-to-all-done.refs_3_.refs_12_), channel_id=1, source_target_pairs={{0,1},{1,0},{2,3},{3,2},{4,5},{5,4},{6,7},{7,6},{8,9},{9,8},{10,11... | collective-permute-start | bytes 12582920 | tf_op jit(solution)/shard_map/ppermute | solution.py:23
  182.9 15.5 %collective-permute-start.15 = (bf16[16,32,4096]{2,1,0:T(8,128)(2,1)}, bf16[16,32,4096]{2,1,0:T(8,128)(2,1)S(1)}, u32[]{:S(2)}, u32[]{:S(2)}) collective-permute-start(bf16[16,32,4096]{2,1,0:T(8,128)(2,1)} %get-tuple-element.68), channel_id=1, source_target_pairs={{0,1},{1,0},{2,3},{3,2},{4,5},{5,4},{6,7},{7,6},{8,9},{9,8},{10,11... | collective-permute-start | bytes 12582920 | tf_op jit(solution)/shard_map/ppermute | solution.py:23
  183.1 15.2 %collective-permute-start.11 = (bf16[128,4096]{1,0:T(8,128)(2,1)S(1)}, bf16[128,4096]{1,0:T(8,128)(2,1)}, u32[]{:S(2)}, u32[]{:S(2)}) collective-permute-start(bf16[128,4096]{1,0:T(8,128)(2,1)S(1)} %constant_dynamic-update-slice_fusion.refs_4_), channel_id=1, source_target_pairs={{0,1},{1,0},{2,3},{3,2},{4,5},{5,4},{6,7},{7,6},{8,9},{9,8},{10,11... | collective-permute-start | bytes 3145736 | tf_op jit(solution)/shard_map/ppermute | solution.py:23
  183.5 14.9 %collective-permute-start.12 = (bf16[128,4096]{1,0:T(8,128)(2,1)S(1)}, bf16[128,4096]{1,0:T(8,128)(2,1)}, u32[]{:S(2)}, u32[]{:S(2)}) collective-permute-start(bf16[128,4096]{1,0:T(8,128)(2,1)S(1)} %collective-permute-done.7.refs_5_), channel_id=1, source_target_pairs={{0,1},{1,0},{2,3},{3,2},{4,5},{5,4},{6,7},{7,6},{8,9},{9,8},{10,11... | collective-permute-start | bytes 3145736 | tf_op jit(solution)/shard_map/ppermute | solution.py:23
  183.6 14.7 %collective-permute-start.13 = (bf16[128,4096]{1,0:T(8,128)(2,1)S(1)}, bf16[128,4096]{1,0:T(8,128)(2,1)}, u32[]{:S(2)}, u32[]{:S(2)}) collective-permute-start(bf16[128,4096]{1,0:T(8,128)(2,1)S(1)} %collective-permute-done.8.refs_6_), channel_id=1, source_target_pairs={{0,1},{1,0},{2,3},{3,2},{4,5},{5,4},{6,7},{7,6},{8,9},{9,8},{10,11... | collective-permute-start | bytes 3145736 | tf_op jit(solution)/shard_map/ppermute | solution.py:23
  184.0 14.4 %collective-permute-start.14 = (bf16[128,4096]{1,0:T(8,128)(2,1)}, bf16[128,4096]{1,0:T(8,128)(2,1)}, u32[]{:S(2)}, u32[]{:S(2)}) collective-permute-start(bf16[128,4096]{1,0:T(8,128)(2,1)} %collective-permute-done.9.refs_7_), channel_id=1, source_target_pairs={{0,1},{1,0},{2,3},{3,2},{4,5},{5,4},{6,7},{7,6},{8,9},{9,8},{10,11... | collective-permute-start | bytes 3145736 | tf_op jit(solution)/shard_map/ppermute | solution.py:23
  202.5 49.3 %collective-permute-start.16 = (bf16[4,32,4096]{2,1,0:T(8,128)(2,1)}, bf16[4,32,4096]{2,1,0:T(8,128)(2,1)S(1)}, u32[]{:S(2)}, u32[]{:S(2)}) collective-permute-start(bf16[4,32,4096]{2,1,0:T(8,128)(2,1)} %get-tuple-element.75), channel_id=1, source_target_pairs={{0,2},{2,16},{16,18},{18,0},{1,3},{3,17},{17,19},{19,1},{4,6},{6,2... | collective-permute-start | bytes 3145736 | tf_op jit(solution)/shard_map/ppermute | solution.py:19
  203.4 48.4 %collective-permute-start.17 = (bf16[4,32,4096]{2,1,0:T(8,128)(2,1)}, bf16[4,32,4096]{2,1,0:T(8,128)(2,1)}, u32[]{:S(2)}, u32[]{:S(2)}) collective-permute-start(bf16[4,32,4096]{2,1,0:T(8,128)(2,1)} %get-tuple-element.76), channel_id=1, source_target_pairs={{0,18},{2,0},{16,2},{18,16},{1,19},{3,1},{17,3},{19,17},{4,22},{6,... | collective-permute-start | bytes 3145736 | tf_op jit(solution)/shard_map/ppermute | solution.py:19
  205.7 46.1 %collective-permute-start.18 = (bf16[4,32,4096]{2,1,0:T(8,128)(2,1)S(1)}, bf16[4,32,4096]{2,1,0:T(8,128)(2,1)}, u32[]{:S(2)}, u32[]{:S(2)}) collective-permute-start(bf16[4,32,4096]{2,1,0:T(8,128)(2,1)S(1)} %get-tuple-element.77), channel_id=1, source_target_pairs={{0,16},{2,18},{16,0},{18,2},{1,17},{3,19},{17,1},{19,3},{4,20},{6,... | collective-permute-start | bytes 3145736 | tf_op jit(solution)/shard_map/ppermute | solution.py:19
  254.0 1.2 copy-start.5
  254.0 9.0 %collective-permute-start.19 = (bf16[512,4096]{1,0:T(8,128)(2,1)}, bf16[512,4096]{1,0:T(8,128)(2,1)S(1)}, u32[]{:S(2)}, u32[]{:S(2)}) collective-permute-start(bf16[512,4096]{1,0:T(8,128)(2,1)} %get-tuple-element.80), channel_id=1, source_target_pairs={{0,1},{1,0},{2,3},{3,2},{4,5},{5,4},{6,7},{7,6},{8,9},{9,8},{10,11... | collective-permute-start | bytes 12582920 | tf_op jit(solution)/shard_map/ppermute | solution.py:23
  266.6 82.5 %all-to-all-start.1 = ((bf16[16,32,4096]{2,1,0:T(8,128)(2,1)}), bf16[16,32,4096]{2,1,0:T(8,128)(2,1)}, u32[]{:S(2)}, u32[]{:S(2)}) async-start(bf16[16,32,4096]{2,1,0:T(8,128)(2,1)} %bitcast.37), calls=%async_computation.1 | async-start | bytes 8388608 | tf_op jit(solution)/shard_map/all_to_all | solution.py:542
  273.9 66.3 %collective-permute-start.21 = (bf16[32,4096]{1,0:T(8,128)(2,1)S(1)}, bf16[32,4096]{1,0:T(8,128)(2,1)S(1)}, u32[]{:S(2)}, u32[]{:S(2)}) collective-permute-start(bf16[32,4096]{1,0:T(8,128)(2,1)S(1)} %get-tuple-element.101), channel_id=1, source_target_pairs={{0,4},{4,8},{8,12},{12,0},{1,5},{5,9},{9,13},{13,1},{2,6},{6,10},{... | collective-permute-start | bytes 786440 | tf_op jit(solution)/shard_map/ppermute | solution.py:19
  275.4 64.8 %collective-permute-start.22 = (bf16[32,4096]{1,0:T(8,128)(2,1)S(1)}, bf16[32,4096]{1,0:T(8,128)(2,1)S(1)}, u32[]{:S(2)}, u32[]{:S(2)}) collective-permute-start(bf16[32,4096]{1,0:T(8,128)(2,1)S(1)} %get-tuple-element.103), channel_id=1, source_target_pairs={{0,12},{4,0},{8,4},{12,8},{1,13},{5,1},{9,5},{13,9},{2,14},{6,2},{... | collective-permute-start | bytes 786440 | tf_op jit(solution)/shard_map/ppermute | solution.py:19
  276.0 67.2 %collective-permute-start.23 = (bf16[32,4096]{1,0:T(8,128)(2,1)S(1)}, bf16[32,4096]{1,0:T(8,128)(2,1)S(1)}, u32[]{:S(2)}, u32[]{:S(2)}) collective-permute-start(bf16[32,4096]{1,0:T(8,128)(2,1)S(1)} %get-tuple-element.102), channel_id=1, source_target_pairs={{0,8},{4,12},{8,0},{12,4},{1,9},{5,13},{9,1},{13,5},{2,10},{6,14},... | collective-permute-start | bytes 786440 | tf_op jit(solution)/shard_map/ppermute | solution.py:19
  312.3 31.8 %collective-permute-start.20 = (bf16[7,6,64,128]{3,2,1,0:T(8,128)(2,1)S(1)}, bf16[7,6,64,128]{3,2,1,0:T(8,128)(2,1)S(1)}, u32[]{:S(2)}, u32[]{:S(2)}) collective-permute-start(bf16[7,6,64,128]{3,2,1,0:T(8,128)(2,1)S(1)} %bitcast.45), channel_id=1, source_target_pairs={{0,16},{16,0},{1,17},{17,1},{2,18},{18,2},{3,19},{19,3},{4,20},{20... | collective-permute-start | bytes 2064392 | tf_op jit(solution)/shard_map/ppermute | solution.py:23
Sparse Core Ops, SparseCore 0:
  43.6 58.1 all-gather.1
  254.2 56.6 reduce-scatter.1

commit v5 on v3

--- a/solution.py
+++ b/solution.py
@@ -65,8 +65,8 @@
     ]
 
 
-def owner_row(place, core, z, x):
-    return core * RING * RING + (place[1] + z) % RING * RING + (place[2] + x) % RING
+def owner_row(core, z, x):
+    return core * RING * RING + z * RING + x % RING
 
 
 def chunk_copies(pieces, buf, sems, place):
@@ -74,7 +74,7 @@
     copies = []
     for n, piece in enumerate(pieces):
         for x in range(RING):
-            at = owner_row(place, n // RING, n % RING, x) * per
+            at = owner_row(n // RING, n % RING, place[2] + x) * per
             copies.append(
                 pltpu.make_async_copy(
                     piece.at[pl.ds(x * per, per)],
@@ -230,10 +230,11 @@
     @pl.when(i == 0)
     def _():
         if not first:
-            for copy in w_copies:
-                copy.start()
+            w_copies[0].start()
         for copy in copies:
             copy.start()
+        if not first:
+            w_copies[1].start()
         if first:
             where = Tiles(half_panels, kept_here, place[0])
             build_input_weights(where, gate_idx, up_idx, tiles, w_ref)
@@ -262,18 +263,18 @@
 
 
 def gradient_kernel(half_panels, kept_here, place, gate_idx, up_idx, down_idx, *refs):
-    dy_pieces, x_pieces = refs[:2], refs[2:10]
-    wd_ref, m_ref, h_ref, back_kept, back_away, out_ref, dy_buf, x_buf, g_ref, acc, dy_sems, x_sems, g_sems = refs[10:]
+    dy_pieces, x_pieces, refs = refs[:2], refs[2:10], refs[10:]
+    wd_ref, m_ref, h_ref, w_gu, back_kept, dx_away, out_ref = refs[:7]
+    dy_buf, x_buf, g_ref, acc, w_ref, dy_sems, x_sems, g_sems = refs[7:]
     i = pl.program_id(0)
     where = Tiles(half_panels, kept_here, place[0])
     rows = dy_buf.shape[0] // 4
     dy_copies = ring_copies(dy_pieces, dy_buf, dy_sems, place)
     x_copies = chunk_copies(x_pieces, x_buf, x_sems, place)
+    w_copy = pltpu.make_async_copy(w_gu, w_ref, g_sems.at[2])
     half_rows = back_kept.shape[0]
-    g_copies = [
-        pltpu.make_async_copy(g_ref.at[pl.ds(n * half_rows, half_rows)], out, g_sems.at[n])
-        for n, out in enumerate((back_kept, back_away))
-    ]
+    g_copy = pltpu.make_async_copy(g_ref.at[pl.ds(0, half_rows)], back_kept, g_sems.at[0])
+    dx_copy = pltpu.make_async_copy(dy_buf.at[pl.ds(0, half_rows)], dx_away, g_sems.at[1])
     hid = h_ref.shape[1]
     cols = dy_buf.shape[1] // 4
     mask = left_half((rows, 2 * BLK))
@@ -282,8 +283,6 @@
     @pl.when(i == 0)
     def _():
         for copy in dy_copies:
-            copy.start()
-        for copy in x_copies:
             copy.start()
 
     for t in range(4):
@@ -309,7 +308,7 @@
             for a in range(RING // 2):
                 for b in range(RING):
                     at = (a * RING + b) * per
-                    chunk = owner_row(place, i // 2, b, (i % 2) * (RING // 2) + a)
+                    chunk = owner_row(i // 2, b, place[2] + (i % 2) * (RING // 2) + a)
                     rows_at = pl.ds(pl.multiple_of(chunk * per, per), per)
                     g_ref[rows_at, lanes] = (
                         spread[at : at + per] * m_ref[0, b, a, :, lanes]
@@ -324,16 +323,18 @@
         )
         acc[pl.ds(at, cols), :hid] = part.astype(BF)
 
+    @pl.when(i == 3)
+    def _():
+        w_copy.start()
+        for copy in x_copies:
+            copy.start()
+
     @pl.when(i == 4)
     def _():
-        for copy in g_copies:
-            copy.start()
+        g_copy.start()
 
     @pl.when(i == 7)
     def _():
-        for copy in x_copies:
-            copy.wait()
-
         def take(step, carry):
             group, m = step // where.pairs, step % where.pairs
             j = where.kept(group, 2 * m)
@@ -350,9 +351,28 @@
 
         lax.fori_loop(0, 2 * RING * where.pairs, take, 0)
 
-    @pl.when(i >= 8)
+    @pl.when(i == 8)
+    def _():
+        w_copy.wait()
+
+    @pl.when((i >= 8) & (i < 12))
     def _():
         at = pl.multiple_of((i - 8) * cols, cols)
+        part = lax.dot_general(
+            g_ref[half_rows:, :], w_ref[pl.ds(at, cols), :], (((1,), (1,)), ((), ())),
+            preferred_element_type=F32,
+        )
+        dy_buf[:half_rows, pl.ds(at, cols)] = part.astype(BF)
+
+    @pl.when(i == 12)
+    def _():
+        dx_copy.start()
+        for copy in x_copies:
+            copy.wait()
+
+    @pl.when(i >= 12)
+    def _():
+        at = pl.multiple_of((i - 12) * cols, cols)
         part = lax.dot_general(
             x_buf[:, pl.ds(at, cols)], g_ref[...], (((0,), (0,)), ((), ())),
             preferred_element_type=F32,
@@ -372,8 +392,8 @@
             return carry
 
         lax.fori_loop(0, 2 * RING * kept_here, take, 0)
-        for copy in g_copies:
-            copy.wait()
+        g_copy.wait()
+        dx_copy.wait()
 
 
 def cost(flops, nbytes):
@@ -474,9 +494,9 @@
     mult, y_sum = lax.optimization_barrier((mult, y_sum))
     y_z = scatter_direct(y_sum, Z)
 
-    steps = 12
+    steps = 16
     x_tile = lambda i: jnp.minimum(i, 3)
-    back_kept, back_away, terms = pl.pallas_call(
+    back_kept, dx_away, terms = pl.pallas_call(
         part(gradient_kernel, half, kept_here),
         grid=(steps,),
         in_specs=[smem] * 4
@@ -487,39 +507,56 @@
                 (1, RING, pair, per, two), lambda i: (x_tile(i) // 2, 0, x_tile(i) % 2, 0, 0)
             ),
             full(tokens, hid),
+            hbm,
         ],
         out_specs=[hbm, hbm, out_full(*tiles.shape)],
-        out_shape=[shape((tokens // 2, two), BF)] * 2 + [shape(tiles.shape, BF)],
+        out_shape=[
+            shape((tokens // 2, two), BF),
+            shape((tokens // 2, width), BF),
+            shape(tiles.shape, BF),
+        ],
         scratch_shapes=[
             pltpu.VMEM((tokens, width), BF),
             pltpu.VMEM((tokens, width), BF),
             pltpu.VMEM((tokens, two), BF),
             pltpu.VMEM((width, two), BF),
+            pltpu.VMEM((width, two), BF),
             pltpu.SemaphoreType.DMA((32,)),
             pltpu.SemaphoreType.DMA((32,)),
-            pltpu.SemaphoreType.DMA((2,)),
+            pltpu.SemaphoreType.DMA((3,)),
         ],
         compiler_params=kernel_params(60),
         cost_estimate=cost(gu_flops + 2 * d_flops, 40 * MIB),
         name="gradients",
     )(
         place, gate_idx, up_idx, down_idx, *dy_pieces, *x_own, *x_core,
-        w_d, mult, hidden.reshape(tokens, hid),
+        w_d, mult, hidden.reshape(tokens, hid), w_gu,
     )
 
     def project(left):
         return lax.dot_general(left, w_gu, (((1,), (1,)), ((), ())), preferred_element_type=F32)
 
-    back_away, y_z = lax.optimization_barrier((back_away, y_z))
+    back_kept, dx_away, terms, y_z = lax.optimization_barrier((back_kept, dx_away, terms, y_z))
+    dx_recv = swap(dx_away, "c")
+    dx_kept, dx_recv = lax.optimization_barrier((project(back_kept).astype(BF), dx_recv))
+
+    def chip_rows(first, count):
+        split = lambda v: v[:, first : first + count].reshape(RING, RING, per, count)
+        return add(split(dx_kept), split(dx_recv))
+
+    def over_x(value):
+        return jnp.sum(lax.all_to_all(value, "x", 0, 0, tiled=True).astype(F32), axis=0).astype(BF)
+
+    x_first = jnp.transpose(chip_rows(0, width // 2), (1, 0, 2, 3))
+    z_first = chip_rows(width // 2, width // 2)
+    y_z, x_first, z_first = lax.optimization_barrier((y_z, x_first, z_first))
+    x_first = over_x(x_first)
+    z_first = scatter_direct([z_first[n] for n in range(RING)], Z)
     y_seq = scatter_direct([y_z[n] for n in range(RING)], "x")
-    dx_away = project(back_away).astype(BF)
-    dx_recv = swap(dx_away, "c")
-    back_kept, dx_away = lax.optimization_barrier((back_kept, dx_away))
-    dx_kept, dx_recv = lax.optimization_barrier((project(back_kept).astype(BF), dx_recv))
-    dx_chip = add(dx_kept, dx_recv).reshape(chunks)
-    dx_chip, y_seq = lax.optimization_barrier((dx_chip, y_seq))
-    dx_parts = lax.all_to_all(dx_chip, ZX, 0, 0, tiled=True)
-    dx_seq = jnp.sum(dx_parts.astype(F32), axis=0).astype(BF)
+    x_first, z_first, y_seq = lax.optimization_barrier((x_first, z_first, y_seq))
+    x_first = scatter_direct([x_first[n] for n in range(RING)], Z)
+    z_first = over_x(z_first)
+    dx_seq = jnp.concatenate([x_first, z_first], axis=1)
 
     summed = lax.psum_scatter(terms, "y", scatter_dimension=0, tiled=True)
     summed = summed.reshape(2, half, per_panel, edge, 2 * edge)

time: 315 us -> 293 us (0.930)
  waiting for transfers between devices: 143 us -> 106 us
  starting transfers between devices: 40.7 us -> 52 us
  matrix products: 14.2 us -> 7.83 us
  Pallas kernels: 68.1 us -> 72.9 us
  local copies, waits for them, and re-layouts: 14.4 us -> 18.7 us
    all_to_all x1 -> x2, waiting for transfers between devices: 45.7 us -> 2.72 us  [over_x(): lax.all_to_all(value, 'x', 0, 0, tiled=True).astype(F32)]
    ppermute x12 -> x18, starting transfers between devices: 15.3 us -> 23.7 us  [shift(): lax.ppermute(value, axis, [(i, (i + step) % RING) for i in range(RING)])]
    reduce_scatter x1, waiting for transfers between devices: 7.35 us -> 0.01 us  [per_device(): summed = lax.psum_scatter(terms, 'y', scatter_dimension=0, tiled=True)]
    ppermute x12 -> x18, waiting for transfers between devices: 61 us -> 68.2 us  [shift(): lax.ppermute(value, axis, [(i, (i + step) % RING) for i in range(RING)])]
    dot_general x2 -> x1, matrix products: 14.2 us -> 7.83 us  [project(): lax.dot_general(left, w_gu, (((1,), (1,)), ((), ())), preferred_element_t...]
    ppermute x9, waiting for transfers between devices: 28.7 us -> 34.7 us  [swap(): return lax.ppermute(value, axis, [(0, 1), (1, 0)])]
    pallas_call x1, Pallas kernels: 35.3 us -> 40 us  [per_device(): pl.pallas_call(part(gradient_kernel, half, kept_here), grid=(steps,), in_...]
    all_to_all x1 -> x2, starting transfers between devices: 6.6 us -> 10.3 us  [over_x(): lax.all_to_all(value, 'x', 0, 0, tiled=True).astype(F32)]
  transfers between devices with their start and end apart: 26 -> 33, of which waited for: 12 -> 13; matrix products, arithmetic and copies ran while one was open for 12% -> 12% of each run, Pallas kernels for 22% -> 25%
where the time goes in v5:
time: 293 us; the launch traced here: 292 us
  waiting for transfers between devices  106 us (36%)
  Pallas kernels  72.9 us (25%)
  starting transfers between devices  52 us (18%)
  other arithmetic  21 us (7%)
  local copies, waits for them, and re-layouts  18.7 us (6%)
  between operations  14.3 us (5%)
  matrix products  7.83 us (3%)
    ppermute x18, waiting for transfers between devices, shift(): lax.ppermute(value, axis, [(i, (i + step) % RING) for i in range(RING)])  68.2 us
    pallas_call x1, Pallas kernels, per_device(): pl.pallas_call(part(gradient_kernel, half, kept_here), grid=(steps,), in_...  40 us
    ppermute x9, waiting for transfers between devices, swap(): return lax.ppermute(value, axis, [(0, 1), (1, 0)])  34.7 us
    pallas_call x2, Pallas kernels, forward(): pl.pallas_call(part(forward_kernel, half, kept_here, first), grid=(2,), i...  32.8 us
    ppermute x18, starting transfers between devices, shift(): lax.ppermute(value, axis, [(i, (i + step) % RING) for i in range(RING)])  23.7 us
    all_to_all x2, starting transfers between devices, gather_all(): return lax.all_to_all(wide, axis, 0, 0, tiled=True)  10.5 us
    all_to_all x2, starting transfers between devices, over_x(): lax.all_to_all(value, 'x', 0, 0, tiled=True).astype(F32)  10.3 us
    dot_general x1, matrix products, project(): lax.dot_general(left, w_gu, (((1,), (1,)), ((), ())), preferred_element_t...  7.83 us
  transfers between devices with their start and end apart: 33, of which 13 were waited for; matrix products, arithmetic and copies ran while one was open for 12% of the time, Pallas kernels for 25%

profile of v5, /device:TPU:26, one launch (start us, length us, event | category | flops | bytes accessed | tf_op | source)
XLA Modules:
  0.0 292.4 jit_solution(6976195539123225907)
XLA Ops:
  7.2 0.6 collective-permute-start.1
  7.8 2.4 collective-permute-start.2
  10.2 1.8 collective-permute-start.3
  12.0 2.0 broadcast_in_dim.4
  14.0 5.4 %all-to-all-start = ((bf16[4,32,4096]{2,1,0:T(8,128)(2,1)}), bf16[4,32,4096]{2,1,0:T(8,128)(2,1)S(1)}, u32[]{:S(2)}, u32[]{:S(2)}) async-start(bf16[4,32,4096]{2,1,0:T(8,128)(2,1)} %broadcast_in_dim.4), calls=%async_computation | async-start | bytes 2097152 | tf_op jit(solution)/shard_map/all_to_all | solution.py:425
  19.5 0.7 reshape.67
  20.5 0.7 reshape.65
  21.2 1.9 reshape.66
  23.2 0.5 pad_maximum_fusion
  23.8 3.6 %collective-permute-start = (bf16[7,6,64,128]{3,2,1,0:T(8,128)(2,1)S(1)}, bf16[7,6,64,128]{3,2,1,0:T(8,128)(2,1)S(1)}, u32[]{:S(2)}, u32[]{:S(2)}) collective-permute-start(bf16[7,6,64,128]{3,2,1,0:T(8,128)(2,1)S(1)} %get-tuple-element.97), channel_id=1, source_target_pairs={{0,16},{16,0},{1,17},{17,1},{2,18},{18,2},{3,19},{19,3},{4,20},{20... | collective-permute-start | bytes 2064392 | tf_op jit(solution)/shard_map/ppermute | solution.py:23
  27.5 1.2 pad_maximum_fusion.2.refs_3_.refs_6_
  28.7 19.8 %collective-permute-done = bf16[7,6,64,128]{3,2,1,0:T(8,128)(2,1)S(1)} collective-permute-done((bf16[7,6,64,128]{3,2,1,0:T(8,128)(2,1)S(1)}, bf16[7,6,64,128]{3,2,1,0:T(8,128)(2,1)S(1)}, u32[]{:S(2)}, u32[]{:S(2)}) %collective-permute-start) | collective-permute-done | bytes 688160 | tf_op jit(solution)/shard_map/ppermute | solution.py:23
  48.5 1.2 pad_maximum_fusion.1
  49.7 2.6 broadcast_in_dim.5
  52.3 5.0 %all-to-all-start.1 = ((bf16[4,4,32,4096]{3,2,1,0:T(8,128)(2,1)}), bf16[4,4,32,4096]{3,2,1,0:T(8,128)(2,1)}, u32[]{:S(2)}, u32[]{:S(2)}) async-start(bf16[4,4,32,4096]{3,2,1,0:T(8,128)(2,1)} %broadcast_in_dim.5), calls=%async_computation.1 | async-start | bytes 8388608 | tf_op jit(solution)/shard_map/all_to_all | solution.py:425
  57.3 0.6 collective-permute-start.9
  57.9 2.7 collective-permute-start.5
  60.6 43.2 %collective-permute-done.9.refs_6_.refs_9_ = bf16[128,4096]{1,0:T(8,128)(2,1)S(1)} collective-permute-done((bf16[128,4096]{1,0:T(8,128)(2,1)S(1)}, bf16[128,4096]{1,0:T(8,128)(2,1)S(1)}, u32[]{:S(2)}, u32[]{:S(2)}) %collective-permute-start.9) | collective-permute-done | bytes 1048608 | tf_op jit(solution)/shard_map/ppermute | solution.py:19
  103.8 0.5 collective-permute-start.6
  104.4 0.6 pad_add_fusion.refs_0_
  105.0 1.6 collective-permute-done.10.refs_8_.refs_13_
  106.6 3.0 %collective-permute-done.6.refs_6_.refs_11_ = bf16[128,4096]{1,0:T(8,128)(2,1)} collective-permute-done((bf16[128,4096]{1,0:T(8,128)(2,1)S(1)}, bf16[128,4096]{1,0:T(8,128)(2,1)}, u32[]{:S(2)}, u32[]{:S(2)}) %collective-permute-start.6) | collective-permute-done | bytes 1048608 | tf_op jit(solution)/shard_map/ppermute | solution.py:23
  110.0 18.6 %forward_away.1 = (f32[2,4,4,32,896]{4,3,2,1,0:T(8,128)}, bf16[2,4,4,32,512]{4,3,2,1,0:T(8,128)(2,1)}, bf16[16,32,4096]{2,1,0:T(8,128)(2,1)}, bf16[4096,896]{1,0:T(8,128)(2,1)}, bf16[4096,512]{1,0:T(8,128)(2,1)}) custom-call(s32[3]{0:T(128)} %pad_add_fusion.refs_0_, s32[14,32]{1,0:T(8,128)} %refs_1_.3, s32[14,32]{1,0:T(8,128)} %refs_2_.3, s32[14,32]{1,0:T(8,128)} %refs_3_.3, ...), custom_call_target="tpu_custom_call" | custom-call | flops 738197504 | bytes 3145728 | tf_op jit(solution)/shard_map/forward_away/pallas_call | solution.py:462
  128.6 0.5 collective-permute-start.12
  129.1 14.2 %forward_kept.1 = (f32[2,4,4,32,896]{4,3,2,1,0:T(8,128)}, bf16[2,4,4,32,512]{4,3,2,1,0:T(8,128)(2,1)}, bf16[16,32,4096]{2,1,0:T(8,128)(2,1)}) custom-call(s32[3]{0:T(128)} %pad_add_fusion.refs_0_, bf16[4096,896]{1,0:T(8,128)(2,1)} %get-tuple-element.51.refs_1_.refs_17_, ...), custom_call_target="tpu_custom_call", output_to_operand_aliasing={{0}: (7, {}), {1}: (8, {})} | custom-call | flops 738197504 | bytes 3145728 | tf_op jit(solution)/shard_map/forward_kept/pallas_call | solution.py:462
  143.3 3.9 %add_convert_fusion.3 = (bf16[4,32,4096]{2,1,0:T(8,128)(2,1)S(1)}, bf16[4,32,4096]{2,1,0:T(8,128)(2,1)S(1)}, bf16[4,32,4096]{2,1,0:T(8,128)(2,1)}, bf16[4,32,4096]{2,1,0:T(8,128)(2,1)S(1)}) fusion(bf16[16,32,4096]{2,1,0:T(8,128)(2,1)S(1)} %collective-permute-done.12, bf16[16,32,4096]{2,1,0:T(8,128)(2,1)} %get-tuple-element.58), kind=kLoop, calls=%fused_computation.5 | loop fusion | flops 8388608 | bytes 12582912 | tf_op jit(solution)/shard_map/convert_element_type | solution.py:43
  147.2 3.2 %collective-permute-start.14 = (bf16[4,32,4096]{2,1,0:T(8,128)(2,1)S(1)}, bf16[4,32,4096]{2,1,0:T(8,128)(2,1)}, u32[]{:S(2)}, u32[]{:S(2)}) collective-permute-start(bf16[4,32,4096]{2,1,0:T(8,128)(2,1)S(1)} %get-tuple-element.67), channel_id=1, source_target_pairs={{0,18},{2,0},{16,2},{18,16},{1,19},{3,1},{17,3},{19,17},{4,22},{6,... | collective-permute-start | bytes 3145736 | tf_op jit(solution)/shard_map/ppermute | solution.py:19
  150.5 40.0 %gradients.1 = (bf16[512,896]{1,0:T(8,128)(2,1)}, bf16[512,4096]{1,0:T(8,128)(2,1)}, bf16[336,64,128]{2,1,0:T(8,128)(2,1)}) custom-call(s32[3]{0:T(128)} %pad_add_fusion.refs_0_, s32[14,32]{1,0:T(8,128)} %refs_1_.3, s32[14,32]{1,0:T(8,128)} %refs_2_.3, s32[14,32]{1,0:T(8,128)} %refs_3_.3, bf16[4,4,32,4096]{3,2,1,0:T(8,128)(2,1)} %all-to-all-done.1.refs_4_, ...), custom_call_target="tpu_custom_call" | custom-call | flops 2013265920 | bytes 5242880 | tf_op jit(solution)/shard_map/gradients/pallas_call | solution.py:499
  190.5 5.9 %collective-permute-done.13 = bf16[4,32,4096]{2,1,0:T(8,128)(2,1)} collective-permute-done((bf16[4,32,4096]{2,1,0:T(8,128)(2,1)}, bf16[4,32,4096]{2,1,0:T(8,128)(2,1)}, u32[]{:S(2)}, u32[]{:S(2)}) %collective-permute-start.13) | collective-permute-done | bytes 1048608 | tf_op jit(solution)/shard_map/ppermute | solution.py:19
  196.4 2.5 add_convert_fusion.2
  199.1 1.0 copy-done.6
  200.1 7.8 %convolution_convert_fusion = bf16[512,4096]{1,0:T(8,128)(2,1)S(1)} fusion(bf16[512,896]{1,0:T(8,128)(2,1)S(1)} %copy-done.6, bf16[4096,896]{1,0:T(8,128)(2,1)} %get-tuple-element.51.refs_1_.refs_17_), kind=kOutput, calls=%fused_computation | convolution fusion | flops 3760193536 | bytes 12451840 | tf_op jit(solution)/shard_map/dot_general | solution.py:537
  208.0 3.7 %add_convert_fusion = (bf16[512,2048]{1,0:T(8,128)(2,1)S(1)}, bf16[512,2048]{1,0:T(8,128)(2,1)S(1)}) fusion(bf16[512,4096]{1,0:T(8,128)(2,1)} %collective-permute-done.16, bf16[512,4096]{1,0:T(8,128)(2,1)S(1)} %convolution_convert_fusion), kind=kLoop, calls=%fused_computation.1 | loop fusion | flops 8388608 | bytes 12582912 | tf_op jit(solution)/shard_map/convert_element_type | solution.py:43
  211.7 1.6 copy.23
  213.3 0.9 slice_bitcast_fusion.5
  214.2 1.4 collective-permute-start.20
  215.5 0.7 collective-permute-start.21
  216.2 2.0 collective-permute-start.22
  218.2 5.9 %all-to-all-start.2 = ((bf16[4,4,32,2048]{3,2,1,0:T(8,128)(2,1)}), bf16[4,4,32,2048]{3,2,1,0:T(8,128)(2,1)}, u32[]{:S(2)}, u32[]{:S(2)}) async-start(bf16[4,4,32,2048]{3,2,1,0:T(8,128)(2,1)} %bitcast.55), calls=%async_computation.2 | async-start | bytes 4194304 | tf_op jit(solution)/shard_map/all_to_all | solution.py:548
  224.1 0.4 collective-permute-start.17
  224.6 2.9 collective-permute-start.18
  227.4 1.1 collective-permute-start.19
  228.5 2.9 collective-permute-done.22
  231.4 1.9 fusion.7
  233.2 6.6 %collective-permute-done.17 = bf16[4,32,2048]{2,1,0:T(8,128)(2,1)S(1)} collective-permute-done((bf16[4,32,2048]{2,1,0:T(8,128)(2,1)S(1)}, bf16[4,32,2048]{2,1,0:T(8,128)(2,1)S(1)}, u32[]{:S(2)}, u32[]{:S(2)}) %collective-permute-start.17) | collective-permute-done | bytes 524320 | tf_op jit(solution)/shard_map/ppermute | solution.py:19
  239.8 8.1 %collective-permute-done.18 = bf16[4,32,2048]{2,1,0:T(8,128)(2,1)S(1)} collective-permute-done((bf16[4,32,2048]{2,1,0:T(8,128)(2,1)S(1)}, bf16[4,32,2048]{2,1,0:T(8,128)(2,1)S(1)}, u32[]{:S(2)}, u32[]{:S(2)}) %collective-permute-start.18) | collective-permute-done | bytes 524320 | tf_op jit(solution)/shard_map/ppermute | solution.py:19
  248.0 1.5 collective-permute-done.19
  249.4 1.1 fusion.2
  250.6 1.3 all-to-all-done.2
  251.8 2.0 reduce_sum.24
  253.9 0.7 slice_bitcast_fusion.8
  254.6 3.2 %collective-permute-start.24 = (bf16[32,2048]{1,0:T(8,128)(2,1)}, bf16[32,2048]{1,0:T(8,128)(2,1)S(1)}, u32[]{:S(2)}, u32[]{:S(2)}) collective-permute-start(bf16[32,2048]{1,0:T(8,128)(2,1)} %get-tuple-element.103), channel_id=1, source_target_pairs={{0,18},{2,0},{16,2},{18,16},{1,19},{3,1},{17,3},{19,17},{4,22},{6,... | collective-permute-start | bytes 393224 | tf_op jit(solution)/shard_map/ppermute | solution.py:19
  257.8 0.8 collective-permute-start.25
  258.6 4.4 %all-to-all-start.3 = ((bf16[4,32,2048]{2,1,0:T(8,128)(2,1)}), bf16[4,32,2048]{2,1,0:T(8,128)(2,1)S(1)}, u32[]{:S(2)}, u32[]{:S(2)}) async-start(bf16[4,32,2048]{2,1,0:T(8,128)(2,1)} %fusion.2), calls=%async_computation.3 | async-start | bytes 1048576 | tf_op jit(solution)/shard_map/all_to_all | solution.py:548
  263.0 1.4 fusion.11
  264.4 2.8 collective-permute-start.26
  267.2 1.0 fusion.10
  268.2 1.5 all-to-all-done.3
  269.7 0.7 pad_maximum_fusion.4
  270.4 10.0 %collective-permute-done.26 = bf16[7,6,64,128]{3,2,1,0:T(8,128)(2,1)S(1)} collective-permute-done((bf16[7,6,64,128]{3,2,1,0:T(8,128)(2,1)S(1)}, bf16[7,6,64,128]{3,2,1,0:T(8,128)(2,1)S(1)}, u32[]{:S(2)}, u32[]{:S(2)}) %collective-permute-start.26) | collective-permute-done | bytes 688160 | tf_op jit(solution)/shard_map/ppermute | solution.py:23
  281.0 0.4 copy.21
  281.4 1.4 reshape.74
  282.8 1.4 reshape.71
  284.2 1.4 reshape.72
  (54 shorter events, 1.8 us)
Async XLA Ops:
  7.2 12.3 %copy-start.3 = (bf16[14,4,4096]{2,1,0:T(4,128)(2,1)S(1)}, bf16[14,4,4096]{2,1,0:T(4,128)(2,1)}, u32[]{:S(2)}) copy-start(bf16[14,4,4096]{2,1,0:T(4,128)(2,1)} %param.14) | copy-start | bytes 1376260
  7.2 20.3 %collective-permute-start.1 = (bf16[32,4096]{1,0:T(8,128)(2,1)}, bf16[32,4096]{1,0:T(8,128)(2,1)}, u32[]{:S(2)}, u32[]{:S(2)}) collective-permute-start(bf16[32,4096]{1,0:T(8,128)(2,1)} %param.8), channel_id=1, source_target_pairs={{0,12},{4,0},{8,4},{12,8},{1,13},{5,1},{9,5},{13,9},{2,14},{6,2},{... | collective-permute-start | bytes 786440 | tf_op jit(solution)/shard_map/ppermute | solution.py:19
  7.8 19.7 %collective-permute-start.2 = (bf16[32,4096]{1,0:T(8,128)(2,1)}, bf16[32,4096]{1,0:T(8,128)(2,1)}, u32[]{:S(2)}, u32[]{:S(2)}) collective-permute-start(bf16[32,4096]{1,0:T(8,128)(2,1)} %param.8), channel_id=1, source_target_pairs={{0,8},{4,12},{8,0},{12,4},{1,9},{5,13},{9,1},{13,5},{2,10},{6,14},... | collective-permute-start | bytes 786440 | tf_op jit(solution)/shard_map/ppermute | solution.py:19
  10.2 17.3 %collective-permute-start.3 = (bf16[32,4096]{1,0:T(8,128)(2,1)}, bf16[32,4096]{1,0:T(8,128)(2,1)}, u32[]{:S(2)}, u32[]{:S(2)}) collective-permute-start(bf16[32,4096]{1,0:T(8,128)(2,1)} %param.8), channel_id=1, source_target_pairs={{0,4},{4,8},{8,12},{12,0},{1,5},{5,9},{9,13},{13,1},{2,6},{6,10},{... | collective-permute-start | bytes 786440 | tf_op jit(solution)/shard_map/ppermute | solution.py:19
  14.0 6.5 %copy-start.4 = (bf16[14,4,4096]{2,1,0:T(4,128)(2,1)S(1)}, bf16[14,4,4096]{2,1,0:T(4,128)(2,1)}, u32[]{:S(2)}) copy-start(bf16[14,4,4096]{2,1,0:T(4,128)(2,1)} %param.10) | copy-start | bytes 1376260
  14.0 34.4 %all-to-all-start = ((bf16[4,32,4096]{2,1,0:T(8,128)(2,1)}), bf16[4,32,4096]{2,1,0:T(8,128)(2,1)S(1)}, u32[]{:S(2)}, u32[]{:S(2)}) async-start(bf16[4,32,4096]{2,1,0:T(8,128)(2,1)} %broadcast_in_dim.4), calls=%async_computation | async-start | bytes 2097152 | tf_op jit(solution)/shard_map/all_to_all | solution.py:425
  19.5 90.5 %all-gather.2.cloned.1.call-start = ((), (), s32[]{:S(2)}) async-start(), calls=%async_computation.5 | async-start | bytes 6881280 | tf_op jit(solution)/shard_map/all_gather | solution.py:431
  23.7 3.8 %copy-start.5 = (bf16[32,4096]{1,0:T(8,128)(2,1)S(1)}, bf16[32,4096]{1,0:T(8,128)(2,1)}, u32[]{:S(2)}) copy-start(bf16[32,4096]{1,0:T(8,128)(2,1)} %param.8) | copy-start | bytes 786436
  23.8 24.6 %collective-permute-start = (bf16[7,6,64,128]{3,2,1,0:T(8,128)(2,1)S(1)}, bf16[7,6,64,128]{3,2,1,0:T(8,128)(2,1)S(1)}, u32[]{:S(2)}, u32[]{:S(2)}) collective-permute-start(bf16[7,6,64,128]{3,2,1,0:T(8,128)(2,1)S(1)} %get-tuple-element.97), channel_id=1, source_target_pairs={{0,16},{16,0},{1,17},{17,1},{2,18},{18,2},{3,19},{19,3},{4,20},{20... | collective-permute-start | bytes 2064392 | tf_op jit(solution)/shard_map/ppermute | solution.py:23
  28.7 31.9 %copy-start = (bf16[128,4096]{1,0:T(8,128)(2,1)}, bf16[128,4096]{1,0:T(8,128)(2,1)S(1)}, u32[]{:S(2)}) copy-start(bf16[128,4096]{1,0:T(8,128)(2,1)S(1)} %pad_maximum_fusion.2.refs_3_.refs_6_) | copy-start | bytes 3145732
  52.3 57.5 %all-to-all-start.1 = ((bf16[4,4,32,4096]{3,2,1,0:T(8,128)(2,1)}), bf16[4,4,32,4096]{3,2,1,0:T(8,128)(2,1)}, u32[]{:S(2)}, u32[]{:S(2)}) async-start(bf16[4,4,32,4096]{3,2,1,0:T(8,128)(2,1)} %broadcast_in_dim.5), calls=%async_computation.1 | async-start | bytes 8388608 | tf_op jit(solution)/shard_map/all_to_all | solution.py:425
  57.3 205.7 %reduce-scatter.2.cloned.1.call-start = ((), (), s32[]{:S(2)}) async-start(), calls=%async_computation.6 | async-start | bytes 6881280 | tf_op jit(solution)/shard_map/reduce_scatter | solution.py:561
  57.3 46.5 %collective-permute-start.9 = (bf16[128,4096]{1,0:T(8,128)(2,1)S(1)}, bf16[128,4096]{1,0:T(8,128)(2,1)S(1)}, u32[]{:S(2)}, u32[]{:S(2)}) collective-permute-start(bf16[128,4096]{1,0:T(8,128)(2,1)S(1)} %pad_maximum_fusion.2.refs_3_.refs_6_), channel_id=1, source_target_pairs={{0,2},{2,16},{16,18},{18,0},{1,3},{3,17},{17,19},{19,1},{4,6},{6,2... | collective-permute-start | bytes 3145736 | tf_op jit(solution)/shard_map/ppermute | solution.py:19
  57.9 45.9 %collective-permute-start.5 = (bf16[128,4096]{1,0:T(8,128)(2,1)S(1)}, bf16[128,4096]{1,0:T(8,128)(2,1)S(1)}, u32[]{:S(2)}, u32[]{:S(2)}) collective-permute-start(bf16[128,4096]{1,0:T(8,128)(2,1)S(1)} %pad_maximum_fusion.2.refs_3_.refs_6_), channel_id=1, source_target_pairs={{0,18},{2,0},{16,2},{18,16},{1,19},{3,1},{17,3},{19,17},{4,22},{6,... | collective-permute-start | bytes 3145736 | tf_op jit(solution)/shard_map/ppermute | solution.py:19
  60.6 43.8 %collective-permute-start.7 = (bf16[128,4096]{1,0:T(8,128)(2,1)S(1)}, bf16[128,4096]{1,0:T(8,128)(2,1)}, u32[]{:S(2)}, u32[]{:S(2)}) collective-permute-start(bf16[128,4096]{1,0:T(8,128)(2,1)S(1)} %pad_maximum_fusion.2.refs_3_.refs_6_), channel_id=1, source_target_pairs={{0,16},{2,18},{16,0},{18,2},{1,17},{3,19},{17,1},{19,3},{4,20},{6,... | collective-permute-start | bytes 3145736 | tf_op jit(solution)/shard_map/ppermute | solution.py:19
  60.6 44.5 %collective-permute-start.4 = (bf16[128,4096]{1,0:T(8,128)(2,1)S(1)}, bf16[128,4096]{1,0:T(8,128)(2,1)}, u32[]{:S(2)}, u32[]{:S(2)}) collective-permute-start(bf16[128,4096]{1,0:T(8,128)(2,1)S(1)} %pad_maximum_fusion.2.refs_3_.refs_6_), channel_id=1, source_target_pairs={{0,1},{1,0},{2,3},{3,2},{4,5},{5,4},{6,7},{7,6},{8,9},{9,8},{10,11... | collective-permute-start | bytes 3145736 | tf_op jit(solution)/shard_map/ppermute | solution.py:23
  103.8 24.8 %copy-start.1 = (bf16[128,4096]{1,0:T(8,128)(2,1)}, bf16[128,4096]{1,0:T(8,128)(2,1)S(1)}, u32[]{:S(2)}) copy-start(bf16[128,4096]{1,0:T(8,128)(2,1)S(1)} %collective-permute-done.9.refs_6_.refs_9_) | copy-start | bytes 3145732
  103.8 2.8 collective-permute-start.10
  103.8 24.8 %copy-start.2 = (bf16[128,4096]{1,0:T(8,128)(2,1)}, bf16[128,4096]{1,0:T(8,128)(2,1)S(1)}, u32[]{:S(2)}) copy-start(bf16[128,4096]{1,0:T(8,128)(2,1)S(1)} %collective-permute-done.5.refs_4_.refs_7_) | copy-start | bytes 3145732
  103.8 5.8 %collective-permute-start.6 = (bf16[128,4096]{1,0:T(8,128)(2,1)S(1)}, bf16[128,4096]{1,0:T(8,128)(2,1)}, u32[]{:S(2)}, u32[]{:S(2)}) collective-permute-start(bf16[128,4096]{1,0:T(8,128)(2,1)S(1)} %collective-permute-done.5.refs_4_.refs_7_), channel_id=1, source_target_pairs={{0,1},{1,0},{2,3},{3,2},{4,5},{5,4},{6,7},{7,6},{8,9},{9,8},{10,11... | collective-permute-start | bytes 3145736 | tf_op jit(solution)/shard_map/ppermute | solution.py:23
  104.3 5.5 %collective-permute-start.8 = (bf16[128,4096]{1,0:T(8,128)(2,1)}, bf16[128,4096]{1,0:T(8,128)(2,1)}, u32[]{:S(2)}, u32[]{:S(2)}) collective-permute-start(bf16[128,4096]{1,0:T(8,128)(2,1)} %collective-permute-done.7.refs_5_.refs_8_), channel_id=1, source_target_pairs={{0,1},{1,0},{2,3},{3,2},{4,5},{5,4},{6,7},{7,6},{8,9},{9,8},{10,11... | collective-permute-start | bytes 3145736 | tf_op jit(solution)/shard_map/ppermute | solution.py:23
  109.8 33.5 %collective-permute-start.11 = (bf16[4,4,32,4096]{3,2,1,0:T(8,128)(2,1)}, bf16[4,4,32,4096]{3,2,1,0:T(8,128)(2,1)}, u32[]{:S(2)}, u32[]{:S(2)}) collective-permute-start(bf16[4,4,32,4096]{3,2,1,0:T(8,128)(2,1)} %all-to-all-done.1.refs_4_), channel_id=1, source_target_pairs={{0,1},{1,0},{2,3},{3,2},{4,5},{5,4},{6,7},{7,6},{8,9},{9,8},{10,11... | collective-permute-start | bytes 12582920 | tf_op jit(solution)/shard_map/ppermute | solution.py:23
  128.6 14.7 %collective-permute-start.12 = (bf16[16,32,4096]{2,1,0:T(8,128)(2,1)}, bf16[16,32,4096]{2,1,0:T(8,128)(2,1)S(1)}, u32[]{:S(2)}, u32[]{:S(2)}) collective-permute-start(bf16[16,32,4096]{2,1,0:T(8,128)(2,1)} %get-tuple-element.59), channel_id=1, source_target_pairs={{0,1},{1,0},{2,3},{3,2},{4,5},{5,4},{6,7},{7,6},{8,9},{9,8},{10,11... | collective-permute-start | bytes 12582920 | tf_op jit(solution)/shard_map/ppermute | solution.py:23
  147.2 49.2 %collective-permute-start.13 = (bf16[4,32,4096]{2,1,0:T(8,128)(2,1)}, bf16[4,32,4096]{2,1,0:T(8,128)(2,1)}, u32[]{:S(2)}, u32[]{:S(2)}) collective-permute-start(bf16[4,32,4096]{2,1,0:T(8,128)(2,1)} %get-tuple-element.66), channel_id=1, source_target_pairs={{0,2},{2,16},{16,18},{18,0},{1,3},{3,17},{17,19},{19,1},{4,6},{6,2... | collective-permute-start | bytes 3145736 | tf_op jit(solution)/shard_map/ppermute | solution.py:19
  147.2 49.2 %collective-permute-start.14 = (bf16[4,32,4096]{2,1,0:T(8,128)(2,1)S(1)}, bf16[4,32,4096]{2,1,0:T(8,128)(2,1)}, u32[]{:S(2)}, u32[]{:S(2)}) collective-permute-start(bf16[4,32,4096]{2,1,0:T(8,128)(2,1)S(1)} %get-tuple-element.67), channel_id=1, source_target_pairs={{0,18},{2,0},{16,2},{18,16},{1,19},{3,1},{17,3},{19,17},{4,22},{6,... | collective-permute-start | bytes 3145736 | tf_op jit(solution)/shard_map/ppermute | solution.py:19
  150.4 46.0 %collective-permute-start.15 = (bf16[4,32,4096]{2,1,0:T(8,128)(2,1)S(1)}, bf16[4,32,4096]{2,1,0:T(8,128)(2,1)}, u32[]{:S(2)}, u32[]{:S(2)}) collective-permute-start(bf16[4,32,4096]{2,1,0:T(8,128)(2,1)S(1)} %get-tuple-element.68), channel_id=1, source_target_pairs={{0,16},{2,18},{16,0},{18,2},{1,17},{3,19},{17,1},{19,3},{4,20},{6,... | collective-permute-start | bytes 3145736 | tf_op jit(solution)/shard_map/ppermute | solution.py:19
  198.9 1.2 copy-start.6
  199.0 9.0 %collective-permute-start.16 = (bf16[512,4096]{1,0:T(8,128)(2,1)}, bf16[512,4096]{1,0:T(8,128)(2,1)}, u32[]{:S(2)}, u32[]{:S(2)}) collective-permute-start(bf16[512,4096]{1,0:T(8,128)(2,1)} %get-tuple-element.71), channel_id=1, source_target_pairs={{0,1},{1,0},{2,3},{3,2},{4,5},{5,4},{6,7},{7,6},{8,9},{9,8},{10,11... | collective-permute-start | bytes 12582920 | tf_op jit(solution)/shard_map/ppermute | solution.py:23
  214.2 13.3 %collective-permute-start.20 = (bf16[32,4096]{1,0:T(8,128)(2,1)}, bf16[32,4096]{1,0:T(8,128)(2,1)S(1)}, u32[]{:S(2)}, u32[]{:S(2)}) collective-permute-start(bf16[32,4096]{1,0:T(8,128)(2,1)} %get-tuple-element.98), channel_id=1, source_target_pairs={{0,4},{4,8},{8,12},{12,0},{1,5},{5,9},{9,13},{13,1},{2,6},{6,10},{... | collective-permute-start | bytes 786440 | tf_op jit(solution)/shard_map/ppermute | solution.py:19
  215.5 13.0 %collective-permute-start.21 = (bf16[32,4096]{1,0:T(8,128)(2,1)}, bf16[32,4096]{1,0:T(8,128)(2,1)}, u32[]{:S(2)}, u32[]{:S(2)}) collective-permute-start(bf16[32,4096]{1,0:T(8,128)(2,1)} %get-tuple-element.100), channel_id=1, source_target_pairs={{0,12},{4,0},{8,4},{12,8},{1,13},{5,1},{9,5},{13,9},{2,14},{6,2},{... | collective-permute-start | bytes 786440 | tf_op jit(solution)/shard_map/ppermute | solution.py:19
  216.2 15.2 %collective-permute-start.22 = (bf16[32,4096]{1,0:T(8,128)(2,1)}, bf16[32,4096]{1,0:T(8,128)(2,1)}, u32[]{:S(2)}, u32[]{:S(2)}) collective-permute-start(bf16[32,4096]{1,0:T(8,128)(2,1)} %get-tuple-element.99), channel_id=1, source_target_pairs={{0,8},{4,12},{8,0},{12,4},{1,9},{5,13},{9,1},{13,5},{2,10},{6,14},... | collective-permute-start | bytes 786440 | tf_op jit(solution)/shard_map/ppermute | solution.py:19
  218.2 33.7 %all-to-all-start.2 = ((bf16[4,4,32,2048]{3,2,1,0:T(8,128)(2,1)}), bf16[4,4,32,2048]{3,2,1,0:T(8,128)(2,1)}, u32[]{:S(2)}, u32[]{:S(2)}) async-start(bf16[4,4,32,2048]{3,2,1,0:T(8,128)(2,1)} %bitcast.55), calls=%async_computation.2 | async-start | bytes 4194304 | tf_op jit(solution)/shard_map/all_to_all | solution.py:548
  224.1 15.7 %collective-permute-start.17 = (bf16[4,32,2048]{2,1,0:T(8,128)(2,1)S(1)}, bf16[4,32,2048]{2,1,0:T(8,128)(2,1)S(1)}, u32[]{:S(2)}, u32[]{:S(2)}) collective-permute-start(bf16[4,32,2048]{2,1,0:T(8,128)(2,1)S(1)} %get-tuple-element.87), channel_id=1, source_target_pairs={{0,2},{2,16},{16,18},{18,0},{1,3},{3,17},{17,19},{19,1},{4,6},{6,2... | collective-permute-start | bytes 1572872 | tf_op jit(solution)/shard_map/ppermute | solution.py:19
  224.6 23.4 %collective-permute-start.18 = (bf16[4,32,2048]{2,1,0:T(8,128)(2,1)S(1)}, bf16[4,32,2048]{2,1,0:T(8,128)(2,1)S(1)}, u32[]{:S(2)}, u32[]{:S(2)}) collective-permute-start(bf16[4,32,2048]{2,1,0:T(8,128)(2,1)S(1)} %get-tuple-element.89), channel_id=1, source_target_pairs={{0,18},{2,0},{16,2},{18,16},{1,19},{3,1},{17,3},{19,17},{4,22},{6,... | collective-permute-start | bytes 1572872 | tf_op jit(solution)/shard_map/ppermute | solution.py:19
  227.4 22.0 %collective-permute-start.19 = (bf16[4,32,2048]{2,1,0:T(8,128)(2,1)S(1)}, bf16[4,32,2048]{2,1,0:T(8,128)(2,1)S(1)}, u32[]{:S(2)}, u32[]{:S(2)}) collective-permute-start(bf16[4,32,2048]{2,1,0:T(8,128)(2,1)S(1)} %get-tuple-element.88), channel_id=1, source_target_pairs={{0,16},{2,18},{16,0},{18,2},{1,17},{3,19},{17,1},{19,3},{4,20},{6,... | collective-permute-start | bytes 1572872 | tf_op jit(solution)/shard_map/ppermute | solution.py:19
  254.6 12.6 %collective-permute-start.23 = (bf16[32,2048]{1,0:T(8,128)(2,1)}, bf16[32,2048]{1,0:T(8,128)(2,1)S(1)}, u32[]{:S(2)}, u32[]{:S(2)}) collective-permute-start(bf16[32,2048]{1,0:T(8,128)(2,1)} %get-tuple-element.101), channel_id=1, source_target_pairs={{0,2},{2,16},{16,18},{18,0},{1,3},{3,17},{17,19},{19,1},{4,6},{6,2... | collective-permute-start | bytes 393224 | tf_op jit(solution)/shard_map/ppermute | solution.py:19
  254.6 12.6 %collective-permute-start.24 = (bf16[32,2048]{1,0:T(8,128)(2,1)}, bf16[32,2048]{1,0:T(8,128)(2,1)S(1)}, u32[]{:S(2)}, u32[]{:S(2)}) collective-permute-start(bf16[32,2048]{1,0:T(8,128)(2,1)} %get-tuple-element.103), channel_id=1, source_target_pairs={{0,18},{2,0},{16,2},{18,16},{1,19},{3,1},{17,3},{19,17},{4,22},{6,... | collective-permute-start | bytes 393224 | tf_op jit(solution)/shard_map/ppermute | solution.py:19
  257.8 9.4 %collective-permute-start.25 = (bf16[32,2048]{1,0:T(8,128)(2,1)S(1)}, bf16[32,2048]{1,0:T(8,128)(2,1)}, u32[]{:S(2)}, u32[]{:S(2)}) collective-permute-start(bf16[32,2048]{1,0:T(8,128)(2,1)S(1)} %get-tuple-element.102), channel_id=1, source_target_pairs={{0,16},{2,18},{16,0},{18,2},{1,17},{3,19},{17,1},{19,3},{4,20},{6,... | collective-permute-start | bytes 393224 | tf_op jit(solution)/shard_map/ppermute | solution.py:19
  258.6 11.0 %all-to-all-start.3 = ((bf16[4,32,2048]{2,1,0:T(8,128)(2,1)}), bf16[4,32,2048]{2,1,0:T(8,128)(2,1)S(1)}, u32[]{:S(2)}, u32[]{:S(2)}) async-start(bf16[4,32,2048]{2,1,0:T(8,128)(2,1)} %fusion.2), calls=%async_computation.3 | async-start | bytes 1048576 | tf_op jit(solution)/shard_map/all_to_all | solution.py:548
  264.4 16.1 %collective-permute-start.26 = (bf16[7,6,64,128]{3,2,1,0:T(8,128)(2,1)S(1)}, bf16[7,6,64,128]{3,2,1,0:T(8,128)(2,1)S(1)}, u32[]{:S(2)}, u32[]{:S(2)}) collective-permute-start(bf16[7,6,64,128]{3,2,1,0:T(8,128)(2,1)S(1)} %bitcast.64), channel_id=1, source_target_pairs={{0,16},{16,0},{1,17},{17,1},{2,18},{18,2},{3,19},{19,3},{4,20},{20... | collective-permute-start | bytes 2064392 | tf_op jit(solution)/shard_map/ppermute | solution.py:23
Sparse Core Ops, SparseCore 0:
  49.9 55.9 all-gather.1
  199.1 56.1 reduce-scatter.1

commit v6 on v5

--- a/solution.py
+++ b/solution.py
@@ -30,13 +30,16 @@
     return [own, above, across, below]
 
 
+def scatter_parts(chunks, axis):
+    return chunks[0], shift(chunks[1], axis, 1), shift(chunks[3], axis, -1), shift(chunks[2], axis, 2)
+
+
+def total(parts):
+    return sum(part.astype(F32) for part in parts).astype(BF)
+
+
 def scatter_direct(chunks, axis):
-    from_below = shift(chunks[1], axis, 1)
-    from_above = shift(chunks[3], axis, -1)
-    from_across = shift(chunks[2], axis, 2)
-    total = chunks[0].astype(F32) + from_below.astype(F32)
-    total = total + from_above.astype(F32) + from_across.astype(F32)
-    return total.astype(BF)
+    return total(scatter_parts(chunks, axis))
 
 
 def add(first, second):
@@ -164,7 +167,7 @@
     lax.fori_loop(0, 2 * RING * where.pairs, put, 0)
 
 
-def back_rows(left, w_ref, out_ref, i):
+def back_rows(left, w_ref, out_ref):
     width = w_ref.shape[0]
     step = min(width, 1024)
     per = out_ref.shape[1]
@@ -176,7 +179,7 @@
         for a in range(RING // 2):
             for b in range(RING):
                 at = (a * RING + b) * per
-                chunk = (i * (RING // 2) + a) * RING + b
+                chunk = a * RING + b
                 out_ref[chunk, :, start : start + step] = part[at : at + per]
 
 
@@ -186,27 +189,26 @@
     mask = left_half((rows, 2 * BLK))
     per = m_ref.shape[3]
     spans = [(a, b, (a * RING + b) * per) for a in range(RING // 2) for b in range(RING)]
-    previous = None
-    for p in range(half_panels):
-        lanes = slice(p * 2 * BLK, (p + 1) * 2 * BLK)
-        here = both[:, lanes]
-        turned = flip(here)
-        gate = jnp.where(mask, here, turned)
-        up = jnp.where(mask, turned, here)
+    for first in range(0, half_panels, 2):
+        group = [slice(p * 2 * BLK, (p + 1) * 2 * BLK) for p in range(first, min(first + 2, half_panels))]
+        low, high = both[:, group[0]], both[:, group[-1]]
+        gate = jnp.where(mask, low, flip(high))
+        up = jnp.where(mask, flip(low), high)
         sigma = jax.nn.sigmoid(gate)
         silu = gate * sigma
-        mult = jnp.where(mask, up * sigma * (1.0 + gate * (1.0 - sigma)), silu)
+        slope = up * sigma * (1.0 + gate * (1.0 - sigma))
+        mults = [jnp.where(mask, slope, flip(silu)), jnp.where(mask, flip(slope), silu)]
+        for lanes, mult in zip(group, mults):
+            for a, b, at in spans:
+                m_ref[0, a, b, :, lanes] = mult[at : at + per]
+        hidden = silu * up
+        if len(group) == 1:
+            hidden = jnp.where(mask, hidden, 0.0)
+        hidden = hidden.astype(BF)
+        out = slice(first * BLK, (first + 2) * BLK)
+        h_ref[:, out] = hidden
         for a, b, at in spans:
-            m_ref[0, a, b, :, lanes] = mult[at : at + per]
-        hidden = silu * up
-        if p % 2 == 0:
-            previous = hidden
-        if p % 2 == 1 or p == half_panels - 1:
-            merged = jnp.where(mask, previous, hidden if p % 2 == 1 else 0.0).astype(BF)
-            out = slice((p // 2) * 128, (p // 2 + 1) * 128)
-            h_ref[:, out] = merged
-            for a, b, at in spans:
-                h2_ref[0, b, a, :, out] = merged[at : at + per]
+            h2_ref[0, b, a, :, out] = hidden[at : at + per]
 
 
 def forward_kernel(half_panels, kept_here, first, place, *refs):
@@ -253,7 +255,7 @@
         def _():
             w_copies[1].wait()
 
-    back_rows(h_ref[...], wd_ref, y_ref, i)
+    back_rows(h_ref[...], wd_ref, y_ref)
     if first:
 
         @pl.when(i == pl.num_programs(0) - 1)
@@ -466,7 +468,7 @@
             out_specs=[
                 pl.BlockSpec((1, pair, RING, per, two), lambda i: (core, i, 0, 0, 0)),
                 pl.BlockSpec((1, RING, pair, per, hid), lambda i: (core, 0, i, 0, 0)),
-                out_full(*chunks),
+                pl.BlockSpec((pair * RING, per, width), lambda i: (i, 0, 0)),
             ] + [hbm] * len(extra_out),
             out_shape=[shape(ordered(two), F32), shape(ordered(hid), BF), shape(chunks, BF)] + extra_out,
             scratch_shapes=[

time: 293 us -> 291 us (level)
  no operation moved by 1% of the time
where the time goes in v6:
time: 291 us
  waiting for transfers between devices  106 us (36%)
  Pallas kernels  71.2 us (24%)
  starting transfers between devices  52 us (18%)
  other arithmetic  21 us (7%)
  local copies, waits for them, and re-layouts  18.7 us (6%)
  between operations  14.3 us (5%)
  matrix products  7.83 us (3%)
    ppermute x18, waiting for transfers between devices, shift(): lax.ppermute(value, axis, [(i, (i + step) % RING) for i in range(RING)])  68.2 us
    pallas_call x1, Pallas kernels, per_device(): pl.pallas_call(part(gradient_kernel, half, kept_here), grid=(steps,), in_...  40 us
    ppermute x9, waiting for transfers between devices, swap(): return lax.ppermute(value, axis, [(0, 1), (1, 0)])  34.7 us
    pallas_call x2, Pallas kernels, forward(): pl.pallas_call(part(forward_kernel, half, kept_here, first), grid=(2,), i...  31.2 us
    ppermute x18, starting transfers between devices, shift(): lax.ppermute(value, axis, [(i, (i + step) % RING) for i in range(RING)])  23.7 us
    all_to_all x2, starting transfers between devices, gather_all(): return lax.all_to_all(wide, axis, 0, 0, tiled=True)  10.5 us
    all_to_all x2, starting transfers between devices, over_x(): lax.all_to_all(value, 'x', 0, 0, tiled=True).astype(F32)  10.2 us
    dot_general x1, matrix products, project(): lax.dot_general(left, w_gu, (((1,), (1,)), ((), ())), preferred_element_t...  7.83 us
  transfers between devices with their start and end apart: 33, of which 13 were waited for; matrix products, arithmetic and copies ran while one was open for 12% of the time, Pallas kernels for 25%

profile of v6, /device:TPU:26, one launch (start us, length us, event | category | flops | bytes accessed | tf_op | source)
XLA Modules:
  0.0 290.8 jit_solution(9165086693042947908)
XLA Ops:
  7.2 0.6 collective-permute-start.1
  7.8 2.4 collective-permute-start.2
  10.2 1.8 collective-permute-start.3
  12.0 2.0 broadcast_in_dim.4
  14.0 5.4 %all-to-all-start = ((bf16[4,32,4096]{2,1,0:T(8,128)(2,1)}), bf16[4,32,4096]{2,1,0:T(8,128)(2,1)S(1)}, u32[]{:S(2)}, u32[]{:S(2)}) async-start(bf16[4,32,4096]{2,1,0:T(8,128)(2,1)} %broadcast_in_dim.4), calls=%async_computation | async-start | bytes 2097152 | tf_op jit(solution)/shard_map/all_to_all | solution.py:427
  19.5 0.7 reshape.67
  20.5 0.7 reshape.65
  21.2 1.9 reshape.66
  23.2 0.5 pad_maximum_fusion
  23.8 3.6 %collective-permute-start = (bf16[7,6,64,128]{3,2,1,0:T(8,128)(2,1)S(1)}, bf16[7,6,64,128]{3,2,1,0:T(8,128)(2,1)S(1)}, u32[]{:S(2)}, u32[]{:S(2)}) collective-permute-start(bf16[7,6,64,128]{3,2,1,0:T(8,128)(2,1)S(1)} %get-tuple-element.97), channel_id=1, source_target_pairs={{0,16},{16,0},{1,17},{17,1},{2,18},{18,2},{3,19},{19,3},{4,20},{20... | collective-permute-start | bytes 2064392 | tf_op jit(solution)/shard_map/ppermute | solution.py:23
  27.5 1.2 pad_maximum_fusion.2.refs_3_.refs_6_
  28.7 19.8 %collective-permute-done = bf16[7,6,64,128]{3,2,1,0:T(8,128)(2,1)S(1)} collective-permute-done((bf16[7,6,64,128]{3,2,1,0:T(8,128)(2,1)S(1)}, bf16[7,6,64,128]{3,2,1,0:T(8,128)(2,1)S(1)}, u32[]{:S(2)}, u32[]{:S(2)}) %collective-permute-start) | collective-permute-done | bytes 688160 | tf_op jit(solution)/shard_map/ppermute | solution.py:23
  48.5 1.2 pad_maximum_fusion.1
  49.7 2.6 broadcast_in_dim.5
  52.3 5.0 %all-to-all-start.1 = ((bf16[4,4,32,4096]{3,2,1,0:T(8,128)(2,1)}), bf16[4,4,32,4096]{3,2,1,0:T(8,128)(2,1)}, u32[]{:S(2)}, u32[]{:S(2)}) async-start(bf16[4,4,32,4096]{3,2,1,0:T(8,128)(2,1)} %broadcast_in_dim.5), calls=%async_computation.1 | async-start | bytes 8388608 | tf_op jit(solution)/shard_map/all_to_all | solution.py:427
  57.3 0.6 collective-permute-start.9
  57.9 2.7 collective-permute-start.5
  60.6 43.2 %collective-permute-done.9.refs_6_.refs_9_ = bf16[128,4096]{1,0:T(8,128)(2,1)S(1)} collective-permute-done((bf16[128,4096]{1,0:T(8,128)(2,1)S(1)}, bf16[128,4096]{1,0:T(8,128)(2,1)S(1)}, u32[]{:S(2)}, u32[]{:S(2)}) %collective-permute-start.9) | collective-permute-done | bytes 1048608 | tf_op jit(solution)/shard_map/ppermute | solution.py:19
  103.8 0.5 collective-permute-start.6
  104.4 0.6 pad_add_fusion.refs_0_
  105.0 1.6 collective-permute-done.10.refs_8_.refs_13_
  106.6 3.0 %collective-permute-done.6.refs_6_.refs_11_ = bf16[128,4096]{1,0:T(8,128)(2,1)} collective-permute-done((bf16[128,4096]{1,0:T(8,128)(2,1)S(1)}, bf16[128,4096]{1,0:T(8,128)(2,1)}, u32[]{:S(2)}, u32[]{:S(2)}) %collective-permute-start.6) | collective-permute-done | bytes 1048608 | tf_op jit(solution)/shard_map/ppermute | solution.py:23
  110.0 17.8 %forward_away.1 = (f32[2,4,4,32,896]{4,3,2,1,0:T(8,128)}, bf16[2,4,4,32,512]{4,3,2,1,0:T(8,128)(2,1)}, bf16[16,32,4096]{2,1,0:T(8,128)(2,1)}, bf16[4096,896]{1,0:T(8,128)(2,1)}, bf16[4096,512]{1,0:T(8,128)(2,1)}) custom-call(s32[3]{0:T(128)} %pad_add_fusion.refs_0_, s32[14,32]{1,0:T(8,128)} %refs_1_.3, s32[14,32]{1,0:T(8,128)} %refs_2_.3, s32[14,32]{1,0:T(8,128)} %refs_3_.3, ...), custom_call_target="tpu_custom_call" | custom-call | flops 738197504 | bytes 3145728 | tf_op jit(solution)/shard_map/forward_away/pallas_call | solution.py:464
  127.8 0.5 collective-permute-start.12
  128.2 13.4 %forward_kept.1 = (f32[2,4,4,32,896]{4,3,2,1,0:T(8,128)}, bf16[2,4,4,32,512]{4,3,2,1,0:T(8,128)(2,1)}, bf16[16,32,4096]{2,1,0:T(8,128)(2,1)}) custom-call(s32[3]{0:T(128)} %pad_add_fusion.refs_0_, bf16[4096,896]{1,0:T(8,128)(2,1)} %get-tuple-element.51.refs_1_.refs_17_, ...), custom_call_target="tpu_custom_call", output_to_operand_aliasing={{0}: (7, {}), {1}: (8, {})} | custom-call | flops 738197504 | bytes 3145728 | tf_op jit(solution)/shard_map/forward_kept/pallas_call | solution.py:464
  141.7 3.9 %add_convert_fusion.3 = (bf16[4,32,4096]{2,1,0:T(8,128)(2,1)S(1)}, bf16[4,32,4096]{2,1,0:T(8,128)(2,1)S(1)}, bf16[4,32,4096]{2,1,0:T(8,128)(2,1)}, bf16[4,32,4096]{2,1,0:T(8,128)(2,1)S(1)}) fusion(bf16[16,32,4096]{2,1,0:T(8,128)(2,1)S(1)} %collective-permute-done.12, bf16[16,32,4096]{2,1,0:T(8,128)(2,1)} %get-tuple-element.58), kind=kLoop, calls=%fused_computation.5 | loop fusion | flops 8388608 | bytes 12582912 | tf_op jit(solution)/shard_map/convert_element_type | solution.py:46
  145.6 3.2 %collective-permute-start.14 = (bf16[4,32,4096]{2,1,0:T(8,128)(2,1)S(1)}, bf16[4,32,4096]{2,1,0:T(8,128)(2,1)}, u32[]{:S(2)}, u32[]{:S(2)}) collective-permute-start(bf16[4,32,4096]{2,1,0:T(8,128)(2,1)S(1)} %get-tuple-element.67), channel_id=1, source_target_pairs={{0,18},{2,0},{16,2},{18,16},{1,19},{3,1},{17,3},{19,17},{4,22},{6,... | collective-permute-start | bytes 3145736 | tf_op jit(solution)/shard_map/ppermute | solution.py:19
  148.8 40.0 %gradients.1 = (bf16[512,896]{1,0:T(8,128)(2,1)}, bf16[512,4096]{1,0:T(8,128)(2,1)}, bf16[336,64,128]{2,1,0:T(8,128)(2,1)}) custom-call(s32[3]{0:T(128)} %pad_add_fusion.refs_0_, s32[14,32]{1,0:T(8,128)} %refs_1_.3, s32[14,32]{1,0:T(8,128)} %refs_2_.3, s32[14,32]{1,0:T(8,128)} %refs_3_.3, bf16[4,4,32,4096]{3,2,1,0:T(8,128)(2,1)} %all-to-all-done.1.refs_4_, ...), custom_call_target="tpu_custom_call" | custom-call | flops 2013265920 | bytes 5242880 | tf_op jit(solution)/shard_map/gradients/pallas_call | solution.py:501
  188.9 5.9 %collective-permute-done.13 = bf16[4,32,4096]{2,1,0:T(8,128)(2,1)} collective-permute-done((bf16[4,32,4096]{2,1,0:T(8,128)(2,1)}, bf16[4,32,4096]{2,1,0:T(8,128)(2,1)}, u32[]{:S(2)}, u32[]{:S(2)}) %collective-permute-start.13) | collective-permute-done | bytes 1048608 | tf_op jit(solution)/shard_map/ppermute | solution.py:19
  194.8 2.5 add_convert_fusion.2
  197.4 1.0 copy-done.6
  198.5 7.8 %convolution_convert_fusion = bf16[512,4096]{1,0:T(8,128)(2,1)S(1)} fusion(bf16[512,896]{1,0:T(8,128)(2,1)S(1)} %copy-done.6, bf16[4096,896]{1,0:T(8,128)(2,1)} %get-tuple-element.51.refs_1_.refs_17_), kind=kOutput, calls=%fused_computation | convolution fusion | flops 3760193536 | bytes 12451840 | tf_op jit(solution)/shard_map/dot_general | solution.py:539
  206.3 3.7 %add_convert_fusion = (bf16[512,2048]{1,0:T(8,128)(2,1)S(1)}, bf16[512,2048]{1,0:T(8,128)(2,1)S(1)}) fusion(bf16[512,4096]{1,0:T(8,128)(2,1)} %collective-permute-done.16, bf16[512,4096]{1,0:T(8,128)(2,1)S(1)} %convolution_convert_fusion), kind=kLoop, calls=%fused_computation.1 | loop fusion | flops 8388608 | bytes 12582912 | tf_op jit(solution)/shard_map/convert_element_type | solution.py:46
  210.1 1.6 copy.23
  211.7 0.9 slice_bitcast_fusion.5
  212.5 1.4 collective-permute-start.20
  213.9 0.7 collective-permute-start.21
  214.6 2.0 collective-permute-start.22
  216.5 5.9 %all-to-all-start.2 = ((bf16[4,4,32,2048]{3,2,1,0:T(8,128)(2,1)}), bf16[4,4,32,2048]{3,2,1,0:T(8,128)(2,1)}, u32[]{:S(2)}, u32[]{:S(2)}) async-start(bf16[4,4,32,2048]{3,2,1,0:T(8,128)(2,1)} %bitcast.55), calls=%async_computation.2 | async-start | bytes 4194304 | tf_op jit(solution)/shard_map/all_to_all | solution.py:550
  222.5 0.4 collective-permute-start.17
  222.9 2.9 collective-permute-start.18
  225.8 1.1 collective-permute-start.19
  226.9 2.9 collective-permute-done.22
  229.7 1.9 fusion.7
  231.6 6.6 %collective-permute-done.17 = bf16[4,32,2048]{2,1,0:T(8,128)(2,1)S(1)} collective-permute-done((bf16[4,32,2048]{2,1,0:T(8,128)(2,1)S(1)}, bf16[4,32,2048]{2,1,0:T(8,128)(2,1)S(1)}, u32[]{:S(2)}, u32[]{:S(2)}) %collective-permute-start.17) | collective-permute-done | bytes 524320 | tf_op jit(solution)/shard_map/ppermute | solution.py:19
  238.2 8.1 %collective-permute-done.18 = bf16[4,32,2048]{2,1,0:T(8,128)(2,1)S(1)} collective-permute-done((bf16[4,32,2048]{2,1,0:T(8,128)(2,1)S(1)}, bf16[4,32,2048]{2,1,0:T(8,128)(2,1)S(1)}, u32[]{:S(2)}, u32[]{:S(2)}) %collective-permute-start.18) | collective-permute-done | bytes 524320 | tf_op jit(solution)/shard_map/ppermute | solution.py:19
  246.3 1.5 collective-permute-done.19
  247.8 1.1 fusion.2
  249.0 1.3 all-to-all-done.2
  250.2 2.0 reduce_sum.24
  252.3 0.7 slice_bitcast_fusion.8
  253.0 3.2 %collective-permute-start.24 = (bf16[32,2048]{1,0:T(8,128)(2,1)}, bf16[32,2048]{1,0:T(8,128)(2,1)S(1)}, u32[]{:S(2)}, u32[]{:S(2)}) collective-permute-start(bf16[32,2048]{1,0:T(8,128)(2,1)} %get-tuple-element.103), channel_id=1, source_target_pairs={{0,18},{2,0},{16,2},{18,16},{1,19},{3,1},{17,3},{19,17},{4,22},{6,... | collective-permute-start | bytes 393224 | tf_op jit(solution)/shard_map/ppermute | solution.py:19
  256.2 0.8 collective-permute-start.25
  257.0 4.4 %all-to-all-start.3 = ((bf16[4,32,2048]{2,1,0:T(8,128)(2,1)}), bf16[4,32,2048]{2,1,0:T(8,128)(2,1)S(1)}, u32[]{:S(2)}, u32[]{:S(2)}) async-start(bf16[4,32,2048]{2,1,0:T(8,128)(2,1)} %fusion.2), calls=%async_computation.3 | async-start | bytes 1048576 | tf_op jit(solution)/shard_map/all_to_all | solution.py:550
  261.4 1.4 fusion.11
  262.8 2.8 collective-permute-start.26
  265.6 1.0 fusion.10
  266.5 1.5 all-to-all-done.3
  268.1 0.7 pad_maximum_fusion.4
  268.8 10.1 %collective-permute-done.26 = bf16[7,6,64,128]{3,2,1,0:T(8,128)(2,1)S(1)} collective-permute-done((bf16[7,6,64,128]{3,2,1,0:T(8,128)(2,1)S(1)}, bf16[7,6,64,128]{3,2,1,0:T(8,128)(2,1)S(1)}, u32[]{:S(2)}, u32[]{:S(2)}) %collective-permute-start.26) | collective-permute-done | bytes 688160 | tf_op jit(solution)/shard_map/ppermute | solution.py:23
  279.4 0.4 copy.21
  279.8 1.4 reshape.74
  281.2 1.4 reshape.71
  282.6 1.4 reshape.72
  (54 shorter events, 1.8 us)
Async XLA Ops:
  7.2 12.3 %copy-start.3 = (bf16[14,4,4096]{2,1,0:T(4,128)(2,1)S(1)}, bf16[14,4,4096]{2,1,0:T(4,128)(2,1)}, u32[]{:S(2)}) copy-start(bf16[14,4,4096]{2,1,0:T(4,128)(2,1)} %param.14) | copy-start | bytes 1376260
  7.2 20.3 %collective-permute-start.1 = (bf16[32,4096]{1,0:T(8,128)(2,1)}, bf16[32,4096]{1,0:T(8,128)(2,1)}, u32[]{:S(2)}, u32[]{:S(2)}) collective-permute-start(bf16[32,4096]{1,0:T(8,128)(2,1)} %param.8), channel_id=1, source_target_pairs={{0,12},{4,0},{8,4},{12,8},{1,13},{5,1},{9,5},{13,9},{2,14},{6,2},{... | collective-permute-start | bytes 786440 | tf_op jit(solution)/shard_map/ppermute | solution.py:19
  7.8 19.7 %collective-permute-start.2 = (bf16[32,4096]{1,0:T(8,128)(2,1)}, bf16[32,4096]{1,0:T(8,128)(2,1)}, u32[]{:S(2)}, u32[]{:S(2)}) collective-permute-start(bf16[32,4096]{1,0:T(8,128)(2,1)} %param.8), channel_id=1, source_target_pairs={{0,8},{4,12},{8,0},{12,4},{1,9},{5,13},{9,1},{13,5},{2,10},{6,14},... | collective-permute-start | bytes 786440 | tf_op jit(solution)/shard_map/ppermute | solution.py:19
  10.2 17.3 %collective-permute-start.3 = (bf16[32,4096]{1,0:T(8,128)(2,1)}, bf16[32,4096]{1,0:T(8,128)(2,1)}, u32[]{:S(2)}, u32[]{:S(2)}) collective-permute-start(bf16[32,4096]{1,0:T(8,128)(2,1)} %param.8), channel_id=1, source_target_pairs={{0,4},{4,8},{8,12},{12,0},{1,5},{5,9},{9,13},{13,1},{2,6},{6,10},{... | collective-permute-start | bytes 786440 | tf_op jit(solution)/shard_map/ppermute | solution.py:19
  14.0 6.5 %copy-start.4 = (bf16[14,4,4096]{2,1,0:T(4,128)(2,1)S(1)}, bf16[14,4,4096]{2,1,0:T(4,128)(2,1)}, u32[]{:S(2)}) copy-start(bf16[14,4,4096]{2,1,0:T(4,128)(2,1)} %param.10) | copy-start | bytes 1376260
  14.0 34.4 %all-to-all-start = ((bf16[4,32,4096]{2,1,0:T(8,128)(2,1)}), bf16[4,32,4096]{2,1,0:T(8,128)(2,1)S(1)}, u32[]{:S(2)}, u32[]{:S(2)}) async-start(bf16[4,32,4096]{2,1,0:T(8,128)(2,1)} %broadcast_in_dim.4), calls=%async_computation | async-start | bytes 2097152 | tf_op jit(solution)/shard_map/all_to_all | solution.py:427
  19.5 90.5 %all-gather.2.cloned.1.call-start = ((), (), s32[]{:S(2)}) async-start(), calls=%async_computation.5 | async-start | bytes 6881280 | tf_op jit(solution)/shard_map/all_gather | solution.py:433
  23.7 3.8 %copy-start.5 = (bf16[32,4096]{1,0:T(8,128)(2,1)S(1)}, bf16[32,4096]{1,0:T(8,128)(2,1)}, u32[]{:S(2)}) copy-start(bf16[32,4096]{1,0:T(8,128)(2,1)} %param.8) | copy-start | bytes 786436
  23.8 24.6 %collective-permute-start = (bf16[7,6,64,128]{3,2,1,0:T(8,128)(2,1)S(1)}, bf16[7,6,64,128]{3,2,1,0:T(8,128)(2,1)S(1)}, u32[]{:S(2)}, u32[]{:S(2)}) collective-permute-start(bf16[7,6,64,128]{3,2,1,0:T(8,128)(2,1)S(1)} %get-tuple-element.97), channel_id=1, source_target_pairs={{0,16},{16,0},{1,17},{17,1},{2,18},{18,2},{3,19},{19,3},{4,20},{20... | collective-permute-start | bytes 2064392 | tf_op jit(solution)/shard_map/ppermute | solution.py:23
  28.7 31.9 %copy-start = (bf16[128,4096]{1,0:T(8,128)(2,1)}, bf16[128,4096]{1,0:T(8,128)(2,1)S(1)}, u32[]{:S(2)}) copy-start(bf16[128,4096]{1,0:T(8,128)(2,1)S(1)} %pad_maximum_fusion.2.refs_3_.refs_6_) | copy-start | bytes 3145732
  52.3 57.5 %all-to-all-start.1 = ((bf16[4,4,32,4096]{3,2,1,0:T(8,128)(2,1)}), bf16[4,4,32,4096]{3,2,1,0:T(8,128)(2,1)}, u32[]{:S(2)}, u32[]{:S(2)}) async-start(bf16[4,4,32,4096]{3,2,1,0:T(8,128)(2,1)} %broadcast_in_dim.5), calls=%async_computation.1 | async-start | bytes 8388608 | tf_op jit(solution)/shard_map/all_to_all | solution.py:427
  57.3 204.1 %reduce-scatter.2.cloned.1.call-start = ((), (), s32[]{:S(2)}) async-start(), calls=%async_computation.6 | async-start | bytes 6881280 | tf_op jit(solution)/shard_map/reduce_scatter | solution.py:563
  57.3 46.5 %collective-permute-start.9 = (bf16[128,4096]{1,0:T(8,128)(2,1)S(1)}, bf16[128,4096]{1,0:T(8,128)(2,1)S(1)}, u32[]{:S(2)}, u32[]{:S(2)}) collective-permute-start(bf16[128,4096]{1,0:T(8,128)(2,1)S(1)} %pad_maximum_fusion.2.refs_3_.refs_6_), channel_id=1, source_target_pairs={{0,2},{2,16},{16,18},{18,0},{1,3},{3,17},{17,19},{19,1},{4,6},{6,2... | collective-permute-start | bytes 3145736 | tf_op jit(solution)/shard_map/ppermute | solution.py:19
  57.9 45.9 %collective-permute-start.5 = (bf16[128,4096]{1,0:T(8,128)(2,1)S(1)}, bf16[128,4096]{1,0:T(8,128)(2,1)S(1)}, u32[]{:S(2)}, u32[]{:S(2)}) collective-permute-start(bf16[128,4096]{1,0:T(8,128)(2,1)S(1)} %pad_maximum_fusion.2.refs_3_.refs_6_), channel_id=1, source_target_pairs={{0,18},{2,0},{16,2},{18,16},{1,19},{3,1},{17,3},{19,17},{4,22},{6,... | collective-permute-start | bytes 3145736 | tf_op jit(solution)/shard_map/ppermute | solution.py:19
  60.6 43.8 %collective-permute-start.7 = (bf16[128,4096]{1,0:T(8,128)(2,1)S(1)}, bf16[128,4096]{1,0:T(8,128)(2,1)}, u32[]{:S(2)}, u32[]{:S(2)}) collective-permute-start(bf16[128,4096]{1,0:T(8,128)(2,1)S(1)} %pad_maximum_fusion.2.refs_3_.refs_6_), channel_id=1, source_target_pairs={{0,16},{2,18},{16,0},{18,2},{1,17},{3,19},{17,1},{19,3},{4,20},{6,... | collective-permute-start | bytes 3145736 | tf_op jit(solution)/shard_map/ppermute | solution.py:19
  60.6 44.5 %collective-permute-start.4 = (bf16[128,4096]{1,0:T(8,128)(2,1)S(1)}, bf16[128,4096]{1,0:T(8,128)(2,1)}, u32[]{:S(2)}, u32[]{:S(2)}) collective-permute-start(bf16[128,4096]{1,0:T(8,128)(2,1)S(1)} %pad_maximum_fusion.2.refs_3_.refs_6_), channel_id=1, source_target_pairs={{0,1},{1,0},{2,3},{3,2},{4,5},{5,4},{6,7},{7,6},{8,9},{9,8},{10,11... | collective-permute-start | bytes 3145736 | tf_op jit(solution)/shard_map/ppermute | solution.py:23
  103.8 23.9 %copy-start.1 = (bf16[128,4096]{1,0:T(8,128)(2,1)}, bf16[128,4096]{1,0:T(8,128)(2,1)S(1)}, u32[]{:S(2)}) copy-start(bf16[128,4096]{1,0:T(8,128)(2,1)S(1)} %collective-permute-done.9.refs_6_.refs_9_) | copy-start | bytes 3145732
  103.8 2.8 collective-permute-start.10
  103.8 23.9 %copy-start.2 = (bf16[128,4096]{1,0:T(8,128)(2,1)}, bf16[128,4096]{1,0:T(8,128)(2,1)S(1)}, u32[]{:S(2)}) copy-start(bf16[128,4096]{1,0:T(8,128)(2,1)S(1)} %collective-permute-done.5.refs_4_.refs_7_) | copy-start | bytes 3145732
  103.8 5.8 %collective-permute-start.6 = (bf16[128,4096]{1,0:T(8,128)(2,1)S(1)}, bf16[128,4096]{1,0:T(8,128)(2,1)}, u32[]{:S(2)}, u32[]{:S(2)}) collective-permute-start(bf16[128,4096]{1,0:T(8,128)(2,1)S(1)} %collective-permute-done.5.refs_4_.refs_7_), channel_id=1, source_target_pairs={{0,1},{1,0},{2,3},{3,2},{4,5},{5,4},{6,7},{7,6},{8,9},{9,8},{10,11... | collective-permute-start | bytes 3145736 | tf_op jit(solution)/shard_map/ppermute | solution.py:23
  104.3 5.5 %collective-permute-start.8 = (bf16[128,4096]{1,0:T(8,128)(2,1)}, bf16[128,4096]{1,0:T(8,128)(2,1)}, u32[]{:S(2)}, u32[]{:S(2)}) collective-permute-start(bf16[128,4096]{1,0:T(8,128)(2,1)} %collective-permute-done.7.refs_5_.refs_8_), channel_id=1, source_target_pairs={{0,1},{1,0},{2,3},{3,2},{4,5},{5,4},{6,7},{7,6},{8,9},{9,8},{10,11... | collective-permute-start | bytes 3145736 | tf_op jit(solution)/shard_map/ppermute | solution.py:23
  109.8 31.8 %collective-permute-start.11 = (bf16[4,4,32,4096]{3,2,1,0:T(8,128)(2,1)}, bf16[4,4,32,4096]{3,2,1,0:T(8,128)(2,1)}, u32[]{:S(2)}, u32[]{:S(2)}) collective-permute-start(bf16[4,4,32,4096]{3,2,1,0:T(8,128)(2,1)} %all-to-all-done.1.refs_4_), channel_id=1, source_target_pairs={{0,1},{1,0},{2,3},{3,2},{4,5},{5,4},{6,7},{7,6},{8,9},{9,8},{10,11... | collective-permute-start | bytes 12582920 | tf_op jit(solution)/shard_map/ppermute | solution.py:23
  127.8 13.9 %collective-permute-start.12 = (bf16[16,32,4096]{2,1,0:T(8,128)(2,1)}, bf16[16,32,4096]{2,1,0:T(8,128)(2,1)S(1)}, u32[]{:S(2)}, u32[]{:S(2)}) collective-permute-start(bf16[16,32,4096]{2,1,0:T(8,128)(2,1)} %get-tuple-element.59), channel_id=1, source_target_pairs={{0,1},{1,0},{2,3},{3,2},{4,5},{5,4},{6,7},{7,6},{8,9},{9,8},{10,11... | collective-permute-start | bytes 12582920 | tf_op jit(solution)/shard_map/ppermute | solution.py:23
  145.6 49.2 %collective-permute-start.13 = (bf16[4,32,4096]{2,1,0:T(8,128)(2,1)}, bf16[4,32,4096]{2,1,0:T(8,128)(2,1)}, u32[]{:S(2)}, u32[]{:S(2)}) collective-permute-start(bf16[4,32,4096]{2,1,0:T(8,128)(2,1)} %get-tuple-element.66), channel_id=1, source_target_pairs={{0,2},{2,16},{16,18},{18,0},{1,3},{3,17},{17,19},{19,1},{4,6},{6,2... | collective-permute-start | bytes 3145736 | tf_op jit(solution)/shard_map/ppermute | solution.py:19
  145.6 49.2 %collective-permute-start.14 = (bf16[4,32,4096]{2,1,0:T(8,128)(2,1)S(1)}, bf16[4,32,4096]{2,1,0:T(8,128)(2,1)}, u32[]{:S(2)}, u32[]{:S(2)}) collective-permute-start(bf16[4,32,4096]{2,1,0:T(8,128)(2,1)S(1)} %get-tuple-element.67), channel_id=1, source_target_pairs={{0,18},{2,0},{16,2},{18,16},{1,19},{3,1},{17,3},{19,17},{4,22},{6,... | collective-permute-start | bytes 3145736 | tf_op jit(solution)/shard_map/ppermute | solution.py:19
  148.8 46.0 %collective-permute-start.15 = (bf16[4,32,4096]{2,1,0:T(8,128)(2,1)S(1)}, bf16[4,32,4096]{2,1,0:T(8,128)(2,1)}, u32[]{:S(2)}, u32[]{:S(2)}) collective-permute-start(bf16[4,32,4096]{2,1,0:T(8,128)(2,1)S(1)} %get-tuple-element.68), channel_id=1, source_target_pairs={{0,16},{2,18},{16,0},{18,2},{1,17},{3,19},{17,1},{19,3},{4,20},{6,... | collective-permute-start | bytes 3145736 | tf_op jit(solution)/shard_map/ppermute | solution.py:19
  197.3 1.2 copy-start.6
  197.3 9.0 %collective-permute-start.16 = (bf16[512,4096]{1,0:T(8,128)(2,1)}, bf16[512,4096]{1,0:T(8,128)(2,1)}, u32[]{:S(2)}, u32[]{:S(2)}) collective-permute-start(bf16[512,4096]{1,0:T(8,128)(2,1)} %get-tuple-element.71), channel_id=1, source_target_pairs={{0,1},{1,0},{2,3},{3,2},{4,5},{5,4},{6,7},{7,6},{8,9},{9,8},{10,11... | collective-permute-start | bytes 12582920 | tf_op jit(solution)/shard_map/ppermute | solution.py:23
  212.5 13.3 %collective-permute-start.20 = (bf16[32,4096]{1,0:T(8,128)(2,1)}, bf16[32,4096]{1,0:T(8,128)(2,1)S(1)}, u32[]{:S(2)}, u32[]{:S(2)}) collective-permute-start(bf16[32,4096]{1,0:T(8,128)(2,1)} %get-tuple-element.98), channel_id=1, source_target_pairs={{0,4},{4,8},{8,12},{12,0},{1,5},{5,9},{9,13},{13,1},{2,6},{6,10},{... | collective-permute-start | bytes 786440 | tf_op jit(solution)/shard_map/ppermute | solution.py:19
  213.9 13.0 %collective-permute-start.21 = (bf16[32,4096]{1,0:T(8,128)(2,1)}, bf16[32,4096]{1,0:T(8,128)(2,1)}, u32[]{:S(2)}, u32[]{:S(2)}) collective-permute-start(bf16[32,4096]{1,0:T(8,128)(2,1)} %get-tuple-element.100), channel_id=1, source_target_pairs={{0,12},{4,0},{8,4},{12,8},{1,13},{5,1},{9,5},{13,9},{2,14},{6,2},{... | collective-permute-start | bytes 786440 | tf_op jit(solution)/shard_map/ppermute | solution.py:19
  214.6 15.2 %collective-permute-start.22 = (bf16[32,4096]{1,0:T(8,128)(2,1)}, bf16[32,4096]{1,0:T(8,128)(2,1)}, u32[]{:S(2)}, u32[]{:S(2)}) collective-permute-start(bf16[32,4096]{1,0:T(8,128)(2,1)} %get-tuple-element.99), channel_id=1, source_target_pairs={{0,8},{4,12},{8,0},{12,4},{1,9},{5,13},{9,1},{13,5},{2,10},{6,14},... | collective-permute-start | bytes 786440 | tf_op jit(solution)/shard_map/ppermute | solution.py:19
  216.5 33.7 %all-to-all-start.2 = ((bf16[4,4,32,2048]{3,2,1,0:T(8,128)(2,1)}), bf16[4,4,32,2048]{3,2,1,0:T(8,128)(2,1)}, u32[]{:S(2)}, u32[]{:S(2)}) async-start(bf16[4,4,32,2048]{3,2,1,0:T(8,128)(2,1)} %bitcast.55), calls=%async_computation.2 | async-start | bytes 4194304 | tf_op jit(solution)/shard_map/all_to_all | solution.py:550
  222.5 15.7 %collective-permute-start.17 = (bf16[4,32,2048]{2,1,0:T(8,128)(2,1)S(1)}, bf16[4,32,2048]{2,1,0:T(8,128)(2,1)S(1)}, u32[]{:S(2)}, u32[]{:S(2)}) collective-permute-start(bf16[4,32,2048]{2,1,0:T(8,128)(2,1)S(1)} %get-tuple-element.87), channel_id=1, source_target_pairs={{0,2},{2,16},{16,18},{18,0},{1,3},{3,17},{17,19},{19,1},{4,6},{6,2... | collective-permute-start | bytes 1572872 | tf_op jit(solution)/shard_map/ppermute | solution.py:19
  222.9 23.4 %collective-permute-start.18 = (bf16[4,32,2048]{2,1,0:T(8,128)(2,1)S(1)}, bf16[4,32,2048]{2,1,0:T(8,128)(2,1)S(1)}, u32[]{:S(2)}, u32[]{:S(2)}) collective-permute-start(bf16[4,32,2048]{2,1,0:T(8,128)(2,1)S(1)} %get-tuple-element.89), channel_id=1, source_target_pairs={{0,18},{2,0},{16,2},{18,16},{1,19},{3,1},{17,3},{19,17},{4,22},{6,... | collective-permute-start | bytes 1572872 | tf_op jit(solution)/shard_map/ppermute | solution.py:19
  225.8 22.0 %collective-permute-start.19 = (bf16[4,32,2048]{2,1,0:T(8,128)(2,1)S(1)}, bf16[4,32,2048]{2,1,0:T(8,128)(2,1)S(1)}, u32[]{:S(2)}, u32[]{:S(2)}) collective-permute-start(bf16[4,32,2048]{2,1,0:T(8,128)(2,1)S(1)} %get-tuple-element.88), channel_id=1, source_target_pairs={{0,16},{2,18},{16,0},{18,2},{1,17},{3,19},{17,1},{19,3},{4,20},{6,... | collective-permute-start | bytes 1572872 | tf_op jit(solution)/shard_map/ppermute | solution.py:19
  253.0 12.6 %collective-permute-start.23 = (bf16[32,2048]{1,0:T(8,128)(2,1)}, bf16[32,2048]{1,0:T(8,128)(2,1)S(1)}, u32[]{:S(2)}, u32[]{:S(2)}) collective-permute-start(bf16[32,2048]{1,0:T(8,128)(2,1)} %get-tuple-element.101), channel_id=1, source_target_pairs={{0,2},{2,16},{16,18},{18,0},{1,3},{3,17},{17,19},{19,1},{4,6},{6,2... | collective-permute-start | bytes 393224 | tf_op jit(solution)/shard_map/ppermute | solution.py:19
  253.0 12.6 %collective-permute-start.24 = (bf16[32,2048]{1,0:T(8,128)(2,1)}, bf16[32,2048]{1,0:T(8,128)(2,1)S(1)}, u32[]{:S(2)}, u32[]{:S(2)}) collective-permute-start(bf16[32,2048]{1,0:T(8,128)(2,1)} %get-tuple-element.103), channel_id=1, source_target_pairs={{0,18},{2,0},{16,2},{18,16},{1,19},{3,1},{17,3},{19,17},{4,22},{6,... | collective-permute-start | bytes 393224 | tf_op jit(solution)/shard_map/ppermute | solution.py:19
  256.2 9.4 %collective-permute-start.25 = (bf16[32,2048]{1,0:T(8,128)(2,1)S(1)}, bf16[32,2048]{1,0:T(8,128)(2,1)}, u32[]{:S(2)}, u32[]{:S(2)}) collective-permute-start(bf16[32,2048]{1,0:T(8,128)(2,1)S(1)} %get-tuple-element.102), channel_id=1, source_target_pairs={{0,16},{2,18},{16,0},{18,2},{1,17},{3,19},{17,1},{19,3},{4,20},{6,... | collective-permute-start | bytes 393224 | tf_op jit(solution)/shard_map/ppermute | solution.py:19
  257.0 11.0 %all-to-all-start.3 = ((bf16[4,32,2048]{2,1,0:T(8,128)(2,1)}), bf16[4,32,2048]{2,1,0:T(8,128)(2,1)S(1)}, u32[]{:S(2)}, u32[]{:S(2)}) async-start(bf16[4,32,2048]{2,1,0:T(8,128)(2,1)} %fusion.2), calls=%async_computation.3 | async-start | bytes 1048576 | tf_op jit(solution)/shard_map/all_to_all | solution.py:550
  262.8 16.1 %collective-permute-start.26 = (bf16[7,6,64,128]{3,2,1,0:T(8,128)(2,1)S(1)}, bf16[7,6,64,128]{3,2,1,0:T(8,128)(2,1)S(1)}, u32[]{:S(2)}, u32[]{:S(2)}) collective-permute-start(bf16[7,6,64,128]{3,2,1,0:T(8,128)(2,1)S(1)} %bitcast.64), channel_id=1, source_target_pairs={{0,16},{16,0},{1,17},{17,1},{2,18},{18,2},{3,19},{19,3},{4,20},{20... | collective-permute-start | bytes 2064392 | tf_op jit(solution)/shard_map/ppermute | solution.py:23
Sparse Core Ops, SparseCore 0:
  49.9 55.9 all-gather.1
  197.5 56.1 reduce-scatter.1

commit v7 on v6

--- a/solution.py
+++ b/solution.py
@@ -562,14 +562,21 @@
 
     summed = lax.psum_scatter(terms, "y", scatter_dimension=0, tiled=True)
     summed = summed.reshape(2, half, per_panel, edge, 2 * edge)
-    other = swap(summed[1], "zh")
-    low = jnp.where(zh == 0, summed[0], other)
-    high = jnp.where(zh == 0, other, summed[0])
-    grads = jnp.concatenate([low, high], axis=0)
-    gu_grads = grads[:, :kept_here]
+    def both_halves(mine, theirs):
+        low = jnp.where(zh == 0, mine, theirs)
+        high = jnp.where(zh == 0, theirs, mine)
+        return jnp.concatenate([low, high], axis=0)
+
+    theirs = swap(summed[1, :, :kept_here], "zh")
+    theirs_down = swap(summed[1, :, kept_here:], "zh")
+    gu_grads = both_halves(summed[0, :, :kept_here], theirs)
     d_gate_vals = gu_grads[..., :edge].reshape(panels, kept_here, square)
     d_up_vals = gu_grads[..., edge:].reshape(panels, kept_here, square)
-    d_grads = grads[:, kept_here:].reshape(panels, pairs, edge, 2, edge)
+    d_gate_vals, d_up_vals, theirs_down = lax.optimization_barrier(
+        (d_gate_vals, d_up_vals, theirs_down)
+    )
+    d_grads = both_halves(summed[0, :, kept_here:], theirs_down)
+    d_grads = d_grads.reshape(panels, pairs, edge, 2, edge)
     d_down_vals = jnp.transpose(d_grads, (0, 1, 3, 4, 2)).reshape(panels, kept_here, square)
     return (y_seq, dx_seq, d_gate_vals, d_up_vals, d_down_vals)
 

time: 291 us -> 295 us (1.014)
  waiting for transfers between devices: 106 us -> 109 us
    all_to_all x2, waiting for transfers between devices: 2.72 us -> 6.45 us  [over_x(): lax.all_to_all(value, 'x', 0, 0, tiled=True).astype(F32)]
    ppermute x9 -> x10, waiting for transfers between devices: 34.7 us -> 32.6 us  [swap(): return lax.ppermute(value, axis, [(0, 1), (1, 0)])]
    ppermute x9 -> x10, starting transfers between devices: 7.65 us -> 8.57 us  [swap(): return lax.ppermute(value, axis, [(0, 1), (1, 0)])]
  transfers between devices with their start and end apart: 33 -> 34, of which waited for: 13 -> 14; matrix products, arithmetic and copies ran while one was open for 12% -> 11% of each run, Pallas kernels for 25% -> 24%
where the time goes in v7:
time: 295 us; the launch traced here: 293 us
  waiting for transfers between devices  109 us (37%)
  Pallas kernels  71.2 us (24%)
  starting transfers between devices  53.2 us (18%)
  other arithmetic  19 us (6%)
  local copies, waits for them, and re-layouts  18.8 us (6%)
  between operations  14.3 us (5%)
  matrix products  7.84 us (3%)
    ppermute x18, waiting for transfers between devices, shift(): lax.ppermute(value, axis, [(i, (i + step) % RING) for i in range(RING)])  69.8 us
    pallas_call x1, Pallas kernels, per_device(): pl.pallas_call(part(gradient_kernel, half, kept_here), grid=(steps,), in_...  40 us
    ppermute x10, waiting for transfers between devices, swap(): return lax.ppermute(value, axis, [(0, 1), (1, 0)])  32.6 us
    pallas_call x2, Pallas kernels, forward(): pl.pallas_call(part(forward_kernel, half, kept_here, first), grid=(2,), i...  31.2 us
    ppermute x18, starting transfers between devices, shift(): lax.ppermute(value, axis, [(i, (i + step) % RING) for i in range(RING)])  24 us
    all_to_all x2, starting transfers between devices, gather_all(): return lax.all_to_all(wide, axis, 0, 0, tiled=True)  10.5 us
    all_to_all x2, starting transfers between devices, over_x(): lax.all_to_all(value, 'x', 0, 0, tiled=True).astype(F32)  10.2 us
    ppermute x10, starting transfers between devices, swap(): return lax.ppermute(value, axis, [(0, 1), (1, 0)])  8.57 us
  transfers between devices with their start and end apart: 34, of which 14 were waited for; matrix products, arithmetic and copies ran while one was open for 11% of the time, Pallas kernels for 24%

profile of v7, /device:TPU:26, one launch (start us, length us, event | category | flops | bytes accessed | tf_op | source)
XLA Modules:
  0.0 293.3 jit_solution(15212136046703329868)
XLA Ops:
  7.2 0.6 collective-permute-start.1
  7.8 2.4 collective-permute-start.2
  10.2 1.8 collective-permute-start.3
  12.0 2.0 broadcast_in_dim.4
  14.1 5.4 %all-to-all-start = ((bf16[4,32,4096]{2,1,0:T(8,128)(2,1)}), bf16[4,32,4096]{2,1,0:T(8,128)(2,1)S(1)}, u32[]{:S(2)}, u32[]{:S(2)}) async-start(bf16[4,32,4096]{2,1,0:T(8,128)(2,1)} %broadcast_in_dim.4), calls=%async_computation | async-start | bytes 2097152 | tf_op jit(solution)/shard_map/all_to_all | solution.py:427
  19.5 0.7 reshape.65
  20.6 0.7 reshape.63
  21.3 1.9 reshape.64
  23.2 0.5 pad_maximum_fusion
  23.9 3.6 %collective-permute-start = (bf16[7,6,64,128]{3,2,1,0:T(8,128)(2,1)S(1)}, bf16[7,6,64,128]{3,2,1,0:T(8,128)(2,1)S(1)}, u32[]{:S(2)}, u32[]{:S(2)}) collective-permute-start(bf16[7,6,64,128]{3,2,1,0:T(8,128)(2,1)S(1)} %get-tuple-element.101), channel_id=1, source_target_pairs={{0,16},{16,0},{1,17},{17,1},{2,18},{18,2},{3,19},{19,3},{4,20},{20... | collective-permute-start | bytes 2064392 | tf_op jit(solution)/shard_map/ppermute | solution.py:23
  27.5 1.2 pad_maximum_fusion.2.refs_3_.refs_6_
  28.7 19.8 %collective-permute-done = bf16[7,6,64,128]{3,2,1,0:T(8,128)(2,1)S(1)} collective-permute-done((bf16[7,6,64,128]{3,2,1,0:T(8,128)(2,1)S(1)}, bf16[7,6,64,128]{3,2,1,0:T(8,128)(2,1)S(1)}, u32[]{:S(2)}, u32[]{:S(2)}) %collective-permute-start) | collective-permute-done | bytes 688160 | tf_op jit(solution)/shard_map/ppermute | solution.py:23
  48.5 1.2 pad_maximum_fusion.1
  49.7 2.6 broadcast_in_dim.5
  52.3 5.0 %all-to-all-start.1 = ((bf16[4,4,32,4096]{3,2,1,0:T(8,128)(2,1)}), bf16[4,4,32,4096]{3,2,1,0:T(8,128)(2,1)}, u32[]{:S(2)}, u32[]{:S(2)}) async-start(bf16[4,4,32,4096]{3,2,1,0:T(8,128)(2,1)} %broadcast_in_dim.5), calls=%async_computation.1 | async-start | bytes 8388608 | tf_op jit(solution)/shard_map/all_to_all | solution.py:427
  57.3 0.6 collective-permute-start.9
  57.9 2.7 collective-permute-start.5
  60.6 43.2 %collective-permute-done.9.refs_6_.refs_9_ = bf16[128,4096]{1,0:T(8,128)(2,1)S(1)} collective-permute-done((bf16[128,4096]{1,0:T(8,128)(2,1)S(1)}, bf16[128,4096]{1,0:T(8,128)(2,1)S(1)}, u32[]{:S(2)}, u32[]{:S(2)}) %collective-permute-start.9) | collective-permute-done | bytes 1048608 | tf_op jit(solution)/shard_map/ppermute | solution.py:19
  104.4 0.6 pad_add_fusion.refs_0_
  105.0 1.6 collective-permute-done.10.refs_8_.refs_13_
  106.6 3.0 %collective-permute-done.6.refs_6_.refs_11_ = bf16[128,4096]{1,0:T(8,128)(2,1)} collective-permute-done((bf16[128,4096]{1,0:T(8,128)(2,1)S(1)}, bf16[128,4096]{1,0:T(8,128)(2,1)}, u32[]{:S(2)}, u32[]{:S(2)}) %collective-permute-start.6) | collective-permute-done | bytes 1048608 | tf_op jit(solution)/shard_map/ppermute | solution.py:23
  110.0 17.8 %forward_away.1 = (f32[2,4,4,32,896]{4,3,2,1,0:T(8,128)}, bf16[2,4,4,32,512]{4,3,2,1,0:T(8,128)(2,1)}, bf16[16,32,4096]{2,1,0:T(8,128)(2,1)}, bf16[4096,896]{1,0:T(8,128)(2,1)}, bf16[4096,512]{1,0:T(8,128)(2,1)}) custom-call(s32[3]{0:T(128)} %pad_add_fusion.refs_0_, s32[14,32]{1,0:T(8,128)} %refs_1_.3, s32[14,32]{1,0:T(8,128)} %refs_2_.3, s32[14,32]{1,0:T(8,128)} %refs_3_.3, ...), custom_call_target="tpu_custom_call" | custom-call | flops 738197504 | bytes 3145728 | tf_op jit(solution)/shard_map/forward_away/pallas_call | solution.py:464
  128.2 13.4 %forward_kept.1 = (f32[2,4,4,32,896]{4,3,2,1,0:T(8,128)}, bf16[2,4,4,32,512]{4,3,2,1,0:T(8,128)(2,1)}, bf16[16,32,4096]{2,1,0:T(8,128)(2,1)}) custom-call(s32[3]{0:T(128)} %pad_add_fusion.refs_0_, bf16[4096,896]{1,0:T(8,128)(2,1)} %get-tuple-element.54.refs_1_.refs_17_, ...), custom_call_target="tpu_custom_call", output_to_operand_aliasing={{0}: (7, {}), {1}: (8, {})} | custom-call | flops 738197504 | bytes 3145728 | tf_op jit(solution)/shard_map/forward_kept/pallas_call | solution.py:464
  141.7 3.9 %add_convert_fusion.3 = (bf16[4,32,4096]{2,1,0:T(8,128)(2,1)S(1)}, bf16[4,32,4096]{2,1,0:T(8,128)(2,1)S(1)}, bf16[4,32,4096]{2,1,0:T(8,128)(2,1)}, bf16[4,32,4096]{2,1,0:T(8,128)(2,1)S(1)}) fusion(bf16[16,32,4096]{2,1,0:T(8,128)(2,1)S(1)} %collective-permute-done.12, bf16[16,32,4096]{2,1,0:T(8,128)(2,1)} %get-tuple-element.61), kind=kLoop, calls=%fused_computation.5 | loop fusion | flops 8388608 | bytes 12582912 | tf_op jit(solution)/shard_map/convert_element_type | solution.py:46
  145.6 3.2 %collective-permute-start.14 = (bf16[4,32,4096]{2,1,0:T(8,128)(2,1)S(1)}, bf16[4,32,4096]{2,1,0:T(8,128)(2,1)}, u32[]{:S(2)}, u32[]{:S(2)}) collective-permute-start(bf16[4,32,4096]{2,1,0:T(8,128)(2,1)S(1)} %get-tuple-element.70), channel_id=1, source_target_pairs={{0,18},{2,0},{16,2},{18,16},{1,19},{3,1},{17,3},{19,17},{4,22},{6,... | collective-permute-start | bytes 3145736 | tf_op jit(solution)/shard_map/ppermute | solution.py:19
  148.8 40.0 %gradients.1 = (bf16[512,896]{1,0:T(8,128)(2,1)}, bf16[512,4096]{1,0:T(8,128)(2,1)}, bf16[336,64,128]{2,1,0:T(8,128)(2,1)}) custom-call(s32[3]{0:T(128)} %pad_add_fusion.refs_0_, s32[14,32]{1,0:T(8,128)} %refs_1_.3, s32[14,32]{1,0:T(8,128)} %refs_2_.3, s32[14,32]{1,0:T(8,128)} %refs_3_.3, bf16[4,4,32,4096]{3,2,1,0:T(8,128)(2,1)} %all-to-all-done.1.refs_4_, ...), custom_call_target="tpu_custom_call" | custom-call | flops 2013265920 | bytes 5242880 | tf_op jit(solution)/shard_map/gradients/pallas_call | solution.py:501
  188.9 5.9 %collective-permute-done.13 = bf16[4,32,4096]{2,1,0:T(8,128)(2,1)} collective-permute-done((bf16[4,32,4096]{2,1,0:T(8,128)(2,1)}, bf16[4,32,4096]{2,1,0:T(8,128)(2,1)}, u32[]{:S(2)}, u32[]{:S(2)}) %collective-permute-start.13) | collective-permute-done | bytes 1048608 | tf_op jit(solution)/shard_map/ppermute | solution.py:19
  194.8 2.5 add_convert_fusion.2
  197.4 1.1 copy-done.7
  198.5 7.8 %convolution_convert_fusion = bf16[512,4096]{1,0:T(8,128)(2,1)S(1)} fusion(bf16[512,896]{1,0:T(8,128)(2,1)S(1)} %copy-done.7, bf16[4096,896]{1,0:T(8,128)(2,1)} %get-tuple-element.54.refs_1_.refs_17_), kind=kOutput, calls=%fused_computation | convolution fusion | flops 3760193536 | bytes 12451840 | tf_op jit(solution)/shard_map/dot_general | solution.py:539
  206.4 1.6 add_convert_fusion
  208.0 1.6 copy.23
  209.6 0.9 slice_bitcast_fusion.7
  210.5 1.2 collective-permute-start.20
  211.7 0.8 collective-permute-start.21
  212.5 1.8 collective-permute-start.22
  214.3 5.9 %all-to-all-start.2 = ((bf16[4,4,32,2048]{3,2,1,0:T(8,128)(2,1)}), bf16[4,4,32,2048]{3,2,1,0:T(8,128)(2,1)}, u32[]{:S(2)}, u32[]{:S(2)}) async-start(bf16[4,4,32,2048]{3,2,1,0:T(8,128)(2,1)} %bitcast.70), calls=%async_computation.2 | async-start | bytes 4194304 | tf_op jit(solution)/shard_map/all_to_all | solution.py:550
  220.3 0.7 collective-permute-start.17
  221.0 2.6 collective-permute-start.18
  223.6 1.0 collective-permute-start.19
  224.6 2.9 collective-permute-done.22
  227.5 1.9 fusion.5
  229.4 6.2 %collective-permute-done.17 = bf16[4,32,2048]{2,1,0:T(8,128)(2,1)S(1)} collective-permute-done((bf16[4,32,2048]{2,1,0:T(8,128)(2,1)S(1)}, bf16[4,32,2048]{2,1,0:T(8,128)(2,1)S(1)}, u32[]{:S(2)}, u32[]{:S(2)}) %collective-permute-start.17) | collective-permute-done | bytes 524320 | tf_op jit(solution)/shard_map/ppermute | solution.py:19
  235.5 8.8 %collective-permute-done.18 = bf16[4,32,2048]{2,1,0:T(8,128)(2,1)S(1)} collective-permute-done((bf16[4,32,2048]{2,1,0:T(8,128)(2,1)S(1)}, bf16[4,32,2048]{2,1,0:T(8,128)(2,1)S(1)}, u32[]{:S(2)}, u32[]{:S(2)}) %collective-permute-start.18) | collective-permute-done | bytes 524320 | tf_op jit(solution)/shard_map/ppermute | solution.py:19
  244.3 1.6 collective-permute-done.19
  245.9 1.1 fusion.2
  247.1 1.1 all-to-all-done.2
  248.1 2.0 reduce_sum.24
  250.2 1.0 collective-permute-start.23
  251.2 2.6 collective-permute-start.24
  253.8 1.0 collective-permute-start.25
  254.7 4.3 %all-to-all-start.3 = ((bf16[4,32,2048]{2,1,0:T(8,128)(2,1)}), bf16[4,32,2048]{2,1,0:T(8,128)(2,1)S(1)}, u32[]{:S(2)}, u32[]{:S(2)}) async-start(bf16[4,32,2048]{2,1,0:T(8,128)(2,1)} %fusion.2), calls=%async_computation.3 | async-start | bytes 1048576 | tf_op jit(solution)/shard_map/all_to_all | solution.py:550
  259.1 1.2 collective-permute-done.25
  260.3 5.4 %all-to-all-done.3 = bf16[4,32,2048]{2,1,0:T(8,128)(2,1)S(1)} async-done(((bf16[4,32,2048]{2,1,0:T(8,128)(2,1)}), bf16[4,32,2048]{2,1,0:T(8,128)(2,1)S(1)}, u32[]{:S(2)}, u32[]{:S(2)}) %all-to-all-start.3) | async-done | bytes 524320 | tf_op jit(solution)/shard_map/all_to_all | solution.py:550
  265.8 1.2 slice_bitcast_fusion.3
  267.0 2.6 collective-permute-start.26
  269.6 0.7 pad_maximum_fusion.5
  270.3 1.0 slice_bitcast_fusion.9
  271.3 1.0 collective-permute-start.27
  272.3 8.0 %collective-permute-done.26 = bf16[7,4,64,128]{3,2,1,0:T(8,128)(2,1)S(1)} collective-permute-done((bf16[7,4,64,128]{3,2,1,0:T(8,128)(2,1)S(1)}, bf16[7,4,64,128]{3,2,1,0:T(8,128)(2,1)S(1)}, u32[]{:S(2)}, u32[]{:S(2)}) %collective-permute-start.26) | collective-permute-done | bytes 458784 | tf_op jit(solution)/shard_map/ppermute | solution.py:23
  280.8 1.4 reshape.70
  282.2 1.4 reshape.71
  283.6 1.0 broadcast_select_fusion.3
  285.0 1.4 reshape.73
  (60 shorter events, 3.4 us)
Async XLA Ops:
  7.2 12.3 %copy-start.4 = (bf16[14,4,4096]{2,1,0:T(4,128)(2,1)S(1)}, bf16[14,4,4096]{2,1,0:T(4,128)(2,1)}, u32[]{:S(2)}) copy-start(bf16[14,4,4096]{2,1,0:T(4,128)(2,1)} %param.14) | copy-start | bytes 1376260
  7.2 20.3 %collective-permute-start.1 = (bf16[32,4096]{1,0:T(8,128)(2,1)}, bf16[32,4096]{1,0:T(8,128)(2,1)}, u32[]{:S(2)}, u32[]{:S(2)}) collective-permute-start(bf16[32,4096]{1,0:T(8,128)(2,1)} %param.8), channel_id=1, source_target_pairs={{0,12},{4,0},{8,4},{12,8},{1,13},{5,1},{9,5},{13,9},{2,14},{6,2},{... | collective-permute-start | bytes 786440 | tf_op jit(solution)/shard_map/ppermute | solution.py:19
  7.8 19.7 %collective-permute-start.2 = (bf16[32,4096]{1,0:T(8,128)(2,1)}, bf16[32,4096]{1,0:T(8,128)(2,1)}, u32[]{:S(2)}, u32[]{:S(2)}) collective-permute-start(bf16[32,4096]{1,0:T(8,128)(2,1)} %param.8), channel_id=1, source_target_pairs={{0,8},{4,12},{8,0},{12,4},{1,9},{5,13},{9,1},{13,5},{2,10},{6,14},... | collective-permute-start | bytes 786440 | tf_op jit(solution)/shard_map/ppermute | solution.py:19
  10.2 17.3 %collective-permute-start.3 = (bf16[32,4096]{1,0:T(8,128)(2,1)}, bf16[32,4096]{1,0:T(8,128)(2,1)}, u32[]{:S(2)}, u32[]{:S(2)}) collective-permute-start(bf16[32,4096]{1,0:T(8,128)(2,1)} %param.8), channel_id=1, source_target_pairs={{0,4},{4,8},{8,12},{12,0},{1,5},{5,9},{9,13},{13,1},{2,6},{6,10},{... | collective-permute-start | bytes 786440 | tf_op jit(solution)/shard_map/ppermute | solution.py:19
  14.1 6.5 %copy-start.5 = (bf16[14,4,4096]{2,1,0:T(4,128)(2,1)S(1)}, bf16[14,4,4096]{2,1,0:T(4,128)(2,1)}, u32[]{:S(2)}) copy-start(bf16[14,4,4096]{2,1,0:T(4,128)(2,1)} %param.10) | copy-start | bytes 1376260
  14.1 34.4 %all-to-all-start = ((bf16[4,32,4096]{2,1,0:T(8,128)(2,1)}), bf16[4,32,4096]{2,1,0:T(8,128)(2,1)S(1)}, u32[]{:S(2)}, u32[]{:S(2)}) async-start(bf16[4,32,4096]{2,1,0:T(8,128)(2,1)} %broadcast_in_dim.4), calls=%async_computation | async-start | bytes 2097152 | tf_op jit(solution)/shard_map/all_to_all | solution.py:427
  19.5 90.5 %all-gather.2.cloned.1.call-start = ((), (), s32[]{:S(2)}) async-start(), calls=%async_computation.5 | async-start | bytes 6881280 | tf_op jit(solution)/shard_map/all_gather | solution.py:433
  23.7 3.8 %copy-start.6 = (bf16[32,4096]{1,0:T(8,128)(2,1)S(1)}, bf16[32,4096]{1,0:T(8,128)(2,1)}, u32[]{:S(2)}) copy-start(bf16[32,4096]{1,0:T(8,128)(2,1)} %param.8) | copy-start | bytes 786436
  23.9 24.6 %collective-permute-start = (bf16[7,6,64,128]{3,2,1,0:T(8,128)(2,1)S(1)}, bf16[7,6,64,128]{3,2,1,0:T(8,128)(2,1)S(1)}, u32[]{:S(2)}, u32[]{:S(2)}) collective-permute-start(bf16[7,6,64,128]{3,2,1,0:T(8,128)(2,1)S(1)} %get-tuple-element.101), channel_id=1, source_target_pairs={{0,16},{16,0},{1,17},{17,1},{2,18},{18,2},{3,19},{19,3},{4,20},{20... | collective-permute-start | bytes 2064392 | tf_op jit(solution)/shard_map/ppermute | solution.py:23
  28.7 31.9 %copy-start = (bf16[128,4096]{1,0:T(8,128)(2,1)}, bf16[128,4096]{1,0:T(8,128)(2,1)S(1)}, u32[]{:S(2)}) copy-start(bf16[128,4096]{1,0:T(8,128)(2,1)S(1)} %pad_maximum_fusion.2.refs_3_.refs_6_) | copy-start | bytes 3145732
  52.3 57.5 %all-to-all-start.1 = ((bf16[4,4,32,4096]{3,2,1,0:T(8,128)(2,1)}), bf16[4,4,32,4096]{3,2,1,0:T(8,128)(2,1)}, u32[]{:S(2)}, u32[]{:S(2)}) async-start(bf16[4,4,32,4096]{3,2,1,0:T(8,128)(2,1)} %broadcast_in_dim.5), calls=%async_computation.1 | async-start | bytes 8388608 | tf_op jit(solution)/shard_map/all_to_all | solution.py:427
  57.3 208.5 %reduce-scatter.2.cloned.1.call-start = ((), (), s32[]{:S(2)}) async-start(), calls=%async_computation.6 | async-start | bytes 6881280 | tf_op jit(solution)/shard_map/reduce_scatter | solution.py:563
  57.3 46.5 %collective-permute-start.9 = (bf16[128,4096]{1,0:T(8,128)(2,1)S(1)}, bf16[128,4096]{1,0:T(8,128)(2,1)S(1)}, u32[]{:S(2)}, u32[]{:S(2)}) collective-permute-start(bf16[128,4096]{1,0:T(8,128)(2,1)S(1)} %pad_maximum_fusion.2.refs_3_.refs_6_), channel_id=1, source_target_pairs={{0,2},{2,16},{16,18},{18,0},{1,3},{3,17},{17,19},{19,1},{4,6},{6,2... | collective-permute-start | bytes 3145736 | tf_op jit(solution)/shard_map/ppermute | solution.py:19
  57.9 45.9 %collective-permute-start.5 = (bf16[128,4096]{1,0:T(8,128)(2,1)S(1)}, bf16[128,4096]{1,0:T(8,128)(2,1)S(1)}, u32[]{:S(2)}, u32[]{:S(2)}) collective-permute-start(bf16[128,4096]{1,0:T(8,128)(2,1)S(1)} %pad_maximum_fusion.2.refs_3_.refs_6_), channel_id=1, source_target_pairs={{0,18},{2,0},{16,2},{18,16},{1,19},{3,1},{17,3},{19,17},{4,22},{6,... | collective-permute-start | bytes 3145736 | tf_op jit(solution)/shard_map/ppermute | solution.py:19
  60.6 43.8 %collective-permute-start.7 = (bf16[128,4096]{1,0:T(8,128)(2,1)S(1)}, bf16[128,4096]{1,0:T(8,128)(2,1)}, u32[]{:S(2)}, u32[]{:S(2)}) collective-permute-start(bf16[128,4096]{1,0:T(8,128)(2,1)S(1)} %pad_maximum_fusion.2.refs_3_.refs_6_), channel_id=1, source_target_pairs={{0,16},{2,18},{16,0},{18,2},{1,17},{3,19},{17,1},{19,3},{4,20},{6,... | collective-permute-start | bytes 3145736 | tf_op jit(solution)/shard_map/ppermute | solution.py:19
  60.6 44.5 %collective-permute-start.4 = (bf16[128,4096]{1,0:T(8,128)(2,1)S(1)}, bf16[128,4096]{1,0:T(8,128)(2,1)}, u32[]{:S(2)}, u32[]{:S(2)}) collective-permute-start(bf16[128,4096]{1,0:T(8,128)(2,1)S(1)} %pad_maximum_fusion.2.refs_3_.refs_6_), channel_id=1, source_target_pairs={{0,1},{1,0},{2,3},{3,2},{4,5},{5,4},{6,7},{7,6},{8,9},{9,8},{10,11... | collective-permute-start | bytes 3145736 | tf_op jit(solution)/shard_map/ppermute | solution.py:23
  103.8 23.9 %copy-start.1 = (bf16[128,4096]{1,0:T(8,128)(2,1)}, bf16[128,4096]{1,0:T(8,128)(2,1)S(1)}, u32[]{:S(2)}) copy-start(bf16[128,4096]{1,0:T(8,128)(2,1)S(1)} %collective-permute-done.9.refs_6_.refs_9_) | copy-start | bytes 3145732
  103.8 2.8 collective-permute-start.10
  103.8 23.9 %copy-start.2 = (bf16[128,4096]{1,0:T(8,128)(2,1)}, bf16[128,4096]{1,0:T(8,128)(2,1)S(1)}, u32[]{:S(2)}) copy-start(bf16[128,4096]{1,0:T(8,128)(2,1)S(1)} %collective-permute-done.5.refs_4_.refs_7_) | copy-start | bytes 3145732
  103.8 5.8 %collective-permute-start.6 = (bf16[128,4096]{1,0:T(8,128)(2,1)S(1)}, bf16[128,4096]{1,0:T(8,128)(2,1)}, u32[]{:S(2)}, u32[]{:S(2)}) collective-permute-start(bf16[128,4096]{1,0:T(8,128)(2,1)S(1)} %collective-permute-done.5.refs_4_.refs_7_), channel_id=1, source_target_pairs={{0,1},{1,0},{2,3},{3,2},{4,5},{5,4},{6,7},{7,6},{8,9},{9,8},{10,11... | collective-permute-start | bytes 3145736 | tf_op jit(solution)/shard_map/ppermute | solution.py:23
  104.3 5.5 %collective-permute-start.8 = (bf16[128,4096]{1,0:T(8,128)(2,1)}, bf16[128,4096]{1,0:T(8,128)(2,1)}, u32[]{:S(2)}, u32[]{:S(2)}) collective-permute-start(bf16[128,4096]{1,0:T(8,128)(2,1)} %collective-permute-done.7.refs_5_.refs_8_), channel_id=1, source_target_pairs={{0,1},{1,0},{2,3},{3,2},{4,5},{5,4},{6,7},{7,6},{8,9},{9,8},{10,11... | collective-permute-start | bytes 3145736 | tf_op jit(solution)/shard_map/ppermute | solution.py:23
  109.8 31.8 %collective-permute-start.11 = (bf16[4,4,32,4096]{3,2,1,0:T(8,128)(2,1)}, bf16[4,4,32,4096]{3,2,1,0:T(8,128)(2,1)}, u32[]{:S(2)}, u32[]{:S(2)}) collective-permute-start(bf16[4,4,32,4096]{3,2,1,0:T(8,128)(2,1)} %all-to-all-done.1.refs_4_), channel_id=1, source_target_pairs={{0,1},{1,0},{2,3},{3,2},{4,5},{5,4},{6,7},{7,6},{8,9},{9,8},{10,11... | collective-permute-start | bytes 12582920 | tf_op jit(solution)/shard_map/ppermute | solution.py:23
  127.8 13.9 %collective-permute-start.12 = (bf16[16,32,4096]{2,1,0:T(8,128)(2,1)}, bf16[16,32,4096]{2,1,0:T(8,128)(2,1)S(1)}, u32[]{:S(2)}, u32[]{:S(2)}) collective-permute-start(bf16[16,32,4096]{2,1,0:T(8,128)(2,1)} %get-tuple-element.62), channel_id=1, source_target_pairs={{0,1},{1,0},{2,3},{3,2},{4,5},{5,4},{6,7},{7,6},{8,9},{9,8},{10,11... | collective-permute-start | bytes 12582920 | tf_op jit(solution)/shard_map/ppermute | solution.py:23
  145.6 49.2 %collective-permute-start.13 = (bf16[4,32,4096]{2,1,0:T(8,128)(2,1)}, bf16[4,32,4096]{2,1,0:T(8,128)(2,1)}, u32[]{:S(2)}, u32[]{:S(2)}) collective-permute-start(bf16[4,32,4096]{2,1,0:T(8,128)(2,1)} %get-tuple-element.69), channel_id=1, source_target_pairs={{0,2},{2,16},{16,18},{18,0},{1,3},{3,17},{17,19},{19,1},{4,6},{6,2... | collective-permute-start | bytes 3145736 | tf_op jit(solution)/shard_map/ppermute | solution.py:19
  145.6 49.2 %collective-permute-start.14 = (bf16[4,32,4096]{2,1,0:T(8,128)(2,1)S(1)}, bf16[4,32,4096]{2,1,0:T(8,128)(2,1)}, u32[]{:S(2)}, u32[]{:S(2)}) collective-permute-start(bf16[4,32,4096]{2,1,0:T(8,128)(2,1)S(1)} %get-tuple-element.70), channel_id=1, source_target_pairs={{0,18},{2,0},{16,2},{18,16},{1,19},{3,1},{17,3},{19,17},{4,22},{6,... | collective-permute-start | bytes 3145736 | tf_op jit(solution)/shard_map/ppermute | solution.py:19
  148.8 46.0 %collective-permute-start.15 = (bf16[4,32,4096]{2,1,0:T(8,128)(2,1)S(1)}, bf16[4,32,4096]{2,1,0:T(8,128)(2,1)}, u32[]{:S(2)}, u32[]{:S(2)}) collective-permute-start(bf16[4,32,4096]{2,1,0:T(8,128)(2,1)S(1)} %get-tuple-element.71), channel_id=1, source_target_pairs={{0,16},{2,18},{16,0},{18,2},{1,17},{3,19},{17,1},{19,3},{4,20},{6,... | collective-permute-start | bytes 3145736 | tf_op jit(solution)/shard_map/ppermute | solution.py:19
  197.3 1.2 copy-start.7
  197.4 9.0 %collective-permute-start.16 = (bf16[512,4096]{1,0:T(8,128)(2,1)}, bf16[512,4096]{1,0:T(8,128)(2,1)S(1)}, u32[]{:S(2)}, u32[]{:S(2)}) collective-permute-start(bf16[512,4096]{1,0:T(8,128)(2,1)} %get-tuple-element.74), channel_id=1, source_target_pairs={{0,1},{1,0},{2,3},{3,2},{4,5},{5,4},{6,7},{7,6},{8,9},{9,8},{10,11... | collective-permute-start | bytes 12582920 | tf_op jit(solution)/shard_map/ppermute | solution.py:23
  210.5 13.2 %collective-permute-start.20 = (bf16[32,4096]{1,0:T(8,128)(2,1)}, bf16[32,4096]{1,0:T(8,128)(2,1)S(1)}, u32[]{:S(2)}, u32[]{:S(2)}) collective-permute-start(bf16[32,4096]{1,0:T(8,128)(2,1)} %get-tuple-element.102), channel_id=1, source_target_pairs={{0,4},{4,8},{8,12},{12,0},{1,5},{5,9},{9,13},{13,1},{2,6},{6,10},{... | collective-permute-start | bytes 786440 | tf_op jit(solution)/shard_map/ppermute | solution.py:19
  211.7 12.9 %collective-permute-start.21 = (bf16[32,4096]{1,0:T(8,128)(2,1)}, bf16[32,4096]{1,0:T(8,128)(2,1)}, u32[]{:S(2)}, u32[]{:S(2)}) collective-permute-start(bf16[32,4096]{1,0:T(8,128)(2,1)} %get-tuple-element.104), channel_id=1, source_target_pairs={{0,12},{4,0},{8,4},{12,8},{1,13},{5,1},{9,5},{13,9},{2,14},{6,2},{... | collective-permute-start | bytes 786440 | tf_op jit(solution)/shard_map/ppermute | solution.py:19
  212.5 15.0 %collective-permute-start.22 = (bf16[32,4096]{1,0:T(8,128)(2,1)}, bf16[32,4096]{1,0:T(8,128)(2,1)}, u32[]{:S(2)}, u32[]{:S(2)}) collective-permute-start(bf16[32,4096]{1,0:T(8,128)(2,1)} %get-tuple-element.103), channel_id=1, source_target_pairs={{0,8},{4,12},{8,0},{12,4},{1,9},{5,13},{9,1},{13,5},{2,10},{6,14},... | collective-permute-start | bytes 786440 | tf_op jit(solution)/shard_map/ppermute | solution.py:19
  214.3 33.8 %all-to-all-start.2 = ((bf16[4,4,32,2048]{3,2,1,0:T(8,128)(2,1)}), bf16[4,4,32,2048]{3,2,1,0:T(8,128)(2,1)}, u32[]{:S(2)}, u32[]{:S(2)}) async-start(bf16[4,4,32,2048]{3,2,1,0:T(8,128)(2,1)} %bitcast.70), calls=%async_computation.2 | async-start | bytes 4194304 | tf_op jit(solution)/shard_map/all_to_all | solution.py:550
  220.3 15.2 %collective-permute-start.17 = (bf16[4,32,2048]{2,1,0:T(8,128)(2,1)S(1)}, bf16[4,32,2048]{2,1,0:T(8,128)(2,1)S(1)}, u32[]{:S(2)}, u32[]{:S(2)}) collective-permute-start(bf16[4,32,2048]{2,1,0:T(8,128)(2,1)S(1)} %get-tuple-element.93), channel_id=1, source_target_pairs={{0,2},{2,16},{16,18},{18,0},{1,3},{3,17},{17,19},{19,1},{4,6},{6,2... | collective-permute-start | bytes 1572872 | tf_op jit(solution)/shard_map/ppermute | solution.py:19
  221.0 23.3 %collective-permute-start.18 = (bf16[4,32,2048]{2,1,0:T(8,128)(2,1)S(1)}, bf16[4,32,2048]{2,1,0:T(8,128)(2,1)S(1)}, u32[]{:S(2)}, u32[]{:S(2)}) collective-permute-start(bf16[4,32,2048]{2,1,0:T(8,128)(2,1)S(1)} %get-tuple-element.95), channel_id=1, source_target_pairs={{0,18},{2,0},{16,2},{18,16},{1,19},{3,1},{17,3},{19,17},{4,22},{6,... | collective-permute-start | bytes 1572872 | tf_op jit(solution)/shard_map/ppermute | solution.py:19
  223.6 22.3 %collective-permute-start.19 = (bf16[4,32,2048]{2,1,0:T(8,128)(2,1)S(1)}, bf16[4,32,2048]{2,1,0:T(8,128)(2,1)S(1)}, u32[]{:S(2)}, u32[]{:S(2)}) collective-permute-start(bf16[4,32,2048]{2,1,0:T(8,128)(2,1)S(1)} %get-tuple-element.94), channel_id=1, source_target_pairs={{0,16},{2,18},{16,0},{18,2},{1,17},{3,19},{17,1},{19,3},{4,20},{6,... | collective-permute-start | bytes 1572872 | tf_op jit(solution)/shard_map/ppermute | solution.py:19
  250.2 8.9 %collective-permute-start.23 = (bf16[32,2048]{1,0:T(8,128)(2,1)S(1)}, bf16[32,2048]{1,0:T(8,128)(2,1)S(1)}, u32[]{:S(2)}, u32[]{:S(2)}) collective-permute-start(bf16[32,2048]{1,0:T(8,128)(2,1)S(1)} %get-tuple-element.107), channel_id=1, source_target_pairs={{0,2},{2,16},{16,18},{18,0},{1,3},{3,17},{17,19},{19,1},{4,6},{6,2... | collective-permute-start | bytes 393224 | tf_op jit(solution)/shard_map/ppermute | solution.py:19
  251.2 7.9 %collective-permute-start.24 = (bf16[32,2048]{1,0:T(8,128)(2,1)S(1)}, bf16[32,2048]{1,0:T(8,128)(2,1)S(1)}, u32[]{:S(2)}, u32[]{:S(2)}) collective-permute-start(bf16[32,2048]{1,0:T(8,128)(2,1)S(1)} %get-tuple-element.109), channel_id=1, source_target_pairs={{0,18},{2,0},{16,2},{18,16},{1,19},{3,1},{17,3},{19,17},{4,22},{6,... | collective-permute-start | bytes 393224 | tf_op jit(solution)/shard_map/ppermute | solution.py:19
  253.8 6.5 %collective-permute-start.25 = (bf16[32,2048]{1,0:T(8,128)(2,1)S(1)}, bf16[32,2048]{1,0:T(8,128)(2,1)S(1)}, u32[]{:S(2)}, u32[]{:S(2)}) collective-permute-start(bf16[32,2048]{1,0:T(8,128)(2,1)S(1)} %get-tuple-element.108), channel_id=1, source_target_pairs={{0,16},{2,18},{16,0},{18,2},{1,17},{3,19},{17,1},{19,3},{4,20},{6,... | collective-permute-start | bytes 393224 | tf_op jit(solution)/shard_map/ppermute | solution.py:19
  254.7 10.9 %all-to-all-start.3 = ((bf16[4,32,2048]{2,1,0:T(8,128)(2,1)}), bf16[4,32,2048]{2,1,0:T(8,128)(2,1)S(1)}, u32[]{:S(2)}, u32[]{:S(2)}) async-start(bf16[4,32,2048]{2,1,0:T(8,128)(2,1)} %fusion.2), calls=%async_computation.3 | async-start | bytes 1048576 | tf_op jit(solution)/shard_map/all_to_all | solution.py:550
  265.8 14.5 %copy-start.3 = (bf16[84,64,128]{2,1,0:T(8,128)(2,1)S(1)}, bf16[84,64,128]{2,1,0:T(8,128)(2,1)}, u32[]{:S(2)}) copy-start(bf16[84,64,128]{2,1,0:T(8,128)(2,1)} %reduce-scatter.2.cloned.1.call-done) | copy-start | bytes 4128772
  267.0 13.3 %collective-permute-start.26 = (bf16[7,4,64,128]{3,2,1,0:T(8,128)(2,1)S(1)}, bf16[7,4,64,128]{3,2,1,0:T(8,128)(2,1)S(1)}, u32[]{:S(2)}, u32[]{:S(2)}) collective-permute-start(bf16[7,4,64,128]{3,2,1,0:T(8,128)(2,1)S(1)} %slice_bitcast_fusion.3), channel_id=1, source_target_pairs={{0,16},{16,0},{1,17},{17,1},{2,18},{18,2},{3,19},{19,3},{4,20},{20... | collective-permute-start | bytes 1376264 | tf_op jit(solution)/shard_map/ppermute | solution.py:23
  271.3 12.3 %collective-permute-start.27 = (bf16[7,2,64,128]{3,2,1,0:T(8,128)(2,1)S(1)}, bf16[7,2,64,128]{3,2,1,0:T(8,128)(2,1)}, u32[]{:S(2)}, u32[]{:S(2)}) collective-permute-start(bf16[7,2,64,128]{3,2,1,0:T(8,128)(2,1)S(1)} %slice_bitcast_fusion.9), channel_id=1, source_target_pairs={{0,16},{16,0},{1,17},{17,1},{2,18},{18,2},{3,19},{19,3},{4,20},{20... | collective-permute-start | bytes 688136 | tf_op jit(solution)/shard_map/ppermute | solution.py:23
Sparse Core Ops, SparseCore 0:
  49.9 55.9 all-gather.1
  197.5 56.1 reduce-scatter.1
